TPU v7x, 32 devices: a whole 2x2x4 slice. The times are simulated.
32 devices in a mesh: batch: 8 (over z, core), seq: 4 (over y, x).
Axes of the slice: x: 2, y: 2, z: 4, core: 2. Of those that a mesh axis runs over, the one named last changes fastest.
Arguments:
- tokens: bfloat16 [32, 336, 1152], P(('batch', 'seq')), may hold values from -8 to 8
- skipped: bfloat16 [32, 336, 1152], P(('batch', 'seq')), may hold values from -8 to 8
- cotangent: bfloat16 [32, 336, 1152], P(('batch', 'seq')), may hold values from -8 to 8
- lengths: int32 [32], P(('batch', 'seq')), may hold values from 1 to 77, as said below
- inflow: float32 [1152, 3456], P('batch', 'seq'), may hold values from -0.1875 to 0.1875
- outflow: float32 [1152, 1152], P('batch', 'seq'), may hold values from -1 to 1
- expand: float32 [1152, 4608], P('batch', 'seq'), may hold values from -0.1875 to 0.1875
- merging: float32 [2304, 1152], P('batch', 'seq'), may hold values from -0.125 to 0.125
- shrink: float32 [4608, 1152], P('batch', 'seq'), may hold values from -0.09375 to 0.09375
- vectors: float32 [11, 1152], P(None, 'batch'), may hold values from -3 to 3
- drift_inflow: float32 [1152, 3456], P('batch', 'seq'), may hold values from -0.0034179688 to 0.0034179688
- drift_outflow: float32 [1152, 1152], P('batch', 'seq'), may hold values from -0.0034179688 to 0.0034179688
- drift_expand: float32 [1152, 4608], P('batch', 'seq'), may hold values from -0.0034179688 to 0.0034179688
- drift_merging: float32 [2304, 1152], P('batch', 'seq'), may hold values from -0.0034179688 to 0.0034179688
- drift_shrink: float32 [4608, 1152], P('batch', 'seq'), may hold values from -0.0034179688 to 0.0034179688
- drift_vectors: float32 [11, 1152], P(None, 'batch'), may hold values from -0.009765625 to 0.009765625
- spread_inflow: float32 [1152, 3456], P('batch', 'seq'), may hold values from 5.3786206e-08 to 2.1514482e-07
- spread_outflow: float32 [1152, 1152], P('batch', 'seq'), may hold values from 5.3786206e-08 to 2.1514482e-07
- spread_expand: float32 [1152, 4608], P('batch', 'seq'), may hold values from 5.3786206e-08 to 2.1514482e-07
- spread_merging: float32 [2304, 1152], P('batch', 'seq'), may hold values from 5.3786206e-08 to 2.1514482e-07
- spread_shrink: float32 [4608, 1152], P('batch', 'seq'), may hold values from 5.3786206e-08 to 2.1514482e-07
- spread_vectors: float32 [11, 1152], P(None, 'batch'), may hold values from 4.840758e-07 to 1.9363033e-06
- shadow_inflow: float32 [1152, 3456], P('batch', 'seq'), may hold values from -0.1875 to 0.1875
- shadow_outflow: float32 [1152, 1152], P('batch', 'seq'), may hold values from -1 to 1
- shadow_expand: float32 [1152, 4608], P('batch', 'seq'), may hold values from -0.1875 to 0.1875
- shadow_merging: float32 [2304, 1152], P('batch', 'seq'), may hold values from -0.125 to 0.125
- shadow_shrink: float32 [4608, 1152], P('batch', 'seq'), may hold values from -0.09375 to 0.09375
- shadow_vectors: float32 [11, 1152], P(None, 'batch'), may hold values from -3 to 3
Outputs:
- result: float32 [32, 336, 1152], P(('batch', 'seq'))
- tokens_grad: float32 [32, 336, 1152], P(('batch', 'seq'))
- skipped_grad: float32 [32, 336, 1152], P(('batch', 'seq'))
- grad_norm: float32 [], replicated
- trained_inflow: float32 [1152, 3456], P('batch', 'seq')
- trained_outflow: float32 [1152, 1152], P('batch', 'seq')
- trained_expand: float32 [1152, 4608], P('batch', 'seq')
- trained_merging: float32 [2304, 1152], P('batch', 'seq')
- trained_shrink: float32 [4608, 1152], P('batch', 'seq')
- trained_vectors: float32 [11, 1152], P(None, 'batch')
- momentum_inflow: float32 [1152, 3456], P('batch', 'seq')
- momentum_outflow: float32 [1152, 1152], P('batch', 'seq')
- momentum_expand: float32 [1152, 4608], P('batch', 'seq')
- momentum_merging: float32 [2304, 1152], P('batch', 'seq')
- momentum_shrink: float32 [4608, 1152], P('batch', 'seq')
- momentum_vectors: float32 [11, 1152], P(None, 'batch')
- variance_inflow: float32 [1152, 3456], P('batch', 'seq')
- variance_outflow: float32 [1152, 1152], P('batch', 'seq')
- variance_expand: float32 [1152, 4608], P('batch', 'seq')
- variance_merging: float32 [2304, 1152], P('batch', 'seq')
- variance_shrink: float32 [4608, 1152], P('batch', 'seq')
- variance_vectors: float32 [11, 1152], P(None, 'batch')
- smoothed_inflow: float32 [1152, 3456], P('batch', 'seq')
- smoothed_outflow: float32 [1152, 1152], P('batch', 'seq')
- smoothed_expand: float32 [1152, 4608], P('batch', 'seq')
- smoothed_merging: float32 [2304, 1152], P('batch', 'seq')
- smoothed_shrink: float32 [4608, 1152], P('batch', 'seq')
- smoothed_vectors: float32 [11, 1152], P(None, 'batch')
- shrink_bias_grad: float32 [1152], P('batch')
Inputs may be any that keep to these rules, and one draw needn't show every extreme that they name: `lengths`: some item has 77 caption tokens and some has 1.
All inputs are finite; a program needn't handle non-finite values.
Results may differ from a plain program's by a relative error of at most 0.024.
Values may be sent and summed in bfloat16 or wider, within the bound.
No kernel may reach another device: no remote copies, remote signals or barrier semaphores. Data moves between devices by JAX's collectives and lax.ppermute only.
A program may use at most 256 MiB of HBM per device.

v0:
```python
from functools import partial

import jax
import jax.numpy as jnp
from jax import lax
from jax.sharding import PartitionSpec as P

HEADS = 16
HEAD_DIM = 72
CAP = 77
PATCHES = 256
STEP = 10


BETA = 0.5
RATES = (0.03, 0.15, 0.03, 0.03, 0.03, 0.3)
DECAY = 0.1
EPS_ADAM = 1e-08
EPS_NORM = 1e-05
SHADOW = 0.7
CLIP = 1.0
MASKED = -1000000000.0


def layer_norm(values, norm_gain, norm_shift):
    center = values - jnp.mean(values, axis=-1, keepdims=True)
    variance_row = jnp.mean(center * center, axis=-1, keepdims=True)
    return center * lax.rsqrt(variance_row + EPS_NORM) * norm_gain + norm_shift


def product(left_side, right_side):
    return jnp.dot(left_side, right_side, preferred_element_type=jnp.float32)


def adamw(master, gradient, drift, spread, shadow, clip_factor, rate):
    clipped = gradient * clip_factor
    momentum = BETA * drift + (1.0 - BETA) * clipped
    variance = BETA * spread + (1.0 - BETA) * clipped * clipped
    correction = 1.0 - BETA**STEP
    direction = momentum / correction / (jnp.sqrt(variance / correction) + EPS_ADAM)
    trained = master - rate * (direction + DECAY * master)
    smoothed = SHADOW * shadow + (1.0 - SHADOW) * trained
    return (trained, momentum, variance, smoothed)


def masked_scores(queries, key_rows, visible_row, scaling):
    scores = (
        jnp.einsum("qhd,khd->hqk", queries, key_rows, preferred_element_type=jnp.float32) * scaling
    )
    return jnp.where(visible_row[None, None, :], scores, MASKED)


def attend_item(pieces, scaling):
    head_block, visible_row = pieces
    scores = masked_scores(head_block[:, 0], head_block[:, 1], visible_row, scaling)
    peak_score = jnp.max(scores, axis=-1, keepdims=True)
    exponent = jnp.exp(scores - peak_score)
    row_total = jnp.sum(exponent, axis=-1, keepdims=True)
    attention = (exponent / row_total).astype(jnp.bfloat16)
    mixed = jnp.einsum(
        "hqk,khd->qhd", attention, head_block[:, 2], preferred_element_type=jnp.float32
    )
    return (mixed.astype(jnp.bfloat16), peak_score + jnp.log(row_total))


def attend_back(pieces, scaling):
    head_block, visible_row, log_total, upstream = pieces
    queries = head_block[:, 0]
    key_rows = head_block[:, 1]
    values = head_block[:, 2]
    scores = masked_scores(queries, key_rows, visible_row, scaling)
    attention = jnp.exp(scores - log_total)
    grad_values = jnp.einsum(
        "hqk,qhd->khd", attention.astype(jnp.bfloat16), upstream, preferred_element_type=jnp.float32
    )
    grad_attention = jnp.einsum(
        "qhd,khd->hqk", upstream, values, preferred_element_type=jnp.float32
    )
    inner_sum = jnp.sum(attention * grad_attention, axis=-1, keepdims=True)
    grad_scores = (attention * (grad_attention - inner_sum)).astype(jnp.bfloat16)
    grad_queries = (
        jnp.einsum("hqk,khd->qhd", grad_scores, key_rows, preferred_element_type=jnp.float32)
        * scaling
    )
    grad_keys = (
        jnp.einsum("hqk,qhd->khd", grad_scores, queries, preferred_element_type=jnp.float32)
        * scaling
    )
    return jnp.stack([grad_queries, grad_keys, grad_values], axis=1).astype(jnp.bfloat16)


def local(
    tokens,
    skipped,
    cotangent,
    lengths,
    inflow,
    outflow,
    expand,
    merging,
    shrink,
    vectors,
    drift_inflow,
    drift_outflow,
    drift_expand,
    drift_merging,
    drift_shrink,
    drift_vectors,
    spread_inflow,
    spread_outflow,
    spread_expand,
    spread_merging,
    spread_shrink,
    spread_vectors,
    shadow_inflow,
    shadow_outflow,
    shadow_expand,
    shadow_merging,
    shadow_shrink,
    shadow_vectors,
):
    item_count, seq_rows, model_width = tokens.shape
    seq_devices = lax.axis_size("seq")
    row_count = item_count * seq_rows
    scaling = HEAD_DIM ** (-0.5)
    halves = [weight.astype(jnp.bfloat16) for weight in (inflow, outflow, expand, merging, shrink)]
    small_half = vectors.astype(jnp.bfloat16)
    sectioned = (
        lax.all_gather(halves[0], "batch", axis=0, tiled=True),
        lax.all_gather(halves[1], "batch", axis=0, tiled=True),
        lax.all_gather(halves[2], "batch", axis=0, tiled=True),
        lax.all_gather(halves[3], "batch", axis=0, tiled=True),
        lax.all_gather(halves[4], "batch", axis=0, tiled=True),
        lax.all_gather(small_half, "batch", axis=1, tiled=True),
    )
    gathered = (
        lax.all_gather(sectioned[0], "seq", axis=1, tiled=True),
        lax.all_gather(sectioned[1], "seq", axis=1, tiled=True),
        lax.all_gather(sectioned[2], "seq", axis=1, tiled=True),
        lax.all_gather(sectioned[3], "seq", axis=1, tiled=True),
        lax.all_gather(sectioned[4], "seq", axis=1, tiled=True),
    )
    table_half = sectioned[5]
    whole_inflow, whole_outflow, whole_expand, whole_merging, whole_shrink = gathered
    table = table_half.astype(jnp.float32)
    expand_rows = whole_expand.shape[1] // model_width
    merging_bias = table[0]
    gain_one = table[1]
    shift_one = table[2]
    outflow_bias = table[3]
    gain_two = table[4]
    shift_two = table[5]
    expand_bias = table[6 : 6 + expand_rows].reshape(-1)
    shrink_bias = table[6 + expand_rows]
    flat_tokens = tokens.reshape(row_count, model_width)
    flat_skipped = skipped.reshape(row_count, model_width)
    joined = jnp.concatenate([flat_tokens, flat_skipped], axis=1)
    merged = product(joined, whole_merging) + merging_bias
    normed_wide, pull_one = jax.vjp(layer_norm, merged, gain_one, shift_one)
    normed = normed_wide.astype(jnp.bfloat16)
    packed = (
        product(normed, whole_inflow)
        .astype(jnp.bfloat16)
        .reshape(item_count, seq_rows, 3, model_width)
    )
    active_heads = HEADS
    group_items = packed.shape[0]
    head_blocks = packed.reshape(group_items, seq_rows, 3, active_heads, HEAD_DIM)
    position = jnp.arange(seq_rows)
    inner_slots = (position >= CAP) & (position < CAP + 1 + PATCHES)
    visible = (position[None, :] < lengths[:, None]) | inner_slots[None, :]
    mixed_heads, log_totals = lax.map(partial(attend_item, scaling=scaling), (head_blocks, visible))
    mixed_rows = mixed_heads.reshape(group_items, seq_rows, active_heads * HEAD_DIM)
    mixed_flat = mixed_rows.reshape(row_count, model_width)
    residual = merged + product(mixed_flat, whole_outflow) + outflow_bias
    normed_two_wide, pull_two = jax.vjp(layer_norm, residual, gain_two, shift_two)
    normed_two = normed_two_wide.astype(jnp.bfloat16)
    preact = product(normed_two, whole_expand) + expand_bias
    hidden_wide, gelu_pull = jax.vjp(partial(jax.nn.gelu, approximate=False), preact)
    hidden = hidden_wide.astype(jnp.bfloat16)
    result = residual + product(hidden, whole_shrink) + shrink_bias
    upstream = cotangent.reshape(row_count, model_width)
    upstream_wide = upstream.astype(jnp.float32)
    grad_shrink = product(hidden.T, upstream)
    grad_hidden = product(upstream, whole_shrink.T)
    grad_preact = gelu_pull(grad_hidden)[0].astype(jnp.bfloat16)
    grad_expand = product(normed_two.T, grad_preact)
    grad_normed_two = product(grad_preact, whole_expand.T)
    back_residual, grad_gain_two, grad_shift_two = pull_two(grad_normed_two)
    grad_residual = upstream_wide + back_residual
    grad_branch = grad_residual.astype(jnp.bfloat16)
    grad_outflow = product(mixed_flat.T, grad_branch)
    grad_mixed = (
        product(grad_branch, whole_outflow.T)
        .astype(jnp.bfloat16)
        .reshape(item_count, seq_rows, model_width)
    )
    grad_spread = grad_mixed
    grad_spread = grad_spread.reshape(group_items, seq_rows, active_heads, HEAD_DIM)
    grad_blocks = lax.map(
        partial(attend_back, scaling=scaling), (head_blocks, visible, log_totals, grad_spread)
    )
    grad_blocks = grad_blocks.reshape(group_items, seq_rows, 3, active_heads * HEAD_DIM)
    grad_packed = grad_blocks.reshape(row_count, 3 * model_width)
    grad_inflow = product(normed.T, grad_packed)
    grad_normed = product(grad_packed, whole_inflow.T)
    back_merged, grad_gain_one, grad_shift_one = pull_one(grad_normed)
    grad_merged = (grad_residual + back_merged).astype(jnp.bfloat16)
    grad_merging = product(joined.T, grad_merged)
    tokens_grad = product(grad_merged, whole_merging[:model_width].T).reshape(
        item_count, seq_rows, model_width
    )
    skipped_grad = product(grad_merged, whole_merging[model_width:].T).reshape(
        item_count, seq_rows, model_width
    )
    grad_table = jnp.concatenate(
        [
            jnp.sum(grad_merged.astype(jnp.float32), axis=0)[None],
            grad_gain_one[None],
            grad_shift_one[None],
            jnp.sum(grad_branch.astype(jnp.float32), axis=0)[None],
            grad_gain_two[None],
            grad_shift_two[None],
            jnp.sum(grad_preact.astype(jnp.float32), axis=0).reshape(expand_rows, model_width),
            jnp.sum(upstream_wide, axis=0)[None],
        ],
        axis=0,
    )
    partial_sums = (
        lax.psum_scatter(
            grad_inflow.astype(jnp.bfloat16), "batch", scatter_dimension=0, tiled=True
        ).astype(jnp.float32),
        lax.psum_scatter(
            grad_outflow.astype(jnp.bfloat16), "batch", scatter_dimension=0, tiled=True
        ).astype(jnp.float32),
        lax.psum_scatter(
            grad_expand.astype(jnp.bfloat16), "batch", scatter_dimension=0, tiled=True
        ).astype(jnp.float32),
        lax.psum_scatter(
            grad_merging.astype(jnp.bfloat16), "batch", scatter_dimension=0, tiled=True
        ).astype(jnp.float32),
        lax.psum_scatter(
            grad_shrink.astype(jnp.bfloat16), "batch", scatter_dimension=0, tiled=True
        ).astype(jnp.float32),
        lax.psum_scatter(
            grad_table.astype(jnp.bfloat16), "batch", scatter_dimension=1, tiled=True
        ).astype(jnp.float32),
    )
    owned_shards = (
        lax.psum_scatter(
            partial_sums[0].astype(jnp.bfloat16), "seq", scatter_dimension=1, tiled=True
        ).astype(jnp.float32),
        lax.psum_scatter(
            partial_sums[1].astype(jnp.bfloat16), "seq", scatter_dimension=1, tiled=True
        ).astype(jnp.float32),
        lax.psum_scatter(
            partial_sums[2].astype(jnp.bfloat16), "seq", scatter_dimension=1, tiled=True
        ).astype(jnp.float32),
        lax.psum_scatter(
            partial_sums[3].astype(jnp.bfloat16), "seq", scatter_dimension=1, tiled=True
        ).astype(jnp.float32),
        lax.psum_scatter(
            partial_sums[4].astype(jnp.bfloat16), "seq", scatter_dimension=1, tiled=True
        ).astype(jnp.float32),
    )
    table_part = partial_sums[5]
    table_grad = lax.psum(table_part, "seq")
    local_square = jnp.sum(table_grad * table_grad) / seq_devices
    for shard_grad in owned_shards:
        local_square = local_square + jnp.sum(shard_grad * shard_grad)
    total_square = lax.psum(local_square, ("batch", "seq"))
    grad_norm = jnp.sqrt(total_square)
    clip_factor = CLIP / jnp.maximum(grad_norm, CLIP)
    masters = (inflow, outflow, expand, merging, shrink, vectors)
    gradients = tuple(owned_shards) + (table_grad,)
    drifts = (drift_inflow, drift_outflow, drift_expand, drift_merging, drift_shrink, drift_vectors)
    spreads = (
        spread_inflow,
        spread_outflow,
        spread_expand,
        spread_merging,
        spread_shrink,
        spread_vectors,
    )
    shadows = (
        shadow_inflow,
        shadow_outflow,
        shadow_expand,
        shadow_merging,
        shadow_shrink,
        shadow_vectors,
    )
    updated = [
        adamw(
            masters[slot_index],
            gradients[slot_index],
            drifts[slot_index],
            spreads[slot_index],
            shadows[slot_index],
            clip_factor,
            RATES[slot_index],
        )
        for slot_index in range(6)
    ]
    shrink_bias_grad = table_grad[table_grad.shape[0] - 1] * clip_factor
    result_block = result.reshape(item_count, seq_rows, model_width)
    return (
        (result_block, tokens_grad, skipped_grad, grad_norm)
        + tuple((entry[0] for entry in updated))
        + tuple((entry[1] for entry in updated))
        + tuple((entry[2] for entry in updated))
        + tuple((entry[3] for entry in updated))
        + (shrink_bias_grad,)
    )


def solution(mesh):
    placed = (
        P(("batch", "seq"), None, None),
        P(("batch", "seq"), None, None),
        P(("batch", "seq"), None, None),
        P(("batch", "seq")),
        P("batch", "seq"),
        P("batch", "seq"),
        P("batch", "seq"),
        P("batch", "seq"),
        P("batch", "seq"),
        P(None, "batch"),
        P("batch", "seq"),
        P("batch", "seq"),
        P("batch", "seq"),
        P("batch", "seq"),
        P("batch", "seq"),
        P(None, "batch"),
        P("batch", "seq"),
        P("batch", "seq"),
        P("batch", "seq"),
        P("batch", "seq"),
        P("batch", "seq"),
        P(None, "batch"),
        P("batch", "seq"),
        P("batch", "seq"),
        P("batch", "seq"),
        P("batch", "seq"),
        P("batch", "seq"),
        P(None, "batch"),
    )
    return jax.shard_map(
        local,
        mesh=mesh,
        in_specs=placed,
        out_specs=(
            P(("batch", "seq"), None, None),
            P(("batch", "seq"), None, None),
            P(("batch", "seq"), None, None),
            P(),
            P("batch", "seq"),
            P("batch", "seq"),
            P("batch", "seq"),
            P("batch", "seq"),
            P("batch", "seq"),
            P(None, "batch"),
            P("batch", "seq"),
            P("batch", "seq"),
            P("batch", "seq"),
            P("batch", "seq"),
            P("batch", "seq"),
            P(None, "batch"),
            P("batch", "seq"),
            P("batch", "seq"),
            P("batch", "seq"),
            P("batch", "seq"),
            P("batch", "seq"),
            P(None, "batch"),
            P("batch", "seq"),
            P("batch", "seq"),
            P("batch", "seq"),
            P("batch", "seq"),
            P("batch", "seq"),
            P(None, "batch"),
            P("batch"),
        ),
        check_vma=False,
    )
```

profile of v0, /device:TPU:0, one launch (start us, length us, event | category | flops | bytes accessed | tf_op | source)
XLA Modules:
  0.0 1273.6 jit_solution(10518630622846288921)
XLA Ops:
  13.8 25.6 %all-gather.12.cloned.1.call-done = bf16[2304,288]{1,0:T(8,128)(2,1)} async-done(((bf16[288,288]{1,0:T(8,128)(2,1)}), bf16[2304,288]{1,0:T(8,128)(2,1)}) %all-gather.12.cloned.1.call-update) | async-done | bytes 1327120 | tf_op jit(solution)/shard_map/all_gather | solution.py:132
  42.0 28.0 %all-gather.16.cloned.1.call-done = bf16[1152,864]{1,0:T(8,128)(2,1)} async-done(((bf16[144,864]{1,0:T(8,128)(2,1)}), bf16[1152,864]{1,0:T(8,128)(2,1)}) %all-gather.16.cloned.1.call-update) | async-done | bytes 1990672 | tf_op jit(solution)/shard_map/all_gather | solution.py:129
  70.0 4.1 copy.134
  74.2 19.1 %all_gather.38 = bf16[1152,288]{1,0:T(8,128)(2,1)S(1)} all-gather(bf16[144,288]{1,0:T(8,128)(2,1)S(1)} %convert_element_type.135), channel_id=1, replica_groups=mesh['batch'=8,'seq'=4] {'batch'}, dimensions={0}, use_global_device_ids=true | all-gather | bytes 746496 | tf_op jit(solution)/shard_map/all_gather | solution.py:130
  94.6 14.7 %all-gather.22.cloned.1.call-done = bf16[1152,1152]{1,0:T(8,128)(2,1)} async-done(((bf16[144,1152]{1,0:T(8,128)(2,1)}), bf16[1152,1152]{1,0:T(8,128)(2,1)}) %all-gather.22.cloned.1.call-update) | async-done | bytes 2654224 | tf_op jit(solution)/shard_map/all_gather | solution.py:131
  109.3 38.5 %all-gather.28.cloned.1.call-done = bf16[8,576,288]{1,2,0:T(8,128)(2,1)} async-done(((bf16[1,576,288]{1,2,0:T(8,128)(2,1)}), bf16[8,576,288]{1,2,0:T(8,128)(2,1)}) %all-gather.28.cloned.1.call-update) | async-done | bytes 2654224 | tf_op jit(solution)/shard_map/all_gather | solution.py:133
  147.9 2.8 copy.138
  150.7 3.2 reshape.204
  154.0 14.3 %all-gather = bf16[8,144,11]{1,2,0:T(8,128)(2,1)S(1)} all-gather(bf16[1,144,11]{1,2,0:T(8,128)(2,1)S(1)} %convert_bitcast_fusion.1), channel_id=1, replica_groups=mesh['batch'=8,'seq'=4] {'batch'}, dimensions={0}, use_global_device_ids=true | all-gather | bytes 28512 | tf_op jit(solution)/shard_map/all_gather | solution.py:134
  169.8 41.2 %all-gather.14.cloned.1.call-done = bf16[2304,1152]{0,1:T(8,128)(2,1)} async-done(((bf16[2304,288]{0,1:T(8,128)(2,1)}), bf16[2304,1152]{0,1:T(8,128)(2,1)}) %all-gather.14.cloned.1.call-update) | async-done | bytes 5308432 | tf_op jit(solution)/shard_map/all_gather | solution.py:140
  211.0 5.1 fusion.62
  216.4 80.4 %all-gather.18.cloned.1.call-done = bf16[1152,3456]{0,1:T(8,128)(2,1)} async-done(((bf16[1152,864]{0,1:T(8,128)(2,1)}), bf16[1152,3456]{0,1:T(8,128)(2,1)}) %all-gather.18.cloned.1.call-update) | async-done | bytes 7962640 | tf_op jit(solution)/shard_map/all_gather | solution.py:137
  296.8 10.5 convolution_convert_fusion.5
  307.3 4.6 copy.135
  320.1 19.1 %all-gather.20.cloned.1.call-done = bf16[1152,1152]{0,1:T(8,128)(2,1)} async-done(((bf16[1152,288]{0,1:T(8,128)(2,1)}), bf16[1152,1152]{0,1:T(8,128)(2,1)}) %all-gather.20.cloned.1.call-update) | async-done | bytes 2654224 | tf_op jit(solution)/shard_map/all_gather | solution.py:138
  339.2 3.9 fusion.64
  345.2 102.0 %all-gather.24.cloned.1.call-done = bf16[1152,4608]{1,0:T(8,128)(2,1)} async-done(((bf16[1152,1152]{1,0:T(8,128)(2,1)}), bf16[1152,4608]{1,0:T(8,128)(2,1)}) %all-gather.24.cloned.1.call-update) | async-done | bytes 10616848 | tf_op jit(solution)/shard_map/all_gather | solution.py:139
  447.2 22.7 %multiply_convert_fusion.1 = (bf16[336,4608]{1,0:T(8,128)(2,1)}, f32[336,4608]{1,0:T(8,128)}, f32[336,4608]{1,0:T(8,128)}) fusion(f32[4608]{0:T(1024)S(1)} %add.269, bf16[1152,4608]{1,0:T(8,128)(2,1)} %all-gather.24.cloned.1.call-done, f32[336,1152]{1,0:T(8,128)} %copy-done.7, f32[1152]{0:T(1024)S(1)} %get-tuple-element.214, ...), kind=kOutput, calls=%fused_computation.17 | convolution fusion | flops 3671377920 | bytes 27678336 | tf_op jit(solution)/shard_map/dot_general | solution.py:32
  469.9 85.3 %all-gather.26.cloned.1.call-done = bf16[4608,1152]{0,1:T(8,128)(2,1)} async-done(((bf16[4608,288]{0,1:T(8,128)(2,1)}), bf16[4608,1152]{0,1:T(8,128)(2,1)}) %all-gather.26.cloned.1.call-update) | async-done | bytes 10616848 | tf_op jit(solution)/shard_map/all_gather | solution.py:141
  555.3 13.3 %fusion.65 = (bf16[4608]{0:T(1024)(128)(2,1)}, bf16[336,4608]{1,0:T(8,128)(2,1)}) fusion(f32[336,4608]{1,0:T(8,128)} %get-tuple-element.253, f32[336,4608]{1,0:T(8,128)} %get-tuple-element.260, bf16[4608,1152]{0,1:T(8,128)(2,1)} %all-gather.26.cloned.1.call-done, bf16[1,336,1152]{2,1,0:T(8,128)(2,1)S(1)} %copy-done.5), kind=kOutput, calls=%fused_computation.157 | convolution fusion | flops 3590475264 | bytes 26883072 | tf_op jit(solution)/shard_map/dot_general | solution.py:32
  568.6 6.9 multiply_reduce_fusion.1
  579.0 3.2 convolution_convert_fusion.4
  582.2 4.2 convolution_convert_fusion.6
  588.2 5.3 multiply_reduce_fusion
  601.2 3.8 multiply_reduce_fusion.2
  607.9 5.0 convolution_convert_fusion.3
  613.6 8.8 convolution_convert_fusion.2
  623.8 10.3 convolution_convert_fusion.1
  634.1 10.9 convolution_convert_fusion
  649.2 38.7 %reduce-scatter.30.cloned.1.call-done = bf16[288,1152]{1,0:T(8,128)(2,1)} async-done(((bf16[2304,1152]{1,0:T(8,128)(2,1)}), bf16[288,1152]{1,0:T(8,128)(2,1)}) %reduce-scatter.30.cloned.1.call-update) | async-done | bytes 663568 | tf_op jit(solution)/shard_map/reduce_scatter | solution.py:239
  690.3 84.0 %reduce-scatter.24.cloned.1.call-done = bf16[144,3456]{1,0:T(8,128)(2,1)} async-done(((bf16[1152,3456]{1,0:T(8,128)(2,1)}), bf16[144,3456]{1,0:T(8,128)(2,1)}) %reduce-scatter.24.cloned.1.call-update) | async-done | bytes 995344 | tf_op jit(solution)/shard_map/reduce_scatter | solution.py:230
  777.0 108.8 %reduce-scatter.28.cloned.1.call-done = bf16[144,4608]{1,0:T(8,128)(2,1)} async-done(((bf16[1152,4608]{1,0:T(8,128)(2,1)}), bf16[144,4608]{1,0:T(8,128)(2,1)}) %reduce-scatter.28.cloned.1.call-update) | async-done | bytes 1327120 | tf_op jit(solution)/shard_map/reduce_scatter | solution.py:236
  885.8 3.8 copy.162
  889.6 107.3 %reduce-scatter.32.cloned.1.call-done = bf16[576,1152]{1,0:T(8,128)(2,1)} async-done(((bf16[4608,1152]{1,0:T(8,128)(2,1)}), bf16[576,1152]{1,0:T(8,128)(2,1)}) %reduce-scatter.32.cloned.1.call-update) | async-done | bytes 1327120 | tf_op jit(solution)/shard_map/reduce_scatter | solution.py:242
  996.9 2.8 copy.166
  1007.4 4.3 convolution_bitcast_fusion
  1011.7 8.3 fusion.14
  1020.0 8.6 reduce-scatter.34.cloned.1.call-done
  1029.4 16.1 %psum.14 = f32[11,144]{1,0:T(8,128)S(1)} all-reduce(bf16[11,144]{1,0:T(8,128)(2,1)S(1)} %copy.157), channel_id=1, replica_groups=mesh['batch'=8,'seq'=4] {'seq'}, use_global_device_ids=true, to_apply=%region_20.21 | all-reduce | flops 1584 | bytes 9504 | tf_op jit(solution)/shard_map/psum | solution.py:267
  1046.8 8.4 reduce-scatter.38.cloned.1.call-done
  1056.9 28.1 %reduce-scatter.42.cloned.1.call-done = bf16[288,288]{1,0:T(8,128)(2,1)} async-done(((bf16[1152,288]{1,0:T(8,128)(2,1)}), bf16[288,288]{1,0:T(8,128)(2,1)}) %reduce-scatter.42.cloned.1.call-update) | async-done | bytes 165904
  1086.8 33.8 %reduce-scatter.36.cloned.1.call-done = bf16[864,144]{1,0:T(8,128)(2,1)} async-done(((bf16[3456,144]{1,0:T(8,128)(2,1)}), bf16[864,144]{1,0:T(8,128)(2,1)}) %reduce-scatter.36.cloned.1.call-update) | async-done | bytes 248848
  1123.9 37.5 %reduce-scatter.40.cloned.1.call-done = bf16[1152,144]{1,0:T(8,128)(2,1)} async-done(((bf16[4608,144]{1,0:T(8,128)(2,1)}), bf16[1152,144]{1,0:T(8,128)(2,1)}) %reduce-scatter.40.cloned.1.call-update) | async-done | bytes 331792
  1163.4 31.9 %reduce-scatter.44.cloned.1.call-done = bf16[288,576]{1,0:T(8,128)(2,1)} async-done(((bf16[1152,576]{1,0:T(8,128)(2,1)}), bf16[288,576]{1,0:T(8,128)(2,1)}) %reduce-scatter.44.cloned.1.call-update) | async-done | bytes 331792
  1199.4 4.5 convolution_bitcast_fusion.1
  1203.9 39.3 %psum.15 = f32[]{:T(128)} all-reduce(f32[]{:T(128)S(6)} %add.283), channel_id=1, replica_groups=mesh['batch'=8,'seq'=4] {'batch','seq'}, use_global_device_ids=true, to_apply=%region_37.38 | all-reduce | flops 1 | bytes 8 | tf_op jit(solution)/shard_map/psum | solution.py:271
  1244.5 3.7 multiply_add_fusion.2
  1258.9 3.6 multiply_add_fusion.4
  (264 shorter events, 81.4 us)
Async XLA Ops:
  7.2 32.2 %all-gather.12.cloned.1.call-start = ((), (), s32[]{:S(2)}) async-start(), calls=%async_computation.11 | async-start | bytes 1990656 | tf_op jit(solution)/shard_map/all_gather | solution.py:132
  9.1 60.9 %all-gather.16.cloned.1.call-start = ((), (), s32[]{:S(2)}) async-start(), calls=%async_computation.13 | async-start | bytes 2322432 | tf_op jit(solution)/shard_map/all_gather | solution.py:129
  10.9 98.3 %all-gather.22.cloned.1.call-start = ((), (), s32[]{:S(2)}) async-start(), calls=%async_computation.16 | async-start | bytes 2985984 | tf_op jit(solution)/shard_map/all_gather | solution.py:131
  12.8 135.0 %all-gather.28.cloned.1.call-start = ((), (), s32[]{:S(2)}) async-start(), calls=%async_computation.24 | async-start | bytes 3317760 | tf_op jit(solution)/shard_map/all_gather | solution.py:133
  13.7 197.3 %all-gather.14.cloned.1.call-start = ((), (), s32[]{:S(2)}) async-start(), calls=%async_computation.12 | async-start | bytes 6635520 | tf_op jit(solution)/shard_map/all_gather | solution.py:140
  42.0 32.2 %copy-start.25 = (f32[144,288]{1,0:T(8,128)S(1)}, f32[144,288]{1,0:T(8,128)}, u32[]{:S(2)}) copy-start(f32[144,288]{1,0:T(8,128)} %param.33) | copy-start | bytes 497668
  42.0 254.8 %all-gather.18.cloned.1.call-start = ((), (), s32[]{:S(2)}) async-start(), calls=%async_computation.14 | async-start | bytes 9953280 | tf_op jit(solution)/shard_map/all_gather | solution.py:137
  74.1 265.0 %all-gather.20.cloned.1.call-start = ((), (), s32[]{:S(2)}) async-start(), calls=%async_computation.15 | async-start | bytes 3317760 | tf_op jit(solution)/shard_map/all_gather | solution.py:138
  94.5 352.7 %all-gather.24.cloned.1.call-start = ((), (), s32[]{:S(2)}) async-start(), calls=%async_computation.17 | async-start | bytes 13271040 | tf_op jit(solution)/shard_map/all_gather | solution.py:139
  109.3 446.0 %all-gather.26.cloned.1.call-start = ((), (), s32[]{:S(2)}) async-start(), calls=%async_computation.18 | async-start | bytes 13271040 | tf_op jit(solution)/shard_map/all_gather | solution.py:141
  153.9 57.1 %copy-start.63 = (bf16[1,336,1152]{2,1,0:T(8,128)(2,1)S(1)}, bf16[1,336,1152]{2,1,0:T(8,128)(2,1)}, u32[]{:S(2)}) copy-start(bf16[1,336,1152]{2,1,0:T(8,128)(2,1)} %param.29) | copy-start | bytes 2322436
  153.9 493.1 %reduce-scatter.26.cloned.1.call-start = ((), (), s32[]{:S(2)}) async-start(), calls=%async_computation.20 | async-start | bytes 2985984 | tf_op jit(solution)/shard_map/reduce_scatter | solution.py:233
  169.8 127.0 %copy-start.58 = (f32[1152]{0:T(1024)}, f32[1152]{0:T(1024)S(1)}, u32[]{:S(2)}) copy-start(f32[1152]{0:T(1024)S(1)} %get-tuple-element.217) | copy-start | bytes 13828
  169.8 277.4 %copy-start.56 = (f32[1152]{0:T(1024)}, f32[1152]{0:T(1024)S(1)}, u32[]{:S(2)}) copy-start(f32[1152]{0:T(1024)S(1)} %get-tuple-element.214) | copy-start | bytes 13828
  169.8 405.7 %copy-start.40 = (f32[1152]{0:T(1024)}, f32[1152]{0:T(1024)S(1)}, u32[]{:S(2)}) copy-start(f32[1152]{0:T(1024)S(1)} %get-tuple-element.215) | copy-start | bytes 13828
  216.1 80.7 %copy-start.1 = (f32[336,1152]{1,0:T(8,128)}, f32[336,1152]{1,0:T(8,128)S(1)}, u32[]{:S(2)}) copy-start(f32[336,1152]{1,0:T(8,128)S(1)} %get-tuple-element.255) | copy-start | bytes 4644868
  216.4 90.9 %copy-start.44 = (f32[336]{0:T(512)}, f32[336]{0:T(512)S(1)}, u32[]{:S(2)}) copy-start(f32[336]{0:T(512)S(1)} %multiply_reduce_fusion.6) | copy-start | bytes 4036
  343.1 232.4 %copy-start.42 = (f32[336]{0:T(512)}, f32[336]{0:T(512)S(1)}, u32[]{:S(2)}) copy-start(f32[336]{0:T(512)S(1)} %broadcast_multiply_fusion) | copy-start | bytes 4036
  344.6 231.0 %copy-start.53 = (f32[336]{0:T(512)}, f32[336]{0:T(512)S(1)}, u32[]{:S(2)}) copy-start(f32[336]{0:T(512)S(1)} %fusion.47) | copy-start | bytes 4036
  447.2 108.1 %copy-start.5 = (bf16[1,336,1152]{2,1,0:T(8,128)(2,1)S(1)}, bf16[1,336,1152]{2,1,0:T(8,128)(2,1)}, u32[]{:S(2)}) copy-start(bf16[1,336,1152]{2,1,0:T(8,128)(2,1)} %param.30) | copy-start | bytes 2322436
  555.3 13.3 %copy-start.8 = (f32[336,1152]{1,0:T(8,128)S(1)}, f32[336,1152]{1,0:T(8,128)}, u32[]{:S(2)}) copy-start(f32[336,1152]{1,0:T(8,128)} %copy-done.7) | copy-start | bytes 4644868
  555.3 13.3 %copy-start.62 = (bf16[1152,4608]{1,0:T(8,128)(2,1)S(1)}, bf16[1152,4608]{1,0:T(8,128)(2,1)}, u32[]{:S(2)}) copy-start(bf16[1152,4608]{1,0:T(8,128)(2,1)} %all-gather.24.cloned.1.call-done) | copy-start | bytes 31850500
  576.1 6.1 copy-start.46
  588.1 99.8 %reduce-scatter.30.cloned.1.call-start = ((), (), s32[]{:S(2)}) async-start(), calls=%async_computation.22 | async-start | bytes 5971968 | tf_op jit(solution)/shard_map/reduce_scatter | solution.py:239
  612.9 161.4 %reduce-scatter.24.cloned.1.call-start = ((), (), s32[]{:S(2)}) async-start(), calls=%async_computation.19 | async-start | bytes 8957952 | tf_op jit(solution)/shard_map/reduce_scatter | solution.py:230
  622.4 263.3 %reduce-scatter.28.cloned.1.call-start = ((), (), s32[]{:S(2)}) async-start(), calls=%async_computation.21 | async-start | bytes 11943936 | tf_op jit(solution)/shard_map/reduce_scatter | solution.py:236
  634.1 362.8 %reduce-scatter.32.cloned.1.call-start = ((), (), s32[]{:S(2)}) async-start(), calls=%async_computation.23 | async-start | bytes 11943936 | tf_op jit(solution)/shard_map/reduce_scatter | solution.py:242
  645.1 383.5 %reduce-scatter.34.cloned.1.call-start = ((), (), s32[]{:S(2)}) async-start(), calls=%async_computation.25 | async-start | bytes 331776
  647.0 408.2 %reduce-scatter.38.cloned.1.call-start = ((), (), s32[]{:S(2)}) async-start(), calls=%async_computation.27 | async-start | bytes 737280
  649.1 435.8 %reduce-scatter.42.cloned.1.call-start = ((), (), s32[]{:S(2)}) async-start(), calls=%async_computation.29 | async-start | bytes 1105920
  690.3 430.3 %reduce-scatter.36.cloned.1.call-start = ((), (), s32[]{:S(2)}) async-start(), calls=%async_computation.26 | async-start | bytes 2211840
  776.9 384.5 %reduce-scatter.40.cloned.1.call-start = ((), (), s32[]{:S(2)}) async-start(), calls=%async_computation.28 | async-start | bytes 2949120
  889.5 110.3 %copy-start.15 = (f32[576,288]{0,1:T(8,128)S(1)}, f32[576,288]{0,1:T(8,128)}, u32[]{:S(2)}) copy-start(f32[576,288]{0,1:T(8,128)} %param.36) | copy-start | bytes 1990660
  889.6 305.8 %reduce-scatter.44.cloned.1.call-start = ((), (), s32[]{:S(2)}) async-start(), calls=%async_computation.30 | async-start | bytes 1843200
  1000.1 7.3 copy-start.28
  1056.2 28.7 %copy-start.23 = (bf16[144,288]{1,0:T(8,128)(2,1)}, bf16[144,288]{1,0:T(8,128)(2,1)S(1)}, u32[]{:S(2)}) copy-start(bf16[144,288]{1,0:T(8,128)(2,1)S(1)} %copy.161) | copy-start | bytes 248836
  1086.1 34.6 %copy-start.20 = (bf16[288,288]{1,0:T(8,128)(2,1)}, bf16[288,288]{1,0:T(8,128)(2,1)S(1)}, u32[]{:S(2)}) copy-start(bf16[288,288]{1,0:T(8,128)(2,1)S(1)} %copy.165) | copy-start | bytes 497668
  1121.8 73.6 %copy-start.17 = (bf16[144,864]{1,0:T(8,128)(2,1)}, bf16[144,864]{1,0:T(8,128)(2,1)S(1)}, u32[]{:S(2)}) copy-start(bf16[144,864]{1,0:T(8,128)(2,1)S(1)} %copy.159) | copy-start | bytes 746500
  1199.4 45.1 %copy-start.10 = (f32[576,288]{1,0:T(8,128)S(1)}, f32[576,288]{1,0:T(8,128)}, u32[]{:S(2)}) copy-start(f32[576,288]{1,0:T(8,128)} %copy.143) | copy-start | bytes 1990660
  1199.4 45.1 %copy-start.11 = (f32[576,288]{1,0:T(8,128)S(1)}, f32[576,288]{1,0:T(8,128)}, u32[]{:S(2)}) copy-start(f32[576,288]{1,0:T(8,128)} %copy.144) | copy-start | bytes 1990660
  1248.2 6.1 copy-start.12
  1248.2 7.3 copy-start.39
  1248.2 7.3 copy-start.49
  1248.2 7.3 copy-start.50
  1248.2 7.2 copy-start.51
  1248.2 7.9 copy-start.21
  1248.2 7.9 copy-start.22
  1248.3 7.9 copy-start.33
  (44 other events, 128.6 us)
Sparse Core Ops, SparseCore 0:
  10.3 29.0 all-gather.11
  41.6 28.3 all-gather.15
  72.2 36.9 all-gather.21
  111.3 36.4 all-gather.27
  150.1 60.8 all-gather.13
  212.7 84.0 all-gather.17
  299.2 39.9 all-gather.19
  341.0 106.1 all-gather.23
  449.0 106.1 all-gather.25
  588.2 37.7 reduce-scatter.25
  628.4 59.4 reduce-scatter.29
  690.0 84.1 reduce-scatter.23
  776.7 109.0 reduce-scatter.27
  887.9 108.9 reduce-scatter.31
  999.7 28.8 reduce-scatter.33
  1031.9 23.2 reduce-scatter.37
  1058.2 26.6 reduce-scatter.41
  1088.1 32.4 reduce-scatter.35
  1124.0 37.3 reduce-scatter.39
  1165.0 30.3 reduce-scatter.43
where the time goes:
time: 1280 us; the launch traced here: 1270 us
  waiting for transfers between devices  922 us (72%)
  matrix products  140 us (11%)
  blocking collectives  88.8 us (7%)
  local copies, waits for them, and re-layouts  68.5 us (5%)
  other arithmetic  31.8 us (2%)
  between operations  21.8 us (2%)
    unnamed x26, waiting for transfers between devices  149 us
    dot_general x16, matrix products, product(): return jnp.dot(left_side, right_side, preferred_element_type=jnp.float32)  126 us
    reduce_scatter x1, waiting for transfers between devices, local(): lax.psum_scatter(grad_expand.astype(jnp.bfloat16), 'batch', scatter_dimen...  109 us
    reduce_scatter x1, waiting for transfers between devices, local(): lax.psum_scatter(grad_shrink.astype(jnp.bfloat16), 'batch', scatter_dimen...  107 us
    all_gather x1, waiting for transfers between devices, local(): lax.all_gather(sectioned[2], 'seq', axis=1, tiled=True)  102 us
    all_gather x1, waiting for transfers between devices, local(): lax.all_gather(sectioned[4], 'seq', axis=1, tiled=True)  85.3 us
    reduce_scatter x1, waiting for transfers between devices, local(): lax.psum_scatter(grad_inflow.astype(jnp.bfloat16), 'batch', scatter_dimen...  84 us
    all_gather x1, waiting for transfers between devices, local(): lax.all_gather(sectioned[0], 'seq', axis=1, tiled=True)  80.4 us
  transfers between devices with their start and end apart: 20, of which 19 were waited for; matrix products, arithmetic and copies ran while one was open for 13% of the time, Pallas kernels for 0%

commit v1 on v0

v1 whole, which is shorter than its diff:
```python
from functools import partial

import jax
import jax.numpy as jnp
from jax import lax
from jax.experimental import pallas as pl
from jax.experimental.pallas import tpu as pltpu
from jax.sharding import PartitionSpec as P

HEADS = 16
HEAD_DIM = 72
CAP = 77
PATCHES = 256
STEP = 10


BETA = 0.5
RATES = (0.03, 0.15, 0.03, 0.03, 0.03, 0.3)
DECAY = 0.1
EPS_ADAM = 1e-08
EPS_NORM = 1e-05
SHADOW = 0.7
CLIP = 1.0
MASKED = -1000000000.0


def adamw(master, gradient, drift, spread, shadow, clip_factor, rate):
    clipped = gradient * clip_factor
    momentum = BETA * drift + (1.0 - BETA) * clipped
    variance = BETA * spread + (1.0 - BETA) * clipped * clipped
    correction = 1.0 - BETA**STEP
    direction = momentum / correction / (jnp.sqrt(variance / correction) + EPS_ADAM)
    trained = master - rate * (direction + DECAY * master)
    smoothed = SHADOW * shadow + (1.0 - SHADOW) * trained
    return (trained, momentum, variance, smoothed)


class Grid:
    def __init__(self):
        self.batch, self.seq = lax.axis_size("batch"), lax.axis_size("seq")
        self.depth = self.batch // 2
        self.b, self.j = lax.axis_index("batch"), lax.axis_index("seq")
        self.z, self.c = self.b // 2, self.b % 2

    def plane(self, value, k):
        if k == 0:
            return value
        return lax.ppermute(value, "seq", [(j, j ^ k) for j in range(self.seq)])

    def line(self, value, k):
        return lax.ppermute(value, "batch", [(b, b ^ (2 * k)) for b in range(self.batch)])

    def core(self, value):
        return lax.ppermute(value, "batch", [(b, b ^ 1) for b in range(self.batch)])


def gather_pieces(grid, shard):
    column = [shard]
    step = 1
    while step < grid.depth:
        column = column + [grid.line(piece, step) for piece in column]
        step *= 2
    column = jnp.stack(column)
    pieces = [grid.plane(column, k) for k in range(grid.seq)]
    return pieces + [grid.core(piece) for piece in pieces]


def swap_plane(grid, parts):
    came = [
        grid.plane(lax.dynamic_index_in_dim(parts, grid.j ^ k, 0, keepdims=False), k)
        for k in range(grid.seq)
    ]
    bit = 1
    while bit < grid.seq:
        came = [
            jnp.where((grid.j & bit) != 0, came[k ^ bit], came[k]) for k in range(grid.seq)
        ]
        bit *= 2
    return came


def scatter_pieces(grid, own, other):
    wide = lambda value: value.astype(jnp.float32)
    low = lambda value: value.astype(jnp.bfloat16)
    order = list(range(1, grid.seq)) + [0]
    halves = {k: low(wide(own[k]) + wide(grid.core(other[k]))) for k in order}
    came = [halves[0]] + [grid.plane(halves[k], k) for k in range(1, grid.seq)]
    step = grid.depth // 2
    column = None
    while step >= 1:
        if column is None:
            away = low(sum(wide(piece[step:]) for piece in came))
            kept = sum(wide(piece[:step]) for piece in came)
        else:
            away, kept = low(column[step:]), column[:step]
        column = kept + wide(grid.line(away, step))
        step //= 2
    return column[0]


def sum_all(grid, value):
    value = value + grid.core(value)
    for shift, size in ((grid.plane, grid.seq), (grid.line, grid.depth)):
        terms = [value] + [shift(value, k) for k in range(1, size)]
        while len(terms) > 1:
            terms = [terms[n] + terms[n + 1] for n in range(0, len(terms), 2)]
        value = terms[0]
    return value


def dot(left_side, right_side, contract=((1,), (0,))):
    return lax.dot_general(
        left_side, right_side, (contract, ((), ())), preferred_element_type=jnp.float32
    )


NN, NT, TN = ((1,), (0,)), ((1,), (1,)), ((0,), (0,))


def fetch(depth, seq, where_ref, pieces, into, sems):
    groups = [[] for _ in range(seq)]
    for core in range(2):
        for k in range(seq):
            for i in range(depth):
                row = (where_ref[0] ^ i) * 2 + (where_ref[1] ^ core)
                copy = pltpu.make_async_copy(
                    pieces[core * seq + k].at[i],
                    into.at[where_ref[2] ^ k, row],
                    sems.at[(core * seq + k) * depth + i],
                )
                copy.start()
                groups[k].append(copy)
    return [copy for group in groups for copy in group]


def weight_rows(buffer, q):
    _, batch, rows, cols = buffer.shape
    return buffer[q].reshape(batch * rows, cols)


def norm_rows(values):
    center = values - jnp.mean(values, axis=-1, keepdims=True)
    scale = lax.rsqrt(jnp.mean(center * center, axis=-1, keepdims=True) + EPS_NORM)
    return center * scale, scale


def norm_pull(grads, gain, values):
    unit, scale = norm_rows(values)
    inner = grads * gain
    back = scale * (
        inner
        - jnp.mean(inner, axis=-1, keepdims=True)
        - unit * jnp.mean(inner * unit, axis=-1, keepdims=True)
    )
    return back, jnp.sum(grads * unit, axis=0, keepdims=True), jnp.sum(grads, axis=0, keepdims=True)


def merge_kernel(depth, seq, where_ref, tokens_ref, skipped_ref, table_ref, *refs):
    pieces, (merged_ref, normed_ref, weight, sems) = refs[: 2 * seq], refs[2 * seq :]
    for copy in fetch(depth, seq, where_ref, pieces, weight, sems):
        copy.wait()
    half = tokens_ref.shape[1]
    blocks = []
    for q in range(seq):
        block = weight_rows(weight, q)
        blocks.append(dot(tokens_ref[...], block[:half]) + dot(skipped_ref[...], block[half:]))
    merged = jnp.concatenate(blocks, axis=1) + table_ref[0:1]
    merged_ref[...] = merged
    normed_ref[...] = (norm_rows(merged)[0] * table_ref[1:2] + table_ref[2:3]).astype(jnp.bfloat16)


def head_of(packed_ref, part, head):
    per_block = packed_ref.shape[2] // HEAD_DIM
    slot = part * HEADS + head
    start = slot % per_block * HEAD_DIM
    return packed_ref[slot // per_block][:, start : start + HEAD_DIM]


def seen_keys(length, rows):
    position = lax.broadcasted_iota(jnp.int32, (1, rows), 1)
    return (position < length) | ((position >= CAP) & (position < CAP + 1 + PATCHES))


def attend_kernel(depth, seq, where_ref, length_ref, normed_ref, merged_ref, table_ref, *refs):
    pieces, rest = refs[: 2 * seq], refs[2 * seq :]
    packed_ref, mixed_ref, logs_ref, residual_ref, normed_two_ref, weight, sems = rest
    for copy in fetch(depth, seq, where_ref, pieces, weight, sems):
        copy.wait()
    split = packed_ref.shape[2]
    rows = normed_ref.shape[0]
    for q in range(seq):
        packed_ref[q] = dot(normed_ref[...], weight_rows(weight, q)[:, :split]).astype(jnp.bfloat16)
    seen = seen_keys(length_ref[0], rows)
    outs, logs = [], []
    for head in range(HEADS):
        query, key, value = (head_of(packed_ref, part, head) for part in range(3))
        scores = jnp.where(seen, dot(query, key, NT) * HEAD_DIM ** (-0.5), MASKED)
        peak = jnp.max(scores, axis=-1, keepdims=True)
        exponent = jnp.exp(scores - peak)
        total = jnp.sum(exponent, axis=-1, keepdims=True)
        outs.append(dot((exponent / total).astype(jnp.bfloat16), value))
        logs.append(peak + jnp.log(total))
    mixed = jnp.concatenate(outs, axis=1).astype(jnp.bfloat16)
    mixed_ref[...] = mixed
    logs_ref[...] = jnp.concatenate(logs, axis=1)
    blocks = [dot(mixed, weight_rows(weight, q)[:, split:]) for q in range(seq)]
    residual = merged_ref[...] + jnp.concatenate(blocks, axis=1) + table_ref[3:4]
    residual_ref[...] = residual
    normed_two = norm_rows(residual)[0] * table_ref[4:5] + table_ref[5:6]
    normed_two_ref[...] = normed_two.astype(jnp.bfloat16)


def error_function(value):
    value = jnp.clip(value, -3.832506856900711, 3.832506856900711)
    square = value * value
    top = jnp.float32(0.00022905065861350646)
    for factor in (0.0034082910107109506, 0.050955695062380861, 0.18520832239976145, 1.128379143519084):
        top = top * square + factor
    under = jnp.float32(-1.1791602954361697e-7)
    for factor in (0.000023547966471313185, 0.0010179625278914885, 0.014070470171167667, 0.11098505178285362, 0.49746925110067538, 1.0):
        under = under * square + factor
    return value * top / under


def hidden_kernel(seq, *refs):
    cots, shrink_ref, outs = refs[:seq], refs[seq], refs[seq + 1 :]
    for k in range(seq):
        outs[k][...] = dot(cots[k][...], shrink_ref[...], NT)


def feed_kernel(norm_ref, gradient_ref, expand_ref, shrink_ref, bias_ref, *refs):
    hidden_ref, grad_preact_ref, forth_ref, back_ref, sums_ref = refs
    preact = dot(norm_ref[...], expand_ref[...]) + bias_ref[...]
    bell = 0.5 + 0.5 * error_function(preact * 0.7071067811865476)
    hidden = (preact * bell).astype(jnp.bfloat16)
    hidden_ref[...] = hidden
    slope = bell + preact * (jnp.exp(preact * preact * -0.5) * 0.3989422804014327)
    grad_preact = (gradient_ref[...] * slope).astype(jnp.bfloat16)
    grad_preact_ref[...] = grad_preact
    sums_ref[...] = jnp.sum(grad_preact.astype(jnp.float32), axis=0, keepdims=True)
    back_ref[...] = dot(grad_preact, expand_ref[...], NT).astype(jnp.bfloat16)
    forth_ref[...] = dot(hidden, shrink_ref[...]).astype(jnp.bfloat16)


def feed_weights_kernel(seq, *refs):
    norms, grads, hiddens, cots = (refs[n * seq : (n + 1) * seq] for n in range(4))
    expand_ref, shrink_ref = refs[4 * seq :]
    expand = sum(dot(norms[k][...], grads[k][...], TN) for k in range(seq))
    expand_ref[...] = expand.astype(jnp.bfloat16)
    shrink = sum(dot(hiddens[k][...], cots[k][...], TN) for k in range(seq))
    shrink_ref[...] = shrink.astype(jnp.bfloat16)


def attend_back_kernel(depth, seq, where_ref, length_ref, cot_ref, residual_ref, table_ref, packed_ref, logs_ref, *refs):
    backs, pieces, rest = refs[:seq], refs[seq : 3 * seq], refs[3 * seq :]
    branch_ref, grad_residual_ref, grad_packed_ref, sums_ref, weight, sems = rest
    copies = fetch(depth, seq, where_ref, pieces, weight, sems)
    wide = lambda value: value.astype(jnp.float32)
    grads = sum(wide(back[...]) for back in backs)
    back, gain_sum, shift_sum = norm_pull(grads, table_ref[4:5], residual_ref[...])
    upstream = wide(cot_ref[...])
    grad_residual = upstream + back
    grad_residual_ref[...] = grad_residual
    branch = grad_residual.astype(jnp.bfloat16)
    wing = branch_ref.shape[2]
    for q in range(seq):
        branch_ref[q] = branch[:, q * wing : (q + 1) * wing]
    sums_ref[0:1] = gain_sum
    sums_ref[1:2] = shift_sum
    sums_ref[2:3] = jnp.sum(wide(branch), axis=0, keepdims=True)
    sums_ref[3:4] = jnp.sum(upstream, axis=0, keepdims=True)
    for copy in copies:
        copy.wait()
    split = packed_ref.shape[2]
    rows = cot_ref.shape[0]
    grad_mixed = sum(
        dot(branch_ref[q], weight_rows(weight, q)[:, split:], NT)
        for q in range(seq)
    ).astype(jnp.bfloat16)
    seen = seen_keys(length_ref[0], rows)
    scaling = HEAD_DIM ** (-0.5)
    found = [[], [], []]
    for head in range(HEADS):
        query, key, value = (head_of(packed_ref, part, head) for part in range(3))
        upper = grad_mixed[:, head * HEAD_DIM : (head + 1) * HEAD_DIM]
        scores = jnp.where(seen, dot(query, key, NT) * scaling, MASKED)
        attention = jnp.exp(scores - logs_ref[:, head : head + 1])
        grad_attention = dot(upper, value, NT)
        inner = jnp.sum(attention * grad_attention, axis=-1, keepdims=True)
        grad_scores = (attention * (grad_attention - inner)).astype(jnp.bfloat16)
        found[0].append(dot(grad_scores, key) * scaling)
        found[1].append(dot(grad_scores, query, TN) * scaling)
        found[2].append(dot(attention.astype(jnp.bfloat16), upper, TN))
    slots = found[0] + found[1] + found[2]
    per_block = split // HEAD_DIM
    for q in range(seq):
        block = jnp.concatenate(slots[q * per_block : (q + 1) * per_block], axis=1)
        grad_packed_ref[q] = block.astype(jnp.bfloat16)


def send_out(depth, where_ref, staged, own_ref, other_ref, sems, base):
    copies = []
    for i in range(depth):
        for core, target in ((0, own_ref), (1, other_ref)):
            copy = pltpu.make_async_copy(
                staged.at[2 * i + (where_ref[1] ^ core)],
                target.at[where_ref[0] ^ i],
                sems.at[base + 2 * i + core],
            )
            copy.start()
            copies.append(copy)
    return copies


def both_weights_kernel(depth, seq, where_ref, normed_ref, mixed_ref, grad_packed_ref, branch_ref, *refs):
    own, other, (staged, sems) = refs[:seq], refs[seq : 2 * seq], refs[2 * seq :]
    copies = []
    for k in reversed(range(seq)):
        q = where_ref[2] ^ k
        first = dot(normed_ref[...], grad_packed_ref[q], TN)
        second = dot(mixed_ref[...], branch_ref[q], TN)
        block = jnp.concatenate([first, second], axis=1).astype(jnp.bfloat16)
        staged[k] = block.reshape(staged.shape[1:])
        copies += send_out(depth, where_ref, staged.at[k], own[k], other[k], sems, k * 2 * depth)
    for copy in copies:
        copy.wait()


def merge_weights_kernel(depth, seq, where_ref, tokens_ref, skipped_ref, grad_ref, *refs):
    own, other, (staged, sems) = refs[:seq], refs[seq : 2 * seq], refs[2 * seq :]
    copies = []
    for k in reversed(range(seq)):
        grads = grad_ref[where_ref[2] ^ k]
        first = dot(tokens_ref[...], grads, TN).astype(jnp.bfloat16)
        second = dot(skipped_ref[...], grads, TN).astype(jnp.bfloat16)
        block = jnp.concatenate([first, second], axis=0)
        staged[k] = block.reshape(staged.shape[1:])
        copies += send_out(depth, where_ref, staged.at[k], own[k], other[k], sems, k * 2 * depth)
    for copy in copies:
        copy.wait()


def norm_back_kernel(depth, seq, where_ref, grad_packed_ref, merged_ref, table_ref, grad_residual_ref, *refs):
    pieces, rest = refs[: 2 * seq], refs[2 * seq :]
    grad_merged_ref, sums_ref, weight, sems = rest
    for copy in fetch(depth, seq, where_ref, pieces, weight, sems):
        copy.wait()
    split = grad_packed_ref.shape[2]
    grads = sum(dot(grad_packed_ref[q], weight_rows(weight, q)[:, :split], NT) for q in range(seq))
    back, gain_sum, shift_sum = norm_pull(grads, table_ref[1:2], merged_ref[...])
    grad_merged = (grad_residual_ref[...] + back).astype(jnp.bfloat16)
    wing = grad_merged_ref.shape[2]
    for q in range(seq):
        grad_merged_ref[q] = grad_merged[:, q * wing : (q + 1) * wing]
    sums_ref[0:1] = jnp.sum(grad_merged.astype(jnp.float32), axis=0, keepdims=True)
    sums_ref[1:2] = gain_sum
    sums_ref[2:3] = shift_sum


def joined_back_kernel(depth, seq, where_ref, grad_ref, *refs):
    pieces, rest = refs[: 2 * seq], refs[2 * seq :]
    tokens_ref, skipped_ref, weight, sems = rest
    for copy in fetch(depth, seq, where_ref, pieces, weight, sems):
        copy.wait()
    half = tokens_ref.shape[1]
    blocks = [weight_rows(weight, q) for q in range(seq)]
    tokens_ref[...] = sum(dot(grad_ref[q], blocks[q][:half], NT) for q in range(seq))
    skipped_ref[...] = sum(dot(grad_ref[q], blocks[q][half:], NT) for q in range(seq))


VMEM = pl.BlockSpec(memory_space=pltpu.VMEM)
SMEM = pl.BlockSpec(memory_space=pltpu.SMEM)
ANY = pl.BlockSpec(memory_space=pl.ANY)


def call(kernel, outs, specs, operands, out_specs=None, scratch=(), flops=0, name=None):
    single = not isinstance(outs, (list, tuple))
    shapes = [outs] if single else list(outs)
    found = pl.pallas_call(
        kernel,
        out_shape=[jax.ShapeDtypeStruct(shape, kind) for shape, kind in shapes],
        in_specs=specs,
        out_specs=out_specs or [VMEM] * len(shapes),
        scratch_shapes=list(scratch),
        compiler_params=pltpu.CompilerParams(vmem_limit_bytes=52 * 1024 * 1024),
        cost_estimate=pl.CostEstimate(flops=flops, bytes_accessed=flops // 300, transcendentals=0),
        name=name,
    )(*operands)
    return found


def local(
    tokens,
    skipped,
    cotangent,
    lengths,
    inflow,
    outflow,
    expand,
    merging,
    shrink,
    vectors,
    drift_inflow,
    drift_outflow,
    drift_expand,
    drift_merging,
    drift_shrink,
    drift_vectors,
    spread_inflow,
    spread_outflow,
    spread_expand,
    spread_merging,
    spread_shrink,
    spread_vectors,
    shadow_inflow,
    shadow_outflow,
    shadow_expand,
    shadow_merging,
    shadow_shrink,
    shadow_vectors,
):

    item_count, seq_rows, model_width = tokens.shape
    row_count = item_count * seq_rows
    grid = Grid()
    S, B, Z = grid.seq, grid.batch, grid.depth
    low = lambda value: value.astype(jnp.bfloat16)
    wide = lambda value: value.astype(jnp.float32)
    bf16, f32 = jnp.bfloat16, jnp.float32
    where = jnp.stack([grid.z, grid.c, grid.j]).astype(jnp.int32)

    table = wide(lax.all_gather(low(vectors), "batch", axis=1, tiled=True))
    merge_rows, merge_cols = merging.shape
    in_rows, in_cols = inflow.shape
    both_cols = in_cols + outflow.shape[1]
    merge_pieces = gather_pieces(grid, low(merging))
    both_pieces = gather_pieces(grid, jnp.concatenate([low(inflow), low(outflow)], axis=1))

    unit = shrink.shape[0] // S
    send_expand = low(expand).reshape(expand.shape[0], B // S, S, unit).transpose(2, 0, 1, 3)
    send_expand = send_expand.reshape(S, expand.shape[0], -1)
    send_shrink = low(shrink).reshape(S, unit, shrink.shape[1])
    expand_rows_own = jnp.concatenate(swap_plane(grid, send_expand), axis=1)
    shrink_rows_own = jnp.concatenate(swap_plane(grid, send_shrink), axis=1)
    expand_part = lax.all_gather(expand_rows_own, "batch", axis=0, tiled=True)
    shrink_part = lax.all_gather(shrink_rows_own, "batch", axis=0, tiled=True)
    units = expand_part.shape[1]

    flat_tokens = tokens.reshape(row_count, model_width)
    flat_skipped = skipped.reshape(row_count, model_width)
    upstream = cotangent.reshape(row_count, model_width)
    upstreams = [grid.plane(upstream, k) for k in range(S)]

    ff_rows = vectors.shape[0] - 7
    expand_bias = table[6 : 6 + ff_rows].reshape(B, S, unit)
    expand_bias = lax.dynamic_index_in_dim(expand_bias, grid.j, 1, keepdims=False).reshape(1, -1)
    shrink_bias = table[6 + ff_rows]

    wide_rows = ((row_count, model_width), f32)
    low_rows = ((row_count, model_width), bf16)
    merge_scratch = [
        pltpu.VMEM((S, B, merge_rows, merge_cols), bf16),
        pltpu.SemaphoreType.DMA((2 * S * Z,)),
    ]
    both_scratch = [
        pltpu.VMEM((S, B, in_rows, both_cols), bf16),
        pltpu.SemaphoreType.DMA((2 * S * Z,)),
    ]
    many = [ANY] * (2 * S)
    layer_flops = 2 * row_count * model_width * model_width

    merged, normed = call(
        partial(merge_kernel, Z, S),
        [wide_rows, low_rows],
        [SMEM, VMEM, VMEM, VMEM] + many,
        (where, flat_tokens, flat_skipped, table, *merge_pieces),
        scratch=merge_scratch,
        flops=2 * layer_flops,
    )
    packed, mixed, logs, residual, normed_two = call(
        partial(attend_kernel, Z, S),
        [
            ((S, row_count, in_cols), bf16),
            low_rows,
            ((row_count, HEADS), f32),
            wide_rows,
            low_rows,
        ],
        [SMEM, SMEM, VMEM, VMEM, VMEM] + many,
        (where, lengths, normed, merged, table, *both_pieces),
        scratch=both_scratch,
        flops=6 * layer_flops,
    )
    norms = [grid.plane(normed_two, k) for k in range(S)]

    unit_rows = ((row_count, units), f32)
    low_units = ((row_count, units), bf16)
    grad_hiddens = call(
        partial(hidden_kernel, S),
        [unit_rows] * S,
        [VMEM] * (S + 1),
        (*upstreams, shrink_part),
        flops=S * layer_flops,
    )
    fed = [
        call(
            feed_kernel,
            [low_units, low_units, low_rows, low_rows, ((1, units), f32)],
            [VMEM] * 5,
            (norms[k], grad_hiddens[k], expand_part, shrink_part, expand_bias),
            flops=4 * layer_flops,
        )
        for k in range(S)
    ]
    hiddens, grad_preacts, forths, backs, unit_sums = zip(*fed)
    backs = [grid.plane(backs[k], k) for k in range(S)]
    grad_expand, grad_shrink = call(
        partial(feed_weights_kernel, S),
        [((model_width, units), bf16), ((units, model_width), bf16)],
        [VMEM] * (4 * S),
        (*norms, *grad_preacts, *hiddens, *upstreams),
        flops=2 * S * layer_flops,
    )
    forths = [grid.plane(forths[k], k) for k in range(S)]
    result = residual + sum(wide(piece) for piece in forths) + shrink_bias
    own_expand = lax.psum_scatter(grad_expand.reshape(B, -1, units), "batch", scatter_dimension=0)
    own_shrink = lax.psum_scatter(grad_shrink.reshape(B, unit, -1), "batch", scatter_dimension=0)
    back_expand = own_expand.reshape(own_expand.shape[0], S, -1).transpose(1, 0, 2)
    back_shrink = own_shrink.reshape(unit, S, -1).transpose(1, 0, 2)
    shard_expand = jnp.stack(swap_plane(grid, back_expand), axis=0)
    shard_expand = shard_expand.reshape(S, expand.shape[0], B // S, unit).transpose(1, 2, 0, 3)
    shard_expand = wide(shard_expand).reshape(expand.shape)
    shard_shrink = wide(jnp.stack(swap_plane(grid, back_shrink), axis=0)).reshape(shrink.shape)

    branches, grad_residual, grad_packed, sums_two = call(
        partial(attend_back_kernel, Z, S),
        [
            ((S, row_count, merge_cols), bf16),
            wide_rows,
            ((S, row_count, in_cols), bf16),
            ((8, model_width), f32),
        ],
        [SMEM, SMEM] + [VMEM] * (5 + S) + many,
        (where, lengths, upstream, residual, table, packed, logs, *backs, *both_pieces),
        scratch=both_scratch,
        flops=4 * layer_flops,
    )
    own_both, other_both = [], []
    found = call(
        partial(both_weights_kernel, Z, S),
        [((Z, in_rows, both_cols), bf16)] * (2 * S),
        [SMEM] + [VMEM] * 4,
        (where, normed, mixed, grad_packed, branches),
        out_specs=[ANY] * (2 * S),
        scratch=[pltpu.VMEM((S, B, in_rows, both_cols), bf16), pltpu.SemaphoreType.DMA((S * B,))],
        flops=4 * layer_flops,
    )
    shard_both = scatter_pieces(grid, found[:S], found[S:])
    shard_inflow, shard_outflow = shard_both[:, :in_cols], shard_both[:, in_cols:]
    grad_merged, sums_one = call(
        partial(norm_back_kernel, Z, S),
        [((S, row_count, merge_cols), bf16), ((8, model_width), f32)],
        [SMEM] + [VMEM] * 4 + many,
        (where, grad_packed, merged, table, grad_residual, *both_pieces),
        scratch=both_scratch,
        flops=3 * layer_flops,
    )
    found = call(
        partial(merge_weights_kernel, Z, S),
        [((Z, merge_rows, merge_cols), bf16)] * (2 * S),
        [SMEM] + [VMEM] * 3,
        (where, flat_tokens, flat_skipped, grad_merged),
        out_specs=[ANY] * (2 * S),
        scratch=[pltpu.VMEM((S, B, merge_rows, merge_cols), bf16), pltpu.SemaphoreType.DMA((S * B,))],
        flops=2 * layer_flops,
    )
    shard_merging = scatter_pieces(grid, found[:S], found[S:])
    tokens_grad, skipped_grad = call(
        partial(joined_back_kernel, Z, S),
        [wide_rows, wide_rows],
        [SMEM, VMEM] + many,
        (where, grad_merged, *merge_pieces),
        scratch=merge_scratch,
        flops=2 * layer_flops,
    )
    tokens_grad = tokens_grad.reshape(tokens.shape)
    skipped_grad = skipped_grad.reshape(tokens.shape)

    expand_sums = sum(unit_sums).reshape(B, 1, unit)
    expand_sums = lax.dynamic_update_slice(jnp.zeros((B, S, unit), f32), expand_sums, (0, grid.j, 0))
    grad_table = jnp.concatenate(
        [sums_one[:3], sums_two[2:3], sums_two[:2], expand_sums.reshape(ff_rows, model_width), sums_two[3:4]],
        axis=0,
    )
    whole_table = sum_all(grid, grad_table)
    table_grad = lax.dynamic_slice_in_dim(whole_table, grid.b * vectors.shape[1], vectors.shape[1], 1)
    gradients = (shard_inflow, shard_outflow, shard_expand, shard_merging, shard_shrink, table_grad)
    local_square = jnp.sum(table_grad * table_grad) / S
    for shard_grad in gradients[:5]:
        local_square = local_square + jnp.sum(shard_grad * shard_grad)
    total_square = sum_all(grid, local_square)
    grad_norm = jnp.sqrt(total_square)
    clip_factor = CLIP / jnp.maximum(grad_norm, CLIP)
    masters = (inflow, outflow, expand, merging, shrink, vectors)
    drifts = (drift_inflow, drift_outflow, drift_expand, drift_merging, drift_shrink, drift_vectors)
    spreads = (
        spread_inflow,
        spread_outflow,
        spread_expand,
        spread_merging,
        spread_shrink,
        spread_vectors,
    )
    shadows = (
        shadow_inflow,
        shadow_outflow,
        shadow_expand,
        shadow_merging,
        shadow_shrink,
        shadow_vectors,
    )
    updated = [
        adamw(
            masters[slot_index],
            gradients[slot_index],
            drifts[slot_index],
            spreads[slot_index],
            shadows[slot_index],
            clip_factor,
            RATES[slot_index],
        )
        for slot_index in range(6)
    ]
    shrink_bias_grad = table_grad[table_grad.shape[0] - 1] * clip_factor
    result_block = result.reshape(tokens.shape)
    return (
        (result_block, tokens_grad, skipped_grad, grad_norm)
        + tuple((entry[0] for entry in updated))
        + tuple((entry[1] for entry in updated))
        + tuple((entry[2] for entry in updated))
        + tuple((entry[3] for entry in updated))
        + (shrink_bias_grad,)
    )


def solution(mesh):
    placed = (
        P(("batch", "seq"), None, None),
        P(("batch", "seq"), None, None),
        P(("batch", "seq"), None, None),
        P(("batch", "seq")),
        P("batch", "seq"),
        P("batch", "seq"),
        P("batch", "seq"),
        P("batch", "seq"),
        P("batch", "seq"),
        P(None, "batch"),
        P("batch", "seq"),
        P("batch", "seq"),
        P("batch", "seq"),
        P("batch", "seq"),
        P("batch", "seq"),
        P(None, "batch"),
        P("batch", "seq"),
        P("batch", "seq"),
        P("batch", "seq"),
        P("batch", "seq"),
        P("batch", "seq"),
        P(None, "batch"),
        P("batch", "seq"),
        P("batch", "seq"),
        P("batch", "seq"),
        P("batch", "seq"),
        P("batch", "seq"),
        P(None, "batch"),
    )
    return jax.shard_map(
        local,
        mesh=mesh,
        in_specs=placed,
        out_specs=(
            P(("batch", "seq"), None, None),
            P(("batch", "seq"), None, None),
            P(("batch", "seq"), None, None),
            P(),
            P("batch", "seq"),
            P("batch", "seq"),
            P("batch", "seq"),
            P("batch", "seq"),
            P("batch", "seq"),
            P(None, "batch"),
            P("batch", "seq"),
            P("batch", "seq"),
            P("batch", "seq"),
            P("batch", "seq"),
            P("batch", "seq"),
            P(None, "batch"),
            P("batch", "seq"),
            P("batch", "seq"),
            P("batch", "seq"),
            P("batch", "seq"),
            P("batch", "seq"),
            P(None, "batch"),
            P("batch", "seq"),
            P("batch", "seq"),
            P("batch", "seq"),
            P("batch", "seq"),
            P("batch", "seq"),
            P(None, "batch"),
            P("batch"),
        ),
        check_vma=False,
    )
```

time: 1280 us -> 685 us (0.54)
  waiting for transfers between devices: 922 us -> 331 us
  Pallas kernels: 0 us -> 160 us
  matrix products: 140 us -> 0 us
  starting transfers between devices: 0.83 us -> 84.4 us
  blocking collectives: 88.8 us -> 14.1 us
  local copies, waits for them, and re-layouts: 68.5 us -> 27.2 us
    all_gather x9 -> x2, waiting for transfers between devices: 435 us -> 0.01 us  [the longest x1 0.01 us: local(): shrink_part = lax.all_gather(shrink_rows_own, 'batch', axis=0, tiled=True)]
    reduce_scatter x5 -> x2, waiting for transfers between devices: 339 us -> 0.02 us  [the longest x1 0.02 us: local(): lax.psum_scatter(grad_expand.reshape(B, -1, units), 'batch', scatter_dime...]
    ppermute x0 -> x76, waiting for transfers between devices: none -> 331 us  [the longest x42 238 us: plane(): return lax.ppermute(value, 'seq', [(j, j ^ k) for j in range(self.seq)])]
    pallas_call x0 -> x13, Pallas kernels: none -> 160 us  [call(): pl.pallas_call(kernel, out_shape=[jax.ShapeDtypeStruct(shape, kind) for s...]
    unnamed x26 -> x4, waiting for transfers between devices: 149 us -> 0.07 us
    dot_general x22 -> x0, matrix products: 140 us -> none  [the longest x16 126 us: product(): return jnp.dot(left_side, right_side, preferred_element_type=jnp.float32)]
    ppermute x0 -> x76, starting transfers between devices: none -> 84.1 us  [the longest x42 55.4 us: plane(): return lax.ppermute(value, 'seq', [(j, j ^ k) for j in range(self.seq)])]
    psum x2 -> x0, blocking collectives: 55.4 us -> none  [the longest x1 39.3 us: local(): total_square = lax.psum(local_square, ('batch', 'seq'))]
  transfers between devices with their start and end apart: 20 -> 80, of which waited for: 19 -> 34; matrix products, arithmetic and copies ran while one was open for 13% -> 4% of each run, Pallas kernels for 0% -> 20%
where the time goes in v1:
time: 685 us; the launch traced here: 676 us
  waiting for transfers between devices  331 us (48%)
  Pallas kernels  160 us (23%)
  starting transfers between devices  84.4 us (12%)
  other arithmetic  33 us (5%)
  local copies, waits for them, and re-layouts  27.2 us (4%)
  between operations  25.5 us (4%)
  blocking collectives  14.1 us (2%)
    ppermute x42, waiting for transfers between devices, plane(): return lax.ppermute(value, 'seq', [(j, j ^ k) for j in range(self.seq)])  238 us
    pallas_call x13, Pallas kernels, call(): pl.pallas_call(kernel, out_shape=[jax.ShapeDtypeStruct(shape, kind) for s...  160 us
    ppermute x16, waiting for transfers between devices, line(): lax.ppermute(value, 'batch', [(b, b ^ 2 * k) for b in range(self.batch)])  87.7 us
    ppermute x42, starting transfers between devices, plane(): return lax.ppermute(value, 'seq', [(j, j ^ k) for j in range(self.seq)])  55.4 us
    ppermute x16, starting transfers between devices, line(): lax.ppermute(value, 'batch', [(b, b ^ 2 * k) for b in range(self.batch)])  24.4 us
    unnamed x151, local copies, waits for them, and re-layouts  14.7 us
    all_gather x1, blocking collectives, local(): table = wide(lax.all_gather(low(vectors), 'batch', axis=1, tiled=True))  14.1 us
  transfers between devices with their start and end apart: 80, of which 34 were waited for; matrix products, arithmetic and copies ran while one was open for 4% of the time, Pallas kernels for 20%

profile of v1, /device:TPU:0, one launch (start us, length us, event | category | flops | bytes accessed | tf_op | source)
XLA Modules:
  0.0 675.8 jit_solution(11838600216240243041)
XLA Ops:
  8.7 4.0 collective-permute-start.23
  13.3 2.8 collective-permute-done.23
  21.1 2.6 collective-permute-start.1
  29.1 2.9 collective-permute-done.26
  34.5 2.5 collective-permute-start.2
  37.0 24.8 %collective-permute-done.10 = bf16[144,1152]{1,0:T(8,128)(2,1)} collective-permute-done((bf16[144,1152]{1,0:T(8,128)(2,1)S(1)}, bf16[144,1152]{1,0:T(8,128)(2,1)}, u32[]{:S(2)}, u32[]{:S(2)}) %collective-permute-start.10) | collective-permute-done | bytes 331808 | tf_op jit(solution)/shard_map/ppermute | solution.py:51
  62.9 23.2 %collective-permute-done.2 = bf16[288,288]{1,0:T(8,128)(2,1)S(1)} collective-permute-done((bf16[288,288]{1,0:T(8,128)(2,1)S(1)}, bf16[288,288]{1,0:T(8,128)(2,1)S(1)}, u32[]{:S(2)}, u32[]{:S(2)}) %collective-permute-start.2) | collective-permute-done | bytes 165920 | tf_op jit(solution)/shard_map/ppermute | solution.py:51
  90.0 2.8 collective-permute-done.12
  92.9 2.5 pad_maximum_fusion.refs_0_.refs_4_
  97.2 11.7 %collective-permute-done.3.refs_1_ = bf16[4,288,288]{2,1,0:T(8,128)(2,1)S(1)} collective-permute-done((bf16[4,288,288]{2,1,0:T(8,128)(2,1)S(1)}, bf16[4,288,288]{2,1,0:T(8,128)(2,1)S(1)}, u32[]{:S(2)}, u32[]{:S(2)}) %collective-permute-start.3) | collective-permute-done | bytes 663584 | tf_op jit(solution)/shard_map/ppermute | solution.py:48
  110.6 19.0 %collective-permute-done.4.refs_2_ = bf16[4,288,288]{2,1,0:T(8,128)(2,1)S(1)} collective-permute-done((bf16[4,288,288]{2,1,0:T(8,128)(2,1)S(1)}, bf16[4,288,288]{2,1,0:T(8,128)(2,1)S(1)}, u32[]{:S(2)}, u32[]{:S(2)}) %collective-permute-start.4) | collective-permute-done | bytes 663584 | tf_op jit(solution)/shard_map/ppermute | solution.py:48
  133.4 23.1 %collective-permute-done.13.refs_1_.refs_5_ = bf16[4,144,1152]{2,1,0:T(8,128)(2,1)} collective-permute-done((bf16[4,144,1152]{2,1,0:T(8,128)(2,1)}, bf16[4,144,1152]{2,1,0:T(8,128)(2,1)}, u32[]{:S(2)}, u32[]{:S(2)}) %collective-permute-start.13) | collective-permute-done | bytes 1327136 | tf_op jit(solution)/shard_map/ppermute | solution.py:48
  156.5 28.6 %collective-permute-done.14.refs_2_.refs_6_ = bf16[4,144,1152]{2,1,0:T(8,128)(2,1)} collective-permute-done((bf16[4,144,1152]{2,1,0:T(8,128)(2,1)}, bf16[4,144,1152]{2,1,0:T(8,128)(2,1)}, u32[]{:S(2)}, u32[]{:S(2)}) %collective-permute-start.14) | collective-permute-done | bytes 1327136 | tf_op jit(solution)/shard_map/ppermute | solution.py:48
  186.6 14.1 %all-gather = bf16[8,144,11]{1,2,0:T(8,128)(2,1)S(1)} all-gather(bf16[1,144,11]{1,2,0:T(8,128)(2,1)S(1)} %convert_bitcast_fusion), channel_id=1, replica_groups=mesh['batch'=8,'seq'=4] {'batch'}, dimensions={0}, use_global_device_ids=true | all-gather | bytes 28512 | tf_op jit(solution)/shard_map/all_gather | solution.py:432
  205.2 9.6 %shard_map.491 = (f32[336,1152]{1,0:T(8,128)}, bf16[336,1152]{1,0:T(8,128)(2,1)S(1)}) custom-call(s32[3]{0:T(128)S(1)} %pad_add_fusion.where_ref, bf16[336,1152]{1,0:T(8,128)(2,1)S(1)} %bitcast.124, bf16[336,1152]{1,0:T(8,128)(2,1)} %bitcast.126, f32[11,1152]{1,0:T(8,128)S(1)} %bitcast.118, bf16[4,288,288]{2,1,0:T(8,128)(2,1)} %copy-done, ...), custom_call_target="tpu_custom_call" | custom-call | flops 1783627776 | bytes 5945425 | tf_op jit(solution)/shard_map/pallas_call | solution.py:379
  215.7 21.3 %shard_map.492 = (bf16[4,336,864]{2,1,0:T(8,128)(2,1)}, bf16[336,1152]{1,0:T(8,128)(2,1)S(1)}, f32[336,16]{1,0:T(8,128)S(1)}, f32[336,1152]{1,0:T(8,128)}, bf16[336,1152]{1,0:T(8,128)(2,1)S(1)}) custom-call(s32[3]{0:T(128)S(1)} %pad_add_fusion.where_ref, s32[1]{0:T(128)S(6)} %copy.156.length_ref, bf16[336,1152]{1,0:T(8,128)(2,1)} %copy-done.10, ...), custom_call_target="tpu_custom_call" | custom-call | flops 5350883328 | bytes 17836276 | tf_op jit(solution)/shard_map/pallas_call | solution.py:379
  241.7 8.3 %shard_map.493 = (f32[336,1152]{1,0:T(8,128)}, f32[336,1152]{1,0:T(8,128)}, f32[336,1152]{1,0:T(8,128)}, f32[336,1152]{1,0:T(8,128)}) custom-call(bf16[336,1152]{1,0:T(8,128)(2,1)S(1)} %bitcast.132, bf16[336,1152]{1,0:T(8,128)(2,1)} %collective-permute-done.20.refs_1_.refs_13_, bf16[336,1152]{1,0:T(8,128)(2,1)} %collective-permute-done.21.refs_2_.refs_14_, ...), custom_call_target="tpu_custom_call" | custom-call | flops 3567255552 | bytes 11890851 | tf_op jit(solution)/shard_map/pallas_call | solution.py:379
  250.0 9.0 %shard_map.494 = (bf16[336,1152]{1,0:T(8,128)(2,1)S(1)}, bf16[336,1152]{1,0:T(8,128)(2,1)S(1)}, bf16[336,1152]{1,0:T(8,128)(2,1)}, bf16[336,1152]{1,0:T(8,128)(2,1)}, f32[1,1152]{1,0:T(1,128)S(1)}) custom-call(bf16[336,1152]{1,0:T(8,128)(2,1)} %copy-done.12, f32[336,1152]{1,0:T(8,128)} %get-tuple-element.90.gradient_ref, ...), custom_call_target="tpu_custom_call" | custom-call | flops 3567255552 | bytes 11890851 | tf_op jit(solution)/shard_map/pallas_call | solution.py:379
  261.6 9.4 %shard_map.495 = (bf16[336,1152]{1,0:T(8,128)(2,1)S(1)}, bf16[336,1152]{1,0:T(8,128)(2,1)S(1)}, bf16[336,1152]{1,0:T(8,128)(2,1)}, bf16[336,1152]{1,0:T(8,128)(2,1)}, f32[1,1152]{1,0:T(1,128)S(1)}) custom-call(bf16[336,1152]{1,0:T(8,128)(2,1)} %copy-done.14, f32[336,1152]{1,0:T(8,128)} %get-tuple-element.92.gradient_ref, ...), custom_call_target="tpu_custom_call" | custom-call | flops 3567255552 | bytes 11890851 | tf_op jit(solution)/shard_map/pallas_call | solution.py:379
  273.7 9.0 %shard_map.496 = (bf16[336,1152]{1,0:T(8,128)(2,1)S(1)}, bf16[336,1152]{1,0:T(8,128)(2,1)S(1)}, bf16[336,1152]{1,0:T(8,128)(2,1)}, bf16[336,1152]{1,0:T(8,128)(2,1)}, f32[1,1152]{1,0:T(1,128)S(1)}) custom-call(bf16[336,1152]{1,0:T(8,128)(2,1)} %collective-permute-done.31.norm_ref.refs_2_, f32[336,1152]{1,0:T(8,128)} %get-tuple-element.94.gradient_ref, ...), custom_call_target="tpu_custom_call" | custom-call | flops 3567255552 | bytes 11890851 | tf_op jit(solution)/shard_map/pallas_call | solution.py:379
  283.6 9.3 %shard_map.497 = (bf16[336,1152]{1,0:T(8,128)(2,1)S(1)}, bf16[336,1152]{1,0:T(8,128)(2,1)S(1)}, bf16[336,1152]{1,0:T(8,128)(2,1)}, bf16[336,1152]{1,0:T(8,128)(2,1)}, f32[1,1152]{1,0:T(1,128)S(1)}) custom-call(bf16[336,1152]{1,0:T(8,128)(2,1)} %collective-permute-done.33.norm_ref.refs_3_, f32[336,1152]{1,0:T(8,128)} %get-tuple-element.96.gradient_ref, ...), custom_call_target="tpu_custom_call" | custom-call | flops 3567255552 | bytes 11890851 | tf_op jit(solution)/shard_map/pallas_call | solution.py:379
  294.7 17.7 %shard_map.502 = (bf16[1152,1152]{1,0:T(8,128)(2,1)}, bf16[1152,1152]{1,0:T(8,128)(2,1)}) custom-call(bf16[336,1152]{1,0:T(8,128)(2,1)S(1)} %copy-done.13, bf16[336,1152]{1,0:T(8,128)(2,1)S(1)} %copy-done.15, bf16[336,1152]{1,0:T(8,128)(2,1)} %collective-permute-done.31.norm_ref.refs_2_, bf16[336,1152]{1,0:T(8,128)(2,1)} %collective-permute-done.33.norm_ref.refs_3_, ...), custom_call_target="tpu_custom_call" | custom-call | flops 7134511104 | bytes 23781704 | tf_op jit(solution)/shard_map/pallas_call | solution.py:379
  316.2 17.0 %collective-permute-done.35.refs_1_ = bf16[336,1152]{1,0:T(8,128)(2,1)} collective-permute-done((bf16[336,1152]{1,0:T(8,128)(2,1)}, bf16[336,1152]{1,0:T(8,128)(2,1)}, u32[]{:S(2)}, u32[]{:S(2)}) %collective-permute-start.35) | collective-permute-done | bytes 774176 | tf_op jit(solution)/shard_map/ppermute | solution.py:48
  333.3 12.9 %collective-permute-done.36.refs_2_ = bf16[336,1152]{1,0:T(8,128)(2,1)} collective-permute-done((bf16[336,1152]{1,0:T(8,128)(2,1)}, bf16[336,1152]{1,0:T(8,128)(2,1)}, u32[]{:S(2)}, u32[]{:S(2)}) %collective-permute-start.36) | collective-permute-done | bytes 774176 | tf_op jit(solution)/shard_map/ppermute | solution.py:48
  346.2 25.2 %shard_map.498 = (bf16[4,336,288]{2,1,0:T(8,128)(2,1)}, f32[336,1152]{1,0:T(8,128)}, bf16[4,336,864]{2,1,0:T(8,128)(2,1)}, f32[8,1152]{1,0:T(8,128)S(1)}) custom-call(s32[3]{0:T(128)S(1)} %pad_add_fusion.where_ref, s32[1]{0:T(128)S(6)} %copy.156.length_ref, bf16[336,1152]{1,0:T(8,128)(2,1)S(1)} %bitcast.133, f32[336,1152]{1,0:T(8,128)} %get-tuple-element.88.residual_ref, ...), custom_call_target="tpu_custom_call" | custom-call | flops 3567255552 | bytes 11890851 | tf_op jit(solution)/shard_map/pallas_call | solution.py:379
  371.4 11.5 %shard_map.499 = (bf16[4,336,288]{2,1,0:T(8,128)(2,1)S(1)}, f32[8,1152]{1,0:T(8,128)S(1)}) custom-call(s32[3]{0:T(128)S(1)} %pad_add_fusion.where_ref, bf16[4,336,864]{2,1,0:T(8,128)(2,1)} %get-tuple-element.104.grad_packed_ref, f32[336,1152]{1,0:T(8,128)} %get-tuple-element.87.merged_ref, f32[11,1152]{1,0:T(8,128)S(1)} %bitcast.123, ...), custom_call_target="tpu_custom_call" | custom-call | flops 2675441664 | bytes 8918138 | tf_op jit(solution)/shard_map/pallas_call | solution.py:379
  383.8 7.4 %shard_map.503 = (bf16[4,288,288]{2,1,0:T(8,128)(2,1)}, bf16[4,288,288]{2,1,0:T(8,128)(2,1)}, bf16[4,288,288]{2,1,0:T(8,128)(2,1)}, bf16[4,288,288]{2,1,0:T(8,12...) custom-call(s32[3]{0:T(128)S(1)} %pad_add_fusion.where_ref, ...), custom_call_target="tpu_custom_call" | custom-call | flops 1783627776 | bytes 5945425 | tf_op jit(solution)/shard_map/pallas_call | solution.py:379
  391.3 11.1 %shard_map.501 = (bf16[4,144,1152]{2,1,0:T(8,128)(2,1)}, bf16[4,144,1152]{2,1,0:T(8,128)(2,1)}, bf16[4,144,1152]{2,1,0:T(8,128)(2,1)}, bf16[4,144,1152]{2,1,0:T(...) custom-call(s32[3]{0:T(128)S(1)} %pad_add_fusion.where_ref, ...), custom_call_target="tpu_custom_call" | custom-call | flops 3567255552 | bytes 11890851 | tf_op jit(solution)/shard_map/pallas_call | solution.py:379
  414.3 9.7 %collective-permute-done.30 = bf16[336,1152]{1,0:T(8,128)(2,1)} collective-permute-done((bf16[336,1152]{1,0:T(8,128)(2,1)}, bf16[336,1152]{1,0:T(8,128)(2,1)}, u32[]{:S(2)}, u32[]{:S(2)}) %collective-permute-start.30) | collective-permute-done | bytes 774176 | tf_op jit(solution)/shard_map/ppermute | solution.py:48
  424.0 20.0 %collective-permute-done.32 = bf16[336,1152]{1,0:T(8,128)(2,1)S(1)} collective-permute-done((bf16[336,1152]{1,0:T(8,128)(2,1)S(1)}, bf16[336,1152]{1,0:T(8,128)(2,1)S(1)}, u32[]{:S(2)}, u32[]{:S(2)}) %collective-permute-start.32) | collective-permute-done | bytes 774176 | tf_op jit(solution)/shard_map/ppermute | solution.py:48
  448.3 2.3 collective-permute-done.38
  453.1 13.5 %collective-permute-done.59 = bf16[4,288,288]{2,1,0:T(8,128)(2,1)S(1)} collective-permute-done((bf16[4,288,288]{2,1,0:T(8,128)(2,1)S(1)}, bf16[4,288,288]{2,1,0:T(8,128)(2,1)S(1)}, u32[]{:S(2)}, u32[]{:S(2)}) %collective-permute-start.59) | collective-permute-done | bytes 663584 | tf_op jit(solution)/shard_map/ppermute | solution.py:48
  467.7 17.6 %collective-permute-done.61 = bf16[4,288,288]{2,1,0:T(8,128)(2,1)S(1)} collective-permute-done((bf16[4,288,288]{2,1,0:T(8,128)(2,1)S(1)}, bf16[4,288,288]{2,1,0:T(8,128)(2,1)S(1)}, u32[]{:S(2)}, u32[]{:S(2)}) %collective-permute-start.61) | collective-permute-done | bytes 663584 | tf_op jit(solution)/shard_map/ppermute | solution.py:48
  486.8 2.9 add_bitcast_fusion
  492.6 21.4 %collective-permute-done.47 = bf16[4,144,1152]{2,1,0:T(8,128)(2,1)S(1)} collective-permute-done((bf16[4,144,1152]{2,1,0:T(8,128)(2,1)S(1)}, bf16[4,144,1152]{2,1,0:T(8,128)(2,1)S(1)}, u32[]{:S(2)}, u32[]{:S(2)}) %collective-permute-start.47) | collective-permute-done | bytes 1327136 | tf_op jit(solution)/shard_map/ppermute | solution.py:48
  515.5 27.8 %collective-permute-done.49 = bf16[4,144,1152]{2,1,0:T(8,128)(2,1)S(1)} collective-permute-done((bf16[4,144,1152]{2,1,0:T(8,128)(2,1)S(1)}, bf16[4,144,1152]{2,1,0:T(8,128)(2,1)S(1)}, u32[]{:S(2)}, u32[]{:S(2)}) %collective-permute-start.49) | collective-permute-done | bytes 1327136 | tf_op jit(solution)/shard_map/ppermute | solution.py:48
  544.2 2.5 collective-permute-start.52
  546.8 2.2 collective-permute-start.43
  551.2 23.9 %collective-permute-done.64 = bf16[2,288,288]{2,1,0:T(8,128)(2,1)S(1)} collective-permute-done((bf16[2,288,288]{2,1,0:T(8,128)(2,1)S(1)}, bf16[2,288,288]{2,1,0:T(8,128)(2,1)S(1)}, u32[]{:S(2)}, u32[]{:S(2)}) %collective-permute-start.64) | collective-permute-done | bytes 331808 | tf_op jit(solution)/shard_map/ppermute | solution.py:51
  575.5 10.7 %collective-permute-done.52 = bf16[2,144,1152]{2,1,0:T(8,128)(2,1)S(1)} collective-permute-done((bf16[2,144,1152]{2,1,0:T(8,128)(2,1)S(1)}, bf16[2,144,1152]{2,1,0:T(8,128)(2,1)S(1)}, u32[]{:S(2)}, u32[]{:S(2)}) %collective-permute-start.52) | collective-permute-done | bytes 663584 | tf_op jit(solution)/shard_map/ppermute | solution.py:51
  586.7 11.6 %shard_map.500 = (f32[336,1152]{1,0:T(8,128)}, f32[336,1152]{1,0:T(8,128)}) custom-call(s32[3]{0:T(128)S(1)} %pad_add_fusion.where_ref, bf16[4,336,288]{2,1,0:T(8,128)(2,1)} %copy-done.4, bf16[4,288,288]{2,1,0:T(8,128)(2,1)S(1)} %copy-done.1, bf16[4,288,288]{2,1,0:T(8,128)(2,1)S(1)} %copy-done.3, bf16[4,288,288]{2,1,0:T(8,128)(2,1)} %copy-done.29, ...), custom_call_target="tpu_custom_call" | custom-call | flops 1783627776 | bytes 5945425 | tf_op jit(solution)/shard_map/pallas_call | solution.py:379
  619.2 2.8 fusion
  626.7 2.9 collective-permute-start.71
  629.6 2.8 collective-permute-start.72
  637.8 4.0 collective-permute-start.74
  641.8 3.0 collective-permute-start.75
  646.1 2.2 collective-permute-done.73
  656.2 2.4 multiply_add_fusion.9
  (364 shorter events, 120.7 us)
Async XLA Ops:
  7.2 234.5 %all-gather.4.cloned.1.call-start = ((), (), s32[]{:S(2)}) async-start(), calls=%async_computation.2 | async-start | bytes 2985984 | tf_op jit(solution)/shard_map/all_gather | solution.py:446
  19.4 230.6 %all-gather.6.cloned.1.call-start = ((), (), s32[]{:S(2)}) async-start(), calls=%async_computation.3 | async-start | bytes 2985984 | tf_op jit(solution)/shard_map/all_gather | solution.py:445
  21.1 41.7 %collective-permute-start.1 = (bf16[288,288]{1,0:T(8,128)(2,1)S(1)}, bf16[288,288]{1,0:T(8,128)(2,1)S(1)}, u32[]{:S(2)}, u32[]{:S(2)}) collective-permute-start(bf16[288,288]{1,0:T(8,128)(2,1)S(1)} %convert_element_type.185), channel_id=1, source_target_pairs={{0,16},{4,20},{8,24},{12,28},{16,0},{20,4},{24,8},{28,12},{1,17},{... | collective-permute-start | bytes 497672 | tf_op jit(solution)/shard_map/ppermute | solution.py:51
  32.0 29.8 %collective-permute-start.10 = (bf16[144,1152]{1,0:T(8,128)(2,1)S(1)}, bf16[144,1152]{1,0:T(8,128)(2,1)}, u32[]{:S(2)}, u32[]{:S(2)}) collective-permute-start(bf16[144,1152]{1,0:T(8,128)(2,1)S(1)} %pad_maximum_fusion.4), channel_id=1, source_target_pairs={{0,8},{4,12},{8,0},{12,4},{16,24},{20,28},{24,16},{28,20},{1,9},{5... | collective-permute-start | bytes 995336 | tf_op jit(solution)/shard_map/ppermute | solution.py:51
  32.9 57.2 %collective-permute-start.11 = (bf16[144,1152]{1,0:T(8,128)(2,1)S(1)}, bf16[144,1152]{1,0:T(8,128)(2,1)}, u32[]{:S(2)}, u32[]{:S(2)}) collective-permute-start(bf16[144,1152]{1,0:T(8,128)(2,1)S(1)} %pad_maximum_fusion.4), channel_id=1, source_target_pairs={{0,16},{4,20},{8,24},{12,28},{16,0},{20,4},{24,8},{28,12},{1,17},{... | collective-permute-start | bytes 995336 | tf_op jit(solution)/shard_map/ppermute | solution.py:51
  34.4 568.8 %reduce-scatter.3.cloned.1.call-start = ((), (), s32[]{:S(2)}) async-start(), calls=%async_computation.4 | async-start | bytes 2985984 | tf_op jit(solution)/shard_map/reduce_scatter | solution.py:526
  34.5 51.6 %collective-permute-start.2 = (bf16[288,288]{1,0:T(8,128)(2,1)S(1)}, bf16[288,288]{1,0:T(8,128)(2,1)S(1)}, u32[]{:S(2)}, u32[]{:S(2)}) collective-permute-start(bf16[288,288]{1,0:T(8,128)(2,1)S(1)} %collective-permute-done), channel_id=1, source_target_pairs={{0,16},{4,20},{8,24},{12,28},{16,0},{20,4},{24,8},{28,12},{1,17},{... | collective-permute-start | bytes 497672 | tf_op jit(solution)/shard_map/ppermute | solution.py:51
  61.8 31.0 %collective-permute-start.12 = (bf16[144,1152]{1,0:T(8,128)(2,1)}, bf16[144,1152]{1,0:T(8,128)(2,1)S(1)}, u32[]{:S(2)}, u32[]{:S(2)}) collective-permute-start(bf16[144,1152]{1,0:T(8,128)(2,1)} %collective-permute-done.10), channel_id=1, source_target_pairs={{0,16},{4,20},{8,24},{12,28},{16,0},{20,4},{24,8},{28,12},{1,17},{... | collective-permute-start | bytes 995336 | tf_op jit(solution)/shard_map/ppermute | solution.py:51
  86.3 22.6 %collective-permute-start.3 = (bf16[4,288,288]{2,1,0:T(8,128)(2,1)S(1)}, bf16[4,288,288]{2,1,0:T(8,128)(2,1)S(1)}, u32[]{:S(2)}, u32[]{:S(2)}) collective-permute-start(bf16[4,288,288]{2,1,0:T(8,128)(2,1)S(1)} %pad_maximum_fusion.1.refs_0_), channel_id=1, source_target_pairs={{0,1},{1,0},{2,3},{3,2},{4,5},{5,4},{6,7},{7,6},{8,9},{9,8},{10,11... | collective-permute-start | bytes 1990664 | tf_op jit(solution)/shard_map/ppermute | solution.py:48
  88.0 41.6 %collective-permute-start.4 = (bf16[4,288,288]{2,1,0:T(8,128)(2,1)S(1)}, bf16[4,288,288]{2,1,0:T(8,128)(2,1)S(1)}, u32[]{:S(2)}, u32[]{:S(2)}) collective-permute-start(bf16[4,288,288]{2,1,0:T(8,128)(2,1)S(1)} %pad_maximum_fusion.1.refs_0_), channel_id=1, source_target_pairs={{0,2},{1,3},{2,0},{3,1},{4,6},{5,7},{6,4},{7,5},{8,10},{9,11},{10,... | collective-permute-start | bytes 1990664 | tf_op jit(solution)/shard_map/ppermute | solution.py:48
  88.7 40.9 %collective-permute-start.5 = (bf16[4,288,288]{2,1,0:T(8,128)(2,1)S(1)}, bf16[4,288,288]{2,1,0:T(8,128)(2,1)}, u32[]{:S(2)}, u32[]{:S(2)}) collective-permute-start(bf16[4,288,288]{2,1,0:T(8,128)(2,1)S(1)} %pad_maximum_fusion.1.refs_0_), channel_id=1, source_target_pairs={{0,3},{1,2},{2,1},{3,0},{4,7},{5,6},{6,5},{7,4},{8,11},{9,10},{10,... | collective-permute-start | bytes 1990664 | tf_op jit(solution)/shard_map/ppermute | solution.py:48
  95.4 61.1 %collective-permute-start.13 = (bf16[4,144,1152]{2,1,0:T(8,128)(2,1)}, bf16[4,144,1152]{2,1,0:T(8,128)(2,1)}, u32[]{:S(2)}, u32[]{:S(2)}) collective-permute-start(bf16[4,144,1152]{2,1,0:T(8,128)(2,1)} %pad_maximum_fusion.refs_0_.refs_4_), channel_id=1, source_target_pairs={{0,1},{1,0},{2,3},{3,2},{4,5},{5,4},{6,7},{7,6},{8,9},{9,8},{10,11... | collective-permute-start | bytes 3981320 | tf_op jit(solution)/shard_map/ppermute | solution.py:48
  97.1 88.0 %collective-permute-start.14 = (bf16[4,144,1152]{2,1,0:T(8,128)(2,1)}, bf16[4,144,1152]{2,1,0:T(8,128)(2,1)}, u32[]{:S(2)}, u32[]{:S(2)}) collective-permute-start(bf16[4,144,1152]{2,1,0:T(8,128)(2,1)} %pad_maximum_fusion.refs_0_.refs_4_), channel_id=1, source_target_pairs={{0,2},{1,3},{2,0},{3,1},{4,6},{5,7},{6,4},{7,5},{8,10},{9,11},{10,... | collective-permute-start | bytes 3981320 | tf_op jit(solution)/shard_map/ppermute | solution.py:48
  109.0 76.1 %collective-permute-start.15 = (bf16[4,144,1152]{2,1,0:T(8,128)(2,1)}, bf16[4,144,1152]{2,1,0:T(8,128)(2,1)}, u32[]{:S(2)}, u32[]{:S(2)}) collective-permute-start(bf16[4,144,1152]{2,1,0:T(8,128)(2,1)} %pad_maximum_fusion.refs_0_.refs_4_), channel_id=1, source_target_pairs={{0,3},{1,2},{2,1},{3,0},{4,7},{5,6},{6,5},{7,4},{8,11},{9,10},{10,... | collective-permute-start | bytes 3981320 | tf_op jit(solution)/shard_map/ppermute | solution.py:48
  132.0 53.6 %collective-permute-start.8 = (bf16[4,288,288]{2,1,0:T(8,128)(2,1)S(1)}, bf16[4,288,288]{2,1,0:T(8,128)(2,1)S(1)}, u32[]{:S(2)}, u32[]{:S(2)}) collective-permute-start(bf16[4,288,288]{2,1,0:T(8,128)(2,1)S(1)} %collective-permute-done.4.refs_2_), channel_id=1, source_target_pairs={{0,4},{4,0},{8,12},{12,8},{16,20},{20,16},{24,28},{28,24},{1,5},{5... | collective-permute-start | bytes 1990664 | tf_op jit(solution)/shard_map/ppermute | solution.py:54
  133.3 68.7 %collective-permute-start.16 = (bf16[4,144,1152]{2,1,0:T(8,128)(2,1)}, bf16[4,144,1152]{2,1,0:T(8,128)(2,1)}, u32[]{:S(2)}, u32[]{:S(2)}) collective-permute-start(bf16[4,144,1152]{2,1,0:T(8,128)(2,1)} %pad_maximum_fusion.refs_0_.refs_4_), channel_id=1, source_target_pairs={{0,4},{4,0},{8,12},{12,8},{16,20},{20,16},{24,28},{28,24},{1,5},{5... | collective-permute-start | bytes 3981320 | tf_op jit(solution)/shard_map/ppermute | solution.py:54
  156.5 47.2 %collective-permute-start.17 = (bf16[4,144,1152]{2,1,0:T(8,128)(2,1)}, bf16[4,144,1152]{2,1,0:T(8,128)(2,1)}, u32[]{:S(2)}, u32[]{:S(2)}) collective-permute-start(bf16[4,144,1152]{2,1,0:T(8,128)(2,1)} %collective-permute-done.13.refs_1_.refs_5_), channel_id=1, source_target_pairs={{0,4},{4,0},{8,12},{12,8},{16,20},{20,16},{24,28},{28,24},{1,5},{5... | collective-permute-start | bytes 3981320 | tf_op jit(solution)/shard_map/ppermute | solution.py:54
  185.1 30.6 %collective-permute-start.18 = (bf16[4,144,1152]{2,1,0:T(8,128)(2,1)}, bf16[4,144,1152]{2,1,0:T(8,128)(2,1)}, u32[]{:S(2)}, u32[]{:S(2)}) collective-permute-start(bf16[4,144,1152]{2,1,0:T(8,128)(2,1)} %collective-permute-done.14.refs_2_.refs_6_), channel_id=1, source_target_pairs={{0,4},{4,0},{8,12},{12,8},{16,20},{20,16},{24,28},{28,24},{1,5},{5... | collective-permute-start | bytes 3981320 | tf_op jit(solution)/shard_map/ppermute | solution.py:54
  185.1 30.6 %collective-permute-start.19 = (bf16[4,144,1152]{2,1,0:T(8,128)(2,1)}, bf16[4,144,1152]{2,1,0:T(8,128)(2,1)}, u32[]{:S(2)}, u32[]{:S(2)}) collective-permute-start(bf16[4,144,1152]{2,1,0:T(8,128)(2,1)} %collective-permute-done.15.refs_3_.refs_7_), channel_id=1, source_target_pairs={{0,4},{4,0},{8,12},{12,8},{16,20},{20,16},{24,28},{28,24},{1,5},{5... | collective-permute-start | bytes 3981320 | tf_op jit(solution)/shard_map/ppermute | solution.py:54
  201.7 38.6 %collective-permute-start.20 = (bf16[336,1152]{1,0:T(8,128)(2,1)S(1)}, bf16[336,1152]{1,0:T(8,128)(2,1)}, u32[]{:S(2)}, u32[]{:S(2)}) collective-permute-start(bf16[336,1152]{1,0:T(8,128)(2,1)S(1)} %bitcast.129), channel_id=1, source_target_pairs={{0,1},{1,0},{2,3},{3,2},{4,5},{5,4},{6,7},{7,6},{8,9},{9,8},{10,11... | collective-permute-start | bytes 2322440 | tf_op jit(solution)/shard_map/ppermute | solution.py:48
  202.0 39.7 %collective-permute-start.21 = (bf16[336,1152]{1,0:T(8,128)(2,1)S(1)}, bf16[336,1152]{1,0:T(8,128)(2,1)}, u32[]{:S(2)}, u32[]{:S(2)}) collective-permute-start(bf16[336,1152]{1,0:T(8,128)(2,1)S(1)} %bitcast.130), channel_id=1, source_target_pairs={{0,2},{1,3},{2,0},{3,1},{4,6},{5,7},{6,4},{7,5},{8,10},{9,11},{10,... | collective-permute-start | bytes 2322440 | tf_op jit(solution)/shard_map/ppermute | solution.py:48
  203.7 38.0 %collective-permute-start.22 = (bf16[336,1152]{1,0:T(8,128)(2,1)S(1)}, bf16[336,1152]{1,0:T(8,128)(2,1)}, u32[]{:S(2)}, u32[]{:S(2)}) collective-permute-start(bf16[336,1152]{1,0:T(8,128)(2,1)S(1)} %bitcast.131), channel_id=1, source_target_pairs={{0,3},{1,2},{2,1},{3,0},{4,7},{5,6},{6,5},{7,4},{8,11},{9,10},{10,... | collective-permute-start | bytes 2322440 | tf_op jit(solution)/shard_map/ppermute | solution.py:48
  237.9 22.8 %collective-permute-start.29 = (bf16[336,1152]{1,0:T(8,128)(2,1)S(1)}, bf16[336,1152]{1,0:T(8,128)(2,1)S(1)}, u32[]{:S(2)}, u32[]{:S(2)}) collective-permute-start(bf16[336,1152]{1,0:T(8,128)(2,1)S(1)} %get-tuple-element.89.norm_ref.refs_0_), channel_id=1, source_target_pairs={{0,1},{1,0},{2,3},{3,2},{4,5},{5,4},{6,7},{7,6},{8,9},{9,8},{10,11... | collective-permute-start | bytes 2322440 | tf_op jit(solution)/shard_map/ppermute | solution.py:48
  238.5 35.2 %collective-permute-start.31 = (bf16[336,1152]{1,0:T(8,128)(2,1)S(1)}, bf16[336,1152]{1,0:T(8,128)(2,1)}, u32[]{:S(2)}, u32[]{:S(2)}) collective-permute-start(bf16[336,1152]{1,0:T(8,128)(2,1)S(1)} %get-tuple-element.89.norm_ref.refs_0_), channel_id=1, source_target_pairs={{0,2},{1,3},{2,0},{3,1},{4,6},{5,7},{6,4},{7,5},{8,10},{9,11},{10,... | collective-permute-start | bytes 2322440 | tf_op jit(solution)/shard_map/ppermute | solution.py:48
  240.3 43.3 %collective-permute-start.33 = (bf16[336,1152]{1,0:T(8,128)(2,1)S(1)}, bf16[336,1152]{1,0:T(8,128)(2,1)}, u32[]{:S(2)}, u32[]{:S(2)}) collective-permute-start(bf16[336,1152]{1,0:T(8,128)(2,1)S(1)} %get-tuple-element.89.norm_ref.refs_0_), channel_id=1, source_target_pairs={{0,3},{1,2},{2,1},{3,0},{4,7},{5,6},{6,5},{7,4},{8,11},{9,10},{10,... | collective-permute-start | bytes 2322440 | tf_op jit(solution)/shard_map/ppermute | solution.py:48
  312.4 296.9 %reduce-scatter.5.cloned.1.call-start = ((), (), s32[]{:S(2)}) async-start(), calls=%async_computation.5 | async-start | bytes 2985984 | tf_op jit(solution)/shard_map/reduce_scatter | solution.py:527
  314.4 31.7 %collective-permute-start.36 = (bf16[336,1152]{1,0:T(8,128)(2,1)}, bf16[336,1152]{1,0:T(8,128)(2,1)}, u32[]{:S(2)}, u32[]{:S(2)}) collective-permute-start(bf16[336,1152]{1,0:T(8,128)(2,1)} %get-tuple-element.102), channel_id=1, source_target_pairs={{0,2},{1,3},{2,0},{3,1},{4,6},{5,7},{6,4},{7,5},{8,10},{9,11},{10,... | collective-permute-start | bytes 2322440 | tf_op jit(solution)/shard_map/ppermute | solution.py:48
  314.8 31.4 %collective-permute-start.37 = (bf16[336,1152]{1,0:T(8,128)(2,1)}, bf16[336,1152]{1,0:T(8,128)(2,1)}, u32[]{:S(2)}, u32[]{:S(2)}) collective-permute-start(bf16[336,1152]{1,0:T(8,128)(2,1)} %get-tuple-element.103), channel_id=1, source_target_pairs={{0,3},{1,2},{2,1},{3,0},{4,7},{5,6},{6,5},{7,4},{8,11},{9,10},{10,... | collective-permute-start | bytes 2322440 | tf_op jit(solution)/shard_map/ppermute | solution.py:48
  406.1 39.0 %collective-permute-start.48 = (bf16[4,144,1152]{2,1,0:T(8,128)(2,1)}, bf16[4,144,1152]{2,1,0:T(8,128)(2,1)S(1)}, u32[]{:S(2)}, u32[]{:S(2)}) collective-permute-start(bf16[4,144,1152]{2,1,0:T(8,128)(2,1)} %get-tuple-element.122), channel_id=1, source_target_pairs={{0,4},{4,0},{8,12},{12,8},{16,20},{20,16},{24,28},{28,24},{1,5},{5... | collective-permute-start | bytes 3981320 | tf_op jit(solution)/shard_map/ppermute | solution.py:54
  408.1 35.9 %collective-permute-start.32 = (bf16[336,1152]{1,0:T(8,128)(2,1)S(1)}, bf16[336,1152]{1,0:T(8,128)(2,1)S(1)}, u32[]{:S(2)}, u32[]{:S(2)}) collective-permute-start(bf16[336,1152]{1,0:T(8,128)(2,1)S(1)} %copy-done.71), channel_id=1, source_target_pairs={{0,2},{1,3},{2,0},{3,1},{4,6},{5,7},{6,4},{7,5},{8,10},{9,11},{10,... | collective-permute-start | bytes 2322440 | tf_op jit(solution)/shard_map/ppermute | solution.py:48
  410.7 36.7 %collective-permute-start.50 = (bf16[4,144,1152]{2,1,0:T(8,128)(2,1)S(1)}, bf16[4,144,1152]{2,1,0:T(8,128)(2,1)S(1)}, u32[]{:S(2)}, u32[]{:S(2)}) collective-permute-start(bf16[4,144,1152]{2,1,0:T(8,128)(2,1)S(1)} %copy-done.68), channel_id=1, source_target_pairs={{0,4},{4,0},{8,12},{12,8},{16,20},{20,16},{24,28},{28,24},{1,5},{5... | collective-permute-start | bytes 3981320 | tf_op jit(solution)/shard_map/ppermute | solution.py:54
  412.5 33.9 %collective-permute-start.34 = (bf16[336,1152]{1,0:T(8,128)(2,1)S(1)}, bf16[336,1152]{1,0:T(8,128)(2,1)S(1)}, u32[]{:S(2)}, u32[]{:S(2)}) collective-permute-start(bf16[336,1152]{1,0:T(8,128)(2,1)S(1)} %copy-done.70), channel_id=1, source_target_pairs={{0,3},{1,2},{2,1},{3,0},{4,7},{5,6},{6,5},{7,4},{8,11},{9,10},{10,... | collective-permute-start | bytes 2322440 | tf_op jit(solution)/shard_map/ppermute | solution.py:48
  424.0 28.0 %collective-permute-start.57 = (bf16[4,288,288]{2,1,0:T(8,128)(2,1)S(1)}, bf16[4,288,288]{2,1,0:T(8,128)(2,1)S(1)}, u32[]{:S(2)}, u32[]{:S(2)}) collective-permute-start(bf16[4,288,288]{2,1,0:T(8,128)(2,1)S(1)} %copy-done.69), channel_id=1, source_target_pairs={{0,4},{4,0},{8,12},{12,8},{16,20},{20,16},{24,28},{28,24},{1,5},{5... | collective-permute-start | bytes 1990664 | tf_op jit(solution)/shard_map/ppermute | solution.py:54
  445.1 40.2 %collective-permute-start.61 = (bf16[4,288,288]{2,1,0:T(8,128)(2,1)S(1)}, bf16[4,288,288]{2,1,0:T(8,128)(2,1)S(1)}, u32[]{:S(2)}, u32[]{:S(2)}) collective-permute-start(bf16[4,288,288]{2,1,0:T(8,128)(2,1)S(1)} %add_convert_fusion.5), channel_id=1, source_target_pairs={{0,2},{1,3},{2,0},{3,1},{4,6},{5,7},{6,4},{7,5},{8,10},{9,11},{10,... | collective-permute-start | bytes 1990664 | tf_op jit(solution)/shard_map/ppermute | solution.py:48
  447.4 42.9 %collective-permute-start.45 = (bf16[4,144,1152]{2,1,0:T(8,128)(2,1)S(1)}, bf16[4,144,1152]{2,1,0:T(8,128)(2,1)S(1)}, u32[]{:S(2)}, u32[]{:S(2)}) collective-permute-start(bf16[4,144,1152]{2,1,0:T(8,128)(2,1)S(1)} %copy-done.67), channel_id=1, source_target_pairs={{0,4},{4,0},{8,12},{12,8},{16,20},{20,16},{24,28},{28,24},{1,5},{5... | collective-permute-start | bytes 3981320 | tf_op jit(solution)/shard_map/ppermute | solution.py:54
  450.6 39.4 %collective-permute-start.63 = (bf16[4,288,288]{2,1,0:T(8,128)(2,1)S(1)}, bf16[4,288,288]{2,1,0:T(8,128)(2,1)S(1)}, u32[]{:S(2)}, u32[]{:S(2)}) collective-permute-start(bf16[4,288,288]{2,1,0:T(8,128)(2,1)S(1)} %add_convert_fusion.4), channel_id=1, source_target_pairs={{0,3},{1,2},{2,1},{3,0},{4,7},{5,6},{6,5},{7,4},{8,11},{9,10},{10,... | collective-permute-start | bytes 1990664 | tf_op jit(solution)/shard_map/ppermute | solution.py:48
  452.0 62.0 %collective-permute-start.47 = (bf16[4,144,1152]{2,1,0:T(8,128)(2,1)S(1)}, bf16[4,144,1152]{2,1,0:T(8,128)(2,1)S(1)}, u32[]{:S(2)}, u32[]{:S(2)}) collective-permute-start(bf16[4,144,1152]{2,1,0:T(8,128)(2,1)S(1)} %add_convert_fusion.2), channel_id=1, source_target_pairs={{0,1},{1,0},{2,3},{3,2},{4,5},{5,4},{6,7},{7,6},{8,9},{9,8},{10,11... | collective-permute-start | bytes 3981320 | tf_op jit(solution)/shard_map/ppermute | solution.py:48
  466.6 76.7 %collective-permute-start.49 = (bf16[4,144,1152]{2,1,0:T(8,128)(2,1)S(1)}, bf16[4,144,1152]{2,1,0:T(8,128)(2,1)S(1)}, u32[]{:S(2)}, u32[]{:S(2)}) collective-permute-start(bf16[4,144,1152]{2,1,0:T(8,128)(2,1)S(1)} %add_convert_fusion.1), channel_id=1, source_target_pairs={{0,2},{1,3},{2,0},{3,1},{4,6},{5,7},{6,4},{7,5},{8,10},{9,11},{10,... | collective-permute-start | bytes 3981320 | tf_op jit(solution)/shard_map/ppermute | solution.py:48
  485.3 58.6 %collective-permute-start.51 = (bf16[4,144,1152]{2,1,0:T(8,128)(2,1)S(1)}, bf16[4,144,1152]{2,1,0:T(8,128)(2,1)S(1)}, u32[]{:S(2)}, u32[]{:S(2)}) collective-permute-start(bf16[4,144,1152]{2,1,0:T(8,128)(2,1)S(1)} %add_convert_fusion), channel_id=1, source_target_pairs={{0,3},{1,2},{2,1},{3,0},{4,7},{5,6},{6,5},{7,4},{8,11},{9,10},{10,... | collective-permute-start | bytes 3981320 | tf_op jit(solution)/shard_map/ppermute | solution.py:48
  490.0 56.7 %collective-permute-start.39 = (f32[11,1152]{1,0:T(8,128)S(1)}, f32[11,1152]{1,0:T(8,128)S(1)}, u32[]{:S(2)}, u32[]{:S(2)}) collective-permute-start(f32[11,1152]{1,0:T(8,128)S(1)} %add.323), channel_id=1, source_target_pairs={{0,1},{1,0},{2,3},{3,2},{4,5},{5,4},{6,7},{7,6},{8,9},{9,8},{10,11... | collective-permute-start | bytes 152072 | tf_op jit(solution)/shard_map/ppermute | solution.py:48
  490.3 56.4 %collective-permute-start.40 = (f32[11,1152]{1,0:T(8,128)S(1)}, f32[11,1152]{1,0:T(8,128)S(1)}, u32[]{:S(2)}, u32[]{:S(2)}) collective-permute-start(f32[11,1152]{1,0:T(8,128)S(1)} %add.323), channel_id=1, source_target_pairs={{0,2},{1,3},{2,0},{3,1},{4,6},{5,7},{6,4},{7,5},{8,10},{9,11},{10,... | collective-permute-start | bytes 152072 | tf_op jit(solution)/shard_map/ppermute | solution.py:48
  514.1 32.6 %collective-permute-start.41 = (f32[11,1152]{1,0:T(8,128)S(1)}, f32[11,1152]{1,0:T(8,128)S(1)}, u32[]{:S(2)}, u32[]{:S(2)}) collective-permute-start(f32[11,1152]{1,0:T(8,128)S(1)} %add.323), channel_id=1, source_target_pairs={{0,3},{1,2},{2,1},{3,0},{4,7},{5,6},{6,5},{7,4},{8,11},{9,10},{10,... | collective-permute-start | bytes 152072 | tf_op jit(solution)/shard_map/ppermute | solution.py:48
  543.3 31.7 %collective-permute-start.64 = (bf16[2,288,288]{2,1,0:T(8,128)(2,1)S(1)}, bf16[2,288,288]{2,1,0:T(8,128)(2,1)S(1)}, u32[]{:S(2)}, u32[]{:S(2)}) collective-permute-start(bf16[2,288,288]{2,1,0:T(8,128)(2,1)S(1)} %add_convert_fusion.9), channel_id=1, source_target_pairs={{0,16},{4,20},{8,24},{12,28},{16,0},{20,4},{24,8},{28,12},{1,17},{... | collective-permute-start | bytes 995336 | tf_op jit(solution)/shard_map/ppermute | solution.py:51
  544.2 42.0 %collective-permute-start.52 = (bf16[2,144,1152]{2,1,0:T(8,128)(2,1)S(1)}, bf16[2,144,1152]{2,1,0:T(8,128)(2,1)S(1)}, u32[]{:S(2)}, u32[]{:S(2)}) collective-permute-start(bf16[2,144,1152]{2,1,0:T(8,128)(2,1)S(1)} %add_convert_fusion.8), channel_id=1, source_target_pairs={{0,16},{4,20},{8,24},{12,28},{16,0},{20,4},{24,8},{28,12},{1,17},{... | collective-permute-start | bytes 1990664 | tf_op jit(solution)/shard_map/ppermute | solution.py:51
  546.7 51.6 %collective-permute-start.42 = (f32[11,1152]{1,0:T(8,128)S(1)}, f32[11,1152]{1,0:T(8,128)S(1)}, u32[]{:S(2)}, u32[]{:S(2)}) collective-permute-start(f32[11,1152]{1,0:T(8,128)S(1)} %add_add_fusion), channel_id=1, source_target_pairs={{0,8},{4,12},{8,0},{12,4},{16,24},{20,28},{24,16},{28,20},{1,9},{5... | collective-permute-start | bytes 152072 | tf_op jit(solution)/shard_map/ppermute | solution.py:51
  546.8 51.5 %collective-permute-start.43 = (f32[11,1152]{1,0:T(8,128)S(1)}, f32[11,1152]{1,0:T(8,128)S(1)}, u32[]{:S(2)}, u32[]{:S(2)}) collective-permute-start(f32[11,1152]{1,0:T(8,128)S(1)} %add_add_fusion), channel_id=1, source_target_pairs={{0,16},{4,20},{8,24},{12,28},{16,0},{20,4},{24,8},{28,12},{1,17},{... | collective-permute-start | bytes 152072 | tf_op jit(solution)/shard_map/ppermute | solution.py:51
  549.0 49.3 %collective-permute-start.44 = (f32[11,1152]{1,0:T(8,128)S(1)}, f32[11,1152]{1,0:T(8,128)S(1)}, u32[]{:S(2)}, u32[]{:S(2)}) collective-permute-start(f32[11,1152]{1,0:T(8,128)S(1)} %add_add_fusion), channel_id=1, source_target_pairs={{0,24},{4,28},{8,16},{12,20},{16,8},{20,12},{24,0},{28,4},{1,25},{... | collective-permute-start | bytes 152072 | tf_op jit(solution)/shard_map/ppermute | solution.py:51
  575.4 24.2 %collective-permute-start.65 = (bf16[1,288,288]{2,1,0:T(8,128)(2,1)S(1)}, bf16[1,288,288]{2,1,0:T(8,128)(2,1)S(1)}, u32[]{:S(2)}, u32[]{:S(2)}) collective-permute-start(bf16[1,288,288]{2,1,0:T(8,128)(2,1)S(1)} %slice.186), channel_id=1, source_target_pairs={{0,8},{4,12},{8,0},{12,4},{16,24},{20,28},{24,16},{28,20},{1,9},{5... | collective-permute-start | bytes 497672 | tf_op jit(solution)/shard_map/ppermute | solution.py:51
  (104 other events, 1306.9 us)
Sparse Core Ops, SparseCore 0:
  19.5 65.2 all-gather.3
  87.0 33.4 all-gather.5
  312.5 36.3 reduce-scatter.2
  405.4 36.0 reduce-scatter.4

commit v2 on v1

--- a/solution.py
+++ b/solution.py
@@ -54,15 +54,39 @@
         return lax.ppermute(value, "batch", [(b, b ^ 1) for b in range(self.batch)])
 
 
-def gather_pieces(grid, shard):
-    column = [shard]
-    step = 1
-    while step < grid.depth:
-        column = column + [grid.line(piece, step) for piece in column]
-        step *= 2
-    column = jnp.stack(column)
-    pieces = [grid.plane(column, k) for k in range(grid.seq)]
-    return pieces + [grid.core(piece) for piece in pieces]
+def after(value, *earlier):
+    return lax.optimization_barrier((value, *earlier))[0] if earlier else value
+
+
+def line_gather(grid, shard):
+    return [shard] + [grid.line(shard, i) for i in range(1, grid.depth)]
+
+
+def plane_gather(grid, column, half, *earlier):
+    if grid.seq != 4:
+        return [(grid.plane(column, k), k, 0) for k in range(grid.seq)]
+    first, second = grid.plane(column, 1), grid.plane(column, 2)
+    far = grid.plane(after(second[:half], *earlier), 1), grid.plane(after(first[half:], *earlier), 2)
+    return [(column, 0, 0), (first, 1, 0), (second, 2, 0), (far[0], 3, 0), (far[1], 3, half)]
+
+
+def core_gather(grid, pieces):
+    arrays = [piece[0] for piece in pieces] + [grid.core(piece[0]) for piece in pieces]
+    places = tuple((core, k, start) for core in range(2) for _, k, start in pieces)
+    return arrays, places
+
+
+def with_table(weight, table):
+    rows, cols = weight.shape
+    spare = -cols % 128
+    chunks = -(-table.shape[1] // spare)
+    width = table.shape[1] // chunks
+    strips = [
+        jnp.pad(table[:, n * width : (n + 1) * width], ((0, 16 - table.shape[0]), (0, spare - width)))
+        for n in range(chunks)
+    ]
+    strip = jnp.pad(jnp.concatenate(strips, axis=0), ((0, rows - 16 * chunks), (0, 0)))
+    return jnp.concatenate([weight, strip], axis=1)
 
 
 def swap_plane(grid, parts):
@@ -79,32 +103,66 @@
     return came
 
 
-def scatter_pieces(grid, own, other):
-    wide = lambda value: value.astype(jnp.float32)
-    low = lambda value: value.astype(jnp.bfloat16)
-    order = list(range(1, grid.seq)) + [0]
-    halves = {k: low(wide(own[k]) + wide(grid.core(other[k]))) for k in order}
-    came = [halves[0]] + [grid.plane(halves[k], k) for k in range(1, grid.seq)]
+def swap_both(grid, first, second):
+    if first.shape != second.shape:
+        return swap_plane(grid, first), swap_plane(grid, second)
+    width = first.shape[2]
+    came = swap_plane(grid, jnp.concatenate([first, second], axis=2))
+    return [piece[:, :width] for piece in came], [piece[:, width:] for piece in came]
+
+
+def scatter_far(grid, own, came):
+    if grid.seq != 4:
+        return []
+    half = grid.depth // 2
+    far = own[3].astype(jnp.float32) + came[3].astype(jnp.float32)
+    return [far[:half].astype(jnp.bfloat16), far[half:].astype(jnp.bfloat16)]
+
+
+def total(*terms):
+    return sum(term.astype(jnp.float32) for term in terms)
+
+
+def scatter_near(grid, own, came, far):
+    half = grid.depth // 2
+    if grid.seq != 4:
+        return [total(own[k], came[k]).astype(jnp.bfloat16) for k in range(1, grid.seq)]
+    one, two = lax.optimization_barrier((grid.plane(far[0], 1), grid.plane(far[1], 2)))
+    sent = []
+    for k, low, high in ((1, (), (two,)), (2, (one,), ())):
+        low = total(own[k][:half], came[k][:half], *low).astype(jnp.bfloat16)
+        high = total(own[k][half:], came[k][half:], *high).astype(jnp.bfloat16)
+        sent.append(jnp.concatenate([low, high], axis=0))
+    return sent
+
+
+def scatter_plane(grid, own, other, sent):
+    came = [grid.plane(value, k) for k, value in enumerate(sent, 1)]
+    half = grid.depth // 2
+    terms = [own[0], other[0], *came]
+    away = total(*[piece[half:] for piece in terms]).astype(jnp.bfloat16)
+    return away, total(*[piece[:half] for piece in terms]), came
+
+
+def scatter_line(grid, away, kept, *earlier):
     step = grid.depth // 2
-    column = None
-    while step >= 1:
-        if column is None:
-            away = low(sum(wide(piece[step:]) for piece in came))
-            kept = sum(wide(piece[:step]) for piece in came)
-        else:
-            away, kept = low(column[step:]), column[:step]
-        column = kept + wide(grid.line(away, step))
+    while True:
+        column = kept + grid.line(away, step).astype(jnp.float32)
         step //= 2
-    return column[0]
-
-
-def sum_all(grid, value):
+        if step == 0:
+            return column[0]
+        away, kept = after(column[step:].astype(jnp.bfloat16), *earlier), column[:step]
+
+
+def sum_all(grid, value, *earlier):
     value = value + grid.core(value)
-    for shift, size in ((grid.plane, grid.seq), (grid.line, grid.depth)):
-        terms = [value] + [shift(value, k) for k in range(1, size)]
-        while len(terms) > 1:
-            terms = [terms[n] + terms[n + 1] for n in range(0, len(terms), 2)]
-        value = terms[0]
+    for shift, size in ((grid.line, grid.depth), (grid.plane, grid.seq)):
+        if shift == grid.plane:
+            value = after(value, *earlier)
+        step = 1
+        while step < size:
+            value = value + shift(value, step)
+            step *= 2
     return value
 
 
@@ -117,20 +175,17 @@
 NN, NT, TN = ((1,), (0,)), ((1,), (1,)), ((0,), (0,))
 
 
-def fetch(depth, seq, where_ref, pieces, into, sems):
-    groups = [[] for _ in range(seq)]
-    for core in range(2):
-        for k in range(seq):
-            for i in range(depth):
-                row = (where_ref[0] ^ i) * 2 + (where_ref[1] ^ core)
-                copy = pltpu.make_async_copy(
-                    pieces[core * seq + k].at[i],
-                    into.at[where_ref[2] ^ k, row],
-                    sems.at[(core * seq + k) * depth + i],
-                )
-                copy.start()
-                groups[k].append(copy)
-    return [copy for group in groups for copy in group]
+def fetch(places, where_ref, pieces, into, sems):
+    copies = []
+    for piece, (core, k, start) in zip(pieces, places):
+        for n in range(piece.shape[0]):
+            row = (where_ref[0] ^ (start + n)) * 2 + (where_ref[1] ^ core)
+            copy = pltpu.make_async_copy(
+                piece.at[n], into.at[where_ref[2] ^ k, row], sems.at[len(copies)]
+            )
+            copy.start()
+            copies.append(copy)
+    return copies
 
 
 def weight_rows(buffer, q):
@@ -155,18 +210,28 @@
     return back, jnp.sum(grads * unit, axis=0, keepdims=True), jnp.sum(grads, axis=0, keepdims=True)
 
 
-def merge_kernel(depth, seq, where_ref, tokens_ref, skipped_ref, table_ref, *refs):
-    pieces, (merged_ref, normed_ref, weight, sems) = refs[: 2 * seq], refs[2 * seq :]
-    for copy in fetch(depth, seq, where_ref, pieces, weight, sems):
+def merge_kernel(places, seq, part, cols, where_ref, tokens_ref, skipped_ref, *refs):
+    pieces, rest = refs[: len(places)], refs[len(places) :]
+    merged_ref, normed_ref, table_ref, weight, sems = rest
+    for copy in fetch(places, where_ref, pieces, weight, sems):
         copy.wait()
+    chunks = -(-part[1] // (weight.shape[3] - cols))
+    width = part[1] // chunks
+    table = [
+        weight[0, b, 16 * n : 16 * n + 16, cols : cols + width].astype(jnp.float32)
+        for b in range(weight.shape[1])
+        for n in range(chunks)
+    ]
+    table = jnp.concatenate(table, axis=1)
+    table_ref[...] = table[: part[0]]
     half = tokens_ref.shape[1]
     blocks = []
     for q in range(seq):
-        block = weight_rows(weight, q)
+        block = weight_rows(weight, q)[:, :cols]
         blocks.append(dot(tokens_ref[...], block[:half]) + dot(skipped_ref[...], block[half:]))
-    merged = jnp.concatenate(blocks, axis=1) + table_ref[0:1]
+    merged = jnp.concatenate(blocks, axis=1) + table[0:1]
     merged_ref[...] = merged
-    normed_ref[...] = (norm_rows(merged)[0] * table_ref[1:2] + table_ref[2:3]).astype(jnp.bfloat16)
+    normed_ref[...] = (norm_rows(merged)[0] * table[1:2] + table[2:3]).astype(jnp.bfloat16)
 
 
 def head_of(packed_ref, part, head):
@@ -181,10 +246,10 @@
     return (position < length) | ((position >= CAP) & (position < CAP + 1 + PATCHES))
 
 
-def attend_kernel(depth, seq, where_ref, length_ref, normed_ref, merged_ref, table_ref, *refs):
-    pieces, rest = refs[: 2 * seq], refs[2 * seq :]
-    packed_ref, mixed_ref, logs_ref, residual_ref, normed_two_ref, weight, sems = rest
-    for copy in fetch(depth, seq, where_ref, pieces, weight, sems):
+def attend_kernel(places, seq, where_ref, length_ref, normed_ref, *refs):
+    pieces, rest = refs[: len(places)], refs[len(places) :]
+    packed_ref, mixed_ref, logs_ref, weight, sems = rest
+    for copy in fetch(places, where_ref, pieces, weight, sems):
         copy.wait()
     split = packed_ref.shape[2]
     rows = normed_ref.shape[0]
@@ -200,10 +265,16 @@
         total = jnp.sum(exponent, axis=-1, keepdims=True)
         outs.append(dot((exponent / total).astype(jnp.bfloat16), value))
         logs.append(peak + jnp.log(total))
-    mixed = jnp.concatenate(outs, axis=1).astype(jnp.bfloat16)
-    mixed_ref[...] = mixed
+    mixed_ref[...] = jnp.concatenate(outs, axis=1).astype(jnp.bfloat16)
     logs_ref[...] = jnp.concatenate(logs, axis=1)
-    blocks = [dot(mixed, weight_rows(weight, q)[:, split:]) for q in range(seq)]
+
+
+def branch_kernel(places, seq, split, where_ref, mixed_ref, merged_ref, table_ref, *refs):
+    pieces, rest = refs[: len(places)], refs[len(places) :]
+    residual_ref, normed_two_ref, weight, sems = rest
+    for copy in fetch(places, where_ref, pieces, weight, sems):
+        copy.wait()
+    blocks = [dot(mixed_ref[...], weight_rows(weight, q)[:, split:]) for q in range(seq)]
     residual = merged_ref[...] + jnp.concatenate(blocks, axis=1) + table_ref[3:4]
     residual_ref[...] = residual
     normed_two = norm_rows(residual)[0] * table_ref[4:5] + table_ref[5:6]
@@ -222,15 +293,17 @@
     return value * top / under
 
 
-def hidden_kernel(seq, *refs):
-    cots, shrink_ref, outs = refs[:seq], refs[seq], refs[seq + 1 :]
-    for k in range(seq):
-        outs[k][...] = dot(cots[k][...], shrink_ref[...], NT)
-
-
-def feed_kernel(norm_ref, gradient_ref, expand_ref, shrink_ref, bias_ref, *refs):
-    hidden_ref, grad_preact_ref, forth_ref, back_ref, sums_ref = refs
-    preact = dot(norm_ref[...], expand_ref[...]) + bias_ref[...]
+def hidden_kernel(parts, shrink_ref, *refs):
+    cots, outs = refs[: len(parts)], refs[len(parts) :]
+    for (n, start), cot in zip(parts, cots):
+        outs[n][start : start + cot.shape[0]] = dot(cot[...], shrink_ref[...], NT)
+
+
+def feed_kernel(parts, *refs):
+    norms, refs = refs[:parts], refs[parts:]
+    gradient_ref, expand_ref, bias_ref, hidden_ref, grad_preact_ref, back_ref, sums_ref = refs
+    norm = jnp.concatenate([norm[...] for norm in norms], axis=0)
+    preact = dot(norm, expand_ref[...]) + bias_ref[...]
     bell = 0.5 + 0.5 * error_function(preact * 0.7071067811865476)
     hidden = (preact * bell).astype(jnp.bfloat16)
     hidden_ref[...] = hidden
@@ -239,22 +312,39 @@
     grad_preact_ref[...] = grad_preact
     sums_ref[...] = jnp.sum(grad_preact.astype(jnp.float32), axis=0, keepdims=True)
     back_ref[...] = dot(grad_preact, expand_ref[...], NT).astype(jnp.bfloat16)
-    forth_ref[...] = dot(hidden, shrink_ref[...]).astype(jnp.bfloat16)
-
-
-def feed_weights_kernel(seq, *refs):
-    norms, grads, hiddens, cots = (refs[n * seq : (n + 1) * seq] for n in range(4))
-    expand_ref, shrink_ref = refs[4 * seq :]
-    expand = sum(dot(norms[k][...], grads[k][...], TN) for k in range(seq))
-    expand_ref[...] = expand.astype(jnp.bfloat16)
-    shrink = sum(dot(hiddens[k][...], cots[k][...], TN) for k in range(seq))
-    shrink_ref[...] = shrink.astype(jnp.bfloat16)
-
-
-def attend_back_kernel(depth, seq, where_ref, length_ref, cot_ref, residual_ref, table_ref, packed_ref, logs_ref, *refs):
-    backs, pieces, rest = refs[:seq], refs[seq : 3 * seq], refs[3 * seq :]
+
+
+def forth_kernel(seq, *refs):
+    hiddens, shrink_ref, outs = refs[:seq], refs[seq], refs[seq + 1 :]
+    for k in range(seq):
+        outs[k][...] = dot(hiddens[k][...], shrink_ref[...]).astype(jnp.bfloat16)
+
+
+def feed_weights_kernel(seq, norm_parts, cot_parts, *refs):
+    norms, refs = refs[: len(norm_parts)], refs[len(norm_parts) :]
+    cots, refs = refs[: len(cot_parts)], refs[len(cot_parts) :]
+    grads, hiddens, outs = refs[:seq], refs[seq : 2 * seq], refs[2 * seq :]
+    expand = shrink = 0.0
+    for (k, start), norm in zip(norm_parts, norms):
+        expand = expand + dot(norm[...], grads[k][start : start + norm.shape[0]], TN)
+    expand = expand.astype(jnp.bfloat16)
+    for (k, start), cot in zip(cot_parts, cots):
+        shrink = shrink + dot(hiddens[k][start : start + cot.shape[0]], cot[...], TN)
+    shrink = shrink.astype(jnp.bfloat16)
+    if len(outs) == 2:
+        outs[0][...], outs[1][...] = expand, shrink
+        return
+    batch, rows = outs[0].shape[0], expand.shape[0] // outs[0].shape[0]
+    for b in range(batch):
+        outs[0][b, :rows] = expand[b * rows : (b + 1) * rows]
+        outs[0][b, rows:] = shrink[b * (outs[0].shape[1] - rows) : (b + 1) * (outs[0].shape[1] - rows)]
+
+
+def attend_back_kernel(places, seq, where_ref, length_ref, cot_ref, residual_ref, table_ref, packed_ref, logs_ref, *refs):
+    backs, refs = refs[:seq], refs[seq:]
+    pieces, rest = refs[: len(places)], refs[len(places) :]
     branch_ref, grad_residual_ref, grad_packed_ref, sums_ref, weight, sems = rest
-    copies = fetch(depth, seq, where_ref, pieces, weight, sems)
+    copies = fetch(places, where_ref, pieces, weight, sems)
     wide = lambda value: value.astype(jnp.float32)
     grads = sum(wide(back[...]) for back in backs)
     back, gain_sum, shift_sum = norm_pull(grads, table_ref[4:5], residual_ref[...])
@@ -340,10 +430,10 @@
         copy.wait()
 
 
-def norm_back_kernel(depth, seq, where_ref, grad_packed_ref, merged_ref, table_ref, grad_residual_ref, *refs):
-    pieces, rest = refs[: 2 * seq], refs[2 * seq :]
+def norm_back_kernel(places, seq, where_ref, grad_packed_ref, merged_ref, table_ref, grad_residual_ref, *refs):
+    pieces, rest = refs[: len(places)], refs[len(places) :]
     grad_merged_ref, sums_ref, weight, sems = rest
-    for copy in fetch(depth, seq, where_ref, pieces, weight, sems):
+    for copy in fetch(places, where_ref, pieces, weight, sems):
         copy.wait()
     split = grad_packed_ref.shape[2]
     grads = sum(dot(grad_packed_ref[q], weight_rows(weight, q)[:, :split], NT) for q in range(seq))
@@ -357,13 +447,14 @@
     sums_ref[2:3] = shift_sum
 
 
-def joined_back_kernel(depth, seq, where_ref, grad_ref, *refs):
-    pieces, rest = refs[: 2 * seq], refs[2 * seq :]
+def joined_back_kernel(places, seq, where_ref, grad_ref, *refs):
+    pieces, rest = refs[: len(places)], refs[len(places) :]
     tokens_ref, skipped_ref, weight, sems = rest
-    for copy in fetch(depth, seq, where_ref, pieces, weight, sems):
+    for copy in fetch(places, where_ref, pieces, weight, sems):
         copy.wait()
     half = tokens_ref.shape[1]
-    blocks = [weight_rows(weight, q) for q in range(seq)]
+    cols = grad_ref.shape[2]
+    blocks = [weight_rows(weight, q)[:, :cols] for q in range(seq)]
     tokens_ref[...] = sum(dot(grad_ref[q], blocks[q][:half], NT) for q in range(seq))
     skipped_ref[...] = sum(dot(grad_ref[q], blocks[q][half:], NT) for q in range(seq))
 
@@ -373,20 +464,21 @@
 ANY = pl.BlockSpec(memory_space=pl.ANY)
 
 
-def call(kernel, outs, specs, operands, out_specs=None, scratch=(), flops=0, name=None):
-    single = not isinstance(outs, (list, tuple))
-    shapes = [outs] if single else list(outs)
-    found = pl.pallas_call(
-        kernel,
-        out_shape=[jax.ShapeDtypeStruct(shape, kind) for shape, kind in shapes],
-        in_specs=specs,
-        out_specs=out_specs or [VMEM] * len(shapes),
+def call(kernel, outs, specs, operands, out_specs=None, scratch=(), flops=0, behind=()):
+    inputs = len(operands)
+
+    def body(*refs):
+        kernel(*refs[:inputs], *refs[inputs + len(behind) :])
+
+    return pl.pallas_call(
+        body,
+        out_shape=[jax.ShapeDtypeStruct(shape, kind) for shape, kind in outs],
+        in_specs=list(specs) + [ANY] * len(behind),
+        out_specs=out_specs or [VMEM] * len(outs),
         scratch_shapes=list(scratch),
         compiler_params=pltpu.CompilerParams(vmem_limit_bytes=52 * 1024 * 1024),
         cost_estimate=pl.CostEstimate(flops=flops, bytes_accessed=flops // 300, transcendentals=0),
-        name=name,
-    )(*operands)
-    return found
+    )(*operands, *behind)
 
 
 def local(
@@ -429,121 +521,169 @@
     bf16, f32 = jnp.bfloat16, jnp.float32
     where = jnp.stack([grid.z, grid.c, grid.j]).astype(jnp.int32)
 
-    table = wide(lax.all_gather(low(vectors), "batch", axis=1, tiled=True))
     merge_rows, merge_cols = merging.shape
+    merge_shard = with_table(low(merging), low(vectors))
+    merge_column = line_gather(grid, merge_shard)
     in_rows, in_cols = inflow.shape
     both_cols = in_cols + outflow.shape[1]
-    merge_pieces = gather_pieces(grid, low(merging))
-    both_pieces = gather_pieces(grid, jnp.concatenate([low(inflow), low(outflow)], axis=1))
-
     unit = shrink.shape[0] // S
     send_expand = low(expand).reshape(expand.shape[0], B // S, S, unit).transpose(2, 0, 1, 3)
     send_expand = send_expand.reshape(S, expand.shape[0], -1)
     send_shrink = low(shrink).reshape(S, unit, shrink.shape[1])
-    expand_rows_own = jnp.concatenate(swap_plane(grid, send_expand), axis=1)
-    shrink_rows_own = jnp.concatenate(swap_plane(grid, send_shrink), axis=1)
-    expand_part = lax.all_gather(expand_rows_own, "batch", axis=0, tiled=True)
-    shrink_part = lax.all_gather(shrink_rows_own, "batch", axis=0, tiled=True)
-    units = expand_part.shape[1]
+    expand_came, shrink_came = swap_both(grid, send_expand, send_shrink)
 
     flat_tokens = tokens.reshape(row_count, model_width)
     flat_skipped = skipped.reshape(row_count, model_width)
     upstream = cotangent.reshape(row_count, model_width)
-    upstreams = [grid.plane(upstream, k) for k in range(S)]
-
-    ff_rows = vectors.shape[0] - 7
-    expand_bias = table[6 : 6 + ff_rows].reshape(B, S, unit)
-    expand_bias = lax.dynamic_index_in_dim(expand_bias, grid.j, 1, keepdims=False).reshape(1, -1)
-    shrink_bias = table[6 + ff_rows]
+    split_rows = row_count // 2 // 16 * 16
+    cot_near = [grid.plane(upstream, k) for k in (range(1, S) if S != 4 else (1, 2))]
+
+    merge_plane = plane_gather(grid, after(jnp.stack(merge_column), *cot_near, expand_came[0]), Z // 2)
+    merge_pieces, merge_places = core_gather(grid, merge_plane)
+
+    both_shard = jnp.concatenate([low(inflow), low(outflow)], axis=1)
+    both_column = line_gather(grid, after(both_shard, *merge_column[1:]))
+
+    merge_far = [piece[0] for piece in merge_plane[-2:]]
+    expand_rows_own = after(jnp.concatenate(expand_came, axis=1), *both_column[1:], *merge_far)
+    shrink_rows_own = after(jnp.concatenate(shrink_came, axis=1), *both_column[1:], *merge_far)
+    shrink_part = lax.all_gather(shrink_rows_own, "batch", axis=0, tiled=True)
+    expand_part = lax.all_gather(expand_rows_own, "batch", axis=0, tiled=True)
+    units = expand_part.shape[1]
 
     wide_rows = ((row_count, model_width), f32)
     low_rows = ((row_count, model_width), bf16)
     merge_scratch = [
-        pltpu.VMEM((S, B, merge_rows, merge_cols), bf16),
+        pltpu.VMEM((S, B, *merge_shard.shape), bf16),
         pltpu.SemaphoreType.DMA((2 * S * Z,)),
     ]
     both_scratch = [
         pltpu.VMEM((S, B, in_rows, both_cols), bf16),
         pltpu.SemaphoreType.DMA((2 * S * Z,)),
     ]
-    many = [ANY] * (2 * S)
+    many_merge = [ANY] * len(merge_pieces)
     layer_flops = 2 * row_count * model_width * model_width
 
-    merged, normed = call(
-        partial(merge_kernel, Z, S),
-        [wide_rows, low_rows],
-        [SMEM, VMEM, VMEM, VMEM] + many,
-        (where, flat_tokens, flat_skipped, table, *merge_pieces),
+    merged, normed, table = call(
+        partial(merge_kernel, merge_places, S, vectors.shape, merge_cols),
+        [wide_rows, low_rows, ((vectors.shape[0], model_width), f32)],
+        [SMEM, VMEM, VMEM] + many_merge,
+        (where, flat_tokens, flat_skipped, *merge_pieces),
         scratch=merge_scratch,
         flops=2 * layer_flops,
     )
-    packed, mixed, logs, residual, normed_two = call(
-        partial(attend_kernel, Z, S),
-        [
-            ((S, row_count, in_cols), bf16),
-            low_rows,
-            ((row_count, HEADS), f32),
-            wide_rows,
-            low_rows,
-        ],
-        [SMEM, SMEM, VMEM, VMEM, VMEM] + many,
-        (where, lengths, normed, merged, table, *both_pieces),
+    ff_rows = vectors.shape[0] - 7
+    expand_bias = table[6 : 6 + ff_rows].reshape(B, S, unit)
+    expand_bias = lax.dynamic_index_in_dim(expand_bias, grid.j, 1, keepdims=False).reshape(1, -1)
+    shrink_bias = table[6 + ff_rows]
+
+    merge_far = [merge_pieces[-1], merge_pieces[-2]]
+    both_plane = plane_gather(grid, after(jnp.stack(both_column), *merge_far), Z // 2, merged)
+    unit_rows = ((row_count, units), f32)
+    low_units = ((row_count, units), bf16)
+    cot_plane = [(upstream, 0, 0)] + [(piece, k, 0) for k, piece in enumerate(cot_near, 1)]
+
+    def grad_hidden_of(chosen):
+        cots = [piece for piece in cot_plane if piece[1] in chosen]
+        parts = tuple((chosen.index(k), start) for _, k, start in cots)
+        return call(
+            partial(hidden_kernel, parts),
+            [unit_rows] * len(chosen),
+            [VMEM] * (len(cots) + 1),
+            (shrink_part, *[piece[0] for piece in cots]),
+            flops=len(chosen) * layer_flops,
+        )
+
+    grad_hiddens = grad_hidden_of([0, 1, 2])
+    both_plane = [
+        (after(piece, *grad_hiddens) if n >= len(both_plane) - 2 else piece, k, start)
+        for n, (piece, k, start) in enumerate(both_plane)
+    ]
+    both_pieces, both_places = core_gather(grid, both_plane)
+    many_both = [ANY] * len(both_pieces)
+    packed, mixed, logs = call(
+        partial(attend_kernel, both_places, S),
+        [((S, row_count, in_cols), bf16), low_rows, ((row_count, HEADS), f32)],
+        [SMEM, SMEM, VMEM] + many_both,
+        (where, lengths, normed, *both_pieces),
         scratch=both_scratch,
         flops=6 * layer_flops,
     )
-    norms = [grid.plane(normed_two, k) for k in range(S)]
-
-    unit_rows = ((row_count, units), f32)
-    low_units = ((row_count, units), bf16)
-    grad_hiddens = call(
-        partial(hidden_kernel, S),
-        [unit_rows] * S,
+    if S == 4:
+        late = both_pieces[-2:]
+        cot_plane.append((grid.plane(after(cot_near[1][:split_rows], *late), 1), 3, 0))
+        cot_plane.append((grid.plane(after(cot_near[0][split_rows:], *late), 2), 3, split_rows))
+
+    residual, normed_two = call(
+        partial(branch_kernel, both_places, S, in_cols),
+        [wide_rows, low_rows],
+        [SMEM, VMEM, VMEM, VMEM] + many_both,
+        (where, mixed, merged, table, *both_pieces),
+        scratch=both_scratch,
+        flops=layer_flops,
+        behind=[piece[0] for piece in cot_plane[3:]],
+    )
+    grad_hiddens += grad_hidden_of(list(range(3, S)))
+    hiddens, grad_preacts, backs, unit_sums = [], [], [], []
+    norm_plane = [(normed_two, 0, 0)]
+    for k in range(S):
+        if k == 1:
+            norm_plane += [(grid.plane(normed_two, n), n, 0) for n in (range(1, S) if S != 4 else (1, 2))]
+        if k == 2 and S == 4:
+            first, second = norm_plane[1][0], norm_plane[2][0]
+            norm_plane.append((grid.plane(after(second[:split_rows], hiddens[1]), 1), 3, 0))
+            norm_plane.append((grid.plane(after(first[split_rows:], hiddens[1]), 2), 3, split_rows))
+        norms = [piece[0] for piece in norm_plane if piece[1] == k]
+        hidden, grad_preact, back, unit_sum = call(
+            partial(feed_kernel, len(norms)),
+            [low_units, low_units, low_rows, ((1, units), f32)],
+            [VMEM] * (len(norms) + 3),
+            (*norms, grad_hiddens[k], expand_part, expand_bias),
+            flops=3 * layer_flops,
+            behind=backs[-1:] and (hiddens[-1],),
+        )
+        hiddens.append(hidden)
+        grad_preacts.append(grad_preact)
+        backs.append(grid.plane(back, k))
+        unit_sums.append(unit_sum)
+    joint = units == model_width
+    fed_rows = model_width // B + unit
+    fed = call(
+        partial(feed_weights_kernel, S, *(tuple(piece[1:] for piece in plane) for plane in (norm_plane, cot_plane))),
+        [((B, fed_rows, units), bf16)] if joint else [((model_width, units), bf16), ((units, model_width), bf16)],
+        [VMEM] * (len(norm_plane) + len(cot_plane) + 2 * S),
+        (*[piece[0] for piece in norm_plane], *[piece[0] for piece in cot_plane], *grad_preacts, *hiddens),
+        flops=2 * S * layer_flops,
+    )
+    if joint:
+        own_fed = lax.psum_scatter(fed[0], "batch", scatter_dimension=0)
+        own_expand, own_shrink = own_fed[:-unit], own_fed[-unit:]
+    else:
+        own_expand = lax.psum_scatter(fed[0].reshape(B, -1, units), "batch", scatter_dimension=0)
+        own_shrink = lax.psum_scatter(fed[1].reshape(B, unit, -1), "batch", scatter_dimension=0)
+    forths = call(
+        partial(forth_kernel, S),
+        [low_rows] * S,
         [VMEM] * (S + 1),
-        (*upstreams, shrink_part),
+        (*hiddens, shrink_part),
         flops=S * layer_flops,
-    )
-    fed = [
-        call(
-            feed_kernel,
-            [low_units, low_units, low_rows, low_rows, ((1, units), f32)],
-            [VMEM] * 5,
-            (norms[k], grad_hiddens[k], expand_part, shrink_part, expand_bias),
-            flops=4 * layer_flops,
-        )
-        for k in range(S)
-    ]
-    hiddens, grad_preacts, forths, backs, unit_sums = zip(*fed)
-    backs = [grid.plane(backs[k], k) for k in range(S)]
-    grad_expand, grad_shrink = call(
-        partial(feed_weights_kernel, S),
-        [((model_width, units), bf16), ((units, model_width), bf16)],
-        [VMEM] * (4 * S),
-        (*norms, *grad_preacts, *hiddens, *upstreams),
-        flops=2 * S * layer_flops,
-    )
-    forths = [grid.plane(forths[k], k) for k in range(S)]
+        behind=fed[:1],
+    )
+    forths = [forths[0]] + [grid.plane(after(forths[k], *backs[1:]), k) for k in range(1, S)]
     result = residual + sum(wide(piece) for piece in forths) + shrink_bias
-    own_expand = lax.psum_scatter(grad_expand.reshape(B, -1, units), "batch", scatter_dimension=0)
-    own_shrink = lax.psum_scatter(grad_shrink.reshape(B, unit, -1), "batch", scatter_dimension=0)
-    back_expand = own_expand.reshape(own_expand.shape[0], S, -1).transpose(1, 0, 2)
-    back_shrink = own_shrink.reshape(unit, S, -1).transpose(1, 0, 2)
-    shard_expand = jnp.stack(swap_plane(grid, back_expand), axis=0)
-    shard_expand = shard_expand.reshape(S, expand.shape[0], B // S, unit).transpose(1, 2, 0, 3)
-    shard_expand = wide(shard_expand).reshape(expand.shape)
-    shard_shrink = wide(jnp.stack(swap_plane(grid, back_shrink), axis=0)).reshape(shrink.shape)
-
     branches, grad_residual, grad_packed, sums_two = call(
-        partial(attend_back_kernel, Z, S),
+        partial(attend_back_kernel, both_places, S),
         [
             ((S, row_count, merge_cols), bf16),
             wide_rows,
             ((S, row_count, in_cols), bf16),
             ((8, model_width), f32),
         ],
-        [SMEM, SMEM] + [VMEM] * (5 + S) + many,
+        [SMEM, SMEM] + [VMEM] * (5 + S) + many_both,
         (where, lengths, upstream, residual, table, packed, logs, *backs, *both_pieces),
         scratch=both_scratch,
         flops=4 * layer_flops,
+        behind=forths[:1],
     )
     own_both, other_both = [], []
     found = call(
@@ -554,50 +694,74 @@
         out_specs=[ANY] * (2 * S),
         scratch=[pltpu.VMEM((S, B, in_rows, both_cols), bf16), pltpu.SemaphoreType.DMA((S * B,))],
         flops=4 * layer_flops,
-    )
-    shard_both = scatter_pieces(grid, found[:S], found[S:])
-    shard_inflow, shard_outflow = shard_both[:, :in_cols], shard_both[:, in_cols:]
+        behind=forths[1:],
+    )
+    both_own, both_other = found[:S], [grid.core(piece) for piece in found[S:]]
+    both_far = scatter_far(grid, both_own, both_other)
+    both_sent = scatter_near(grid, both_own, both_other, both_far)
+    both_away, both_kept, both_came = scatter_plane(grid, both_own, both_other, both_sent)
     grad_merged, sums_one = call(
-        partial(norm_back_kernel, Z, S),
+        partial(norm_back_kernel, both_places, S),
         [((S, row_count, merge_cols), bf16), ((8, model_width), f32)],
-        [SMEM] + [VMEM] * 4 + many,
+        [SMEM] + [VMEM] * 4 + many_both,
         (where, grad_packed, merged, table, grad_residual, *both_pieces),
         scratch=both_scratch,
         flops=3 * layer_flops,
+        behind=both_far,
     )
     found = call(
         partial(merge_weights_kernel, Z, S),
         [((Z, merge_rows, merge_cols), bf16)] * (2 * S),
         [SMEM] + [VMEM] * 3,
         (where, flat_tokens, flat_skipped, grad_merged),
+        behind=both_sent,
         out_specs=[ANY] * (2 * S),
         scratch=[pltpu.VMEM((S, B, merge_rows, merge_cols), bf16), pltpu.SemaphoreType.DMA((S * B,))],
         flops=2 * layer_flops,
     )
-    shard_merging = scatter_pieces(grid, found[:S], found[S:])
+    merge_own, merge_other = found[:S], [grid.core(piece) for piece in found[S:]]
+    merge_far = [after(piece, *both_came) for piece in scatter_far(grid, merge_own, merge_other)]
+    merge_sent = scatter_near(grid, merge_own, merge_other, merge_far)
+    merge_away, merge_kept, _ = scatter_plane(grid, merge_own, merge_other, merge_sent)
+    shard_both = scatter_line(grid, both_away, both_kept, merge_away)
+    shard_inflow, shard_outflow = shard_both[:, :in_cols], shard_both[:, in_cols:]
     tokens_grad, skipped_grad = call(
-        partial(joined_back_kernel, Z, S),
+        partial(joined_back_kernel, merge_places, S),
         [wide_rows, wide_rows],
-        [SMEM, VMEM] + many,
+        [SMEM, VMEM] + many_merge,
         (where, grad_merged, *merge_pieces),
         scratch=merge_scratch,
         flops=2 * layer_flops,
+        behind=merge_sent,
     )
     tokens_grad = tokens_grad.reshape(tokens.shape)
     skipped_grad = skipped_grad.reshape(tokens.shape)
 
+    own_expand, own_shrink = after(own_expand, merge_away), after(own_shrink, merge_away)
+    back_expand = own_expand.reshape(own_expand.shape[0], S, -1).transpose(1, 0, 2)
+    back_shrink = own_shrink.reshape(unit, S, -1).transpose(1, 0, 2)
+    expand_came, shrink_came = swap_both(grid, back_expand, back_shrink)
+    shard_expand = jnp.stack(expand_came, axis=0)
+    shard_expand = shard_expand.reshape(S, expand.shape[0], B // S, unit).transpose(1, 2, 0, 3)
+    shard_expand = wide(shard_expand).reshape(expand.shape)
+    shard_shrink = wide(jnp.stack(shrink_came, axis=0)).reshape(shrink.shape)
+    shard_merging = scatter_line(grid, merge_away, merge_kept, *expand_came, *shrink_came)
     expand_sums = sum(unit_sums).reshape(B, 1, unit)
     expand_sums = lax.dynamic_update_slice(jnp.zeros((B, S, unit), f32), expand_sums, (0, grid.j, 0))
     grad_table = jnp.concatenate(
         [sums_one[:3], sums_two[2:3], sums_two[:2], expand_sums.reshape(ff_rows, model_width), sums_two[3:4]],
         axis=0,
     )
-    whole_table = sum_all(grid, grad_table)
+    whole_table = sum_all(grid, grad_table, merge_away)
     table_grad = lax.dynamic_slice_in_dim(whole_table, grid.b * vectors.shape[1], vectors.shape[1], 1)
     gradients = (shard_inflow, shard_outflow, shard_expand, shard_merging, shard_shrink, table_grad)
     local_square = jnp.sum(table_grad * table_grad) / S
     for shard_grad in gradients[:5]:
         local_square = local_square + jnp.sum(shard_grad * shard_grad)
+    local_square, shard_expand, shard_shrink = lax.optimization_barrier(
+        (local_square, shard_expand, shard_shrink)
+    )
+    gradients = (shard_inflow, shard_outflow, shard_expand, shard_merging, shard_shrink, table_grad)
     total_square = sum_all(grid, local_square)
     grad_norm = jnp.sqrt(total_square)
     clip_factor = CLIP / jnp.maximum(grad_norm, CLIP)

time: 685 us -> 492 us (0.72)
  waiting for transfers between devices: 331 us -> 144 us
  blocking collectives: 14.1 us -> 0 us
  Pallas kernels: 160 us -> 168 us
  other arithmetic: 33 us -> 40.5 us
    ppermute x42 -> x40, waiting for transfers between devices: 238 us -> 98.6 us  [plane(): return lax.ppermute(value, 'seq', [(j, j ^ k) for j in range(self.seq)])]
    ppermute x16 -> x14, waiting for transfers between devices: 87.7 us -> 35.5 us  [line(): lax.ppermute(value, 'batch', [(b, b ^ 2 * k) for b in range(self.batch)])]
    all_gather x1 -> x0, blocking collectives: 14.1 us -> none  [local(): table = wide(lax.all_gather(low(vectors), 'batch', axis=1, tiled=True))]
    slice x2 -> x17, local copies, waits for them, and re-layouts: 0.07 us -> 11.7 us  [the longest x2 3.04 us: plane_gather(): first[half:]]
    ppermute x42 -> x40, starting transfers between devices: 55.4 us -> 47 us  [plane(): return lax.ppermute(value, 'seq', [(j, j ^ k) for j in range(self.seq)])]
    pallas_call x13 -> x16, Pallas kernels: 160 us -> 168 us  [call(): pl.pallas_call(body, out_shape=[jax.ShapeDtypeStruct(shape, kind) for sha...]
    unnamed x151 -> x155, local copies, waits for them, and re-layouts: 14.7 us -> 9.04 us
    ppermute x16 -> x14, starting transfers between devices: 24.4 us -> 27.3 us  [line(): lax.ppermute(value, 'batch', [(b, b ^ 2 * k) for b in range(self.batch)])]
  transfers between devices with their start and end apart: 80 -> 77, of which waited for: 34 -> 35; matrix products, arithmetic and copies ran while one was open for 4% -> 9% of each run, Pallas kernels for 20% -> 35%
where the time goes in v2:
time: 492 us; the launch traced here: 487 us
  Pallas kernels  168 us (34%)
  waiting for transfers between devices  144 us (29%)
  starting transfers between devices  79.8 us (16%)
  other arithmetic  40.5 us (8%)
  local copies, waits for them, and re-layouts  29.7 us (6%)
  between operations  24.1 us (5%)
    pallas_call x16, Pallas kernels, call(): pl.pallas_call(body, out_shape=[jax.ShapeDtypeStruct(shape, kind) for sha...  168 us
    ppermute x40, waiting for transfers between devices, plane(): return lax.ppermute(value, 'seq', [(j, j ^ k) for j in range(self.seq)])  98.6 us
    ppermute x40, starting transfers between devices, plane(): return lax.ppermute(value, 'seq', [(j, j ^ k) for j in range(self.seq)])  47 us
    ppermute x14, waiting for transfers between devices, line(): lax.ppermute(value, 'batch', [(b, b ^ 2 * k) for b in range(self.batch)])  35.5 us
    ppermute x14, starting transfers between devices, line(): lax.ppermute(value, 'batch', [(b, b ^ 2 * k) for b in range(self.batch)])  27.3 us
    add x6, other arithmetic, adamw(): smoothed = SHADOW * shadow + (1.0 - SHADOW) * trained  10.7 us
    ppermute x20, waiting for transfers between devices, core(): return lax.ppermute(value, 'batch', [(b, b ^ 1) for b in range(self.batch)])  10.1 us
  transfers between devices with their start and end apart: 77, of which 35 were waited for; matrix products, arithmetic and copies ran while one was open for 9% of the time, Pallas kernels for 35%

profile of v2, /device:TPU:0, one launch (start us, length us, event | category | flops | bytes accessed | tf_op | source)
XLA Modules:
  0.0 486.6 jit_solution(17354531188088542297)
XLA Ops:
  11.4 3.9 collective-permute-start.5
  16.1 4.1 collective-permute-start.2
  26.6 11.5 %collective-permute-done.1 = bf16[288,384]{1,0:T(8,128)(2,1)S(1)} collective-permute-done((bf16[288,384]{1,0:T(8,128)(2,1)S(1)}, bf16[288,384]{1,0:T(8,128)(2,1)S(1)}, u32[]{:S(2)}, u32[]{:S(2)}) %collective-permute-start.1) | collective-permute-done | bytes 221216 | tf_op jit(solution)/shard_map/ppermute | solution.py:51
  38.3 5.0 %collective-permute-done.3.refs_2_.refs_6_ = bf16[336,1152]{1,0:T(8,128)(2,1)S(1)} collective-permute-done((bf16[336,1152]{1,0:T(8,128)(2,1)S(1)}, bf16[336,1152]{1,0:T(8,128)(2,1)S(1)}, u32[]{:S(2)}, u32[]{:S(2)}) %collective-permute-start.3) | collective-permute-done | bytes 774176 | tf_op jit(solution)/shard_map/ppermute | solution.py:48
  46.9 3.7 collective-permute-start.19
  51.4 13.8 %collective-permute-done.9.refs_5_.refs_4_ = bf16[4,288,384]{2,1,0:T(8,128)(2,1)} collective-permute-done((bf16[4,288,384]{2,1,0:T(8,128)(2,1)S(1)}, bf16[4,288,384]{2,1,0:T(8,128)(2,1)}, u32[]{:S(2)}, u32[]{:S(2)}) %collective-permute-start.9) | collective-permute-done | bytes 884768 | tf_op jit(solution)/shard_map/ppermute | solution.py:48
  70.8 6.7 %collective-permute-done.18 = bf16[144,1152]{1,0:T(8,128)(2,1)} collective-permute-done((bf16[144,1152]{1,0:T(8,128)(2,1)S(1)}, bf16[144,1152]{1,0:T(8,128)(2,1)}, u32[]{:S(2)}, u32[]{:S(2)}) %collective-permute-start.18) | collective-permute-done | bytes 331808 | tf_op jit(solution)/shard_map/ppermute | solution.py:51
  80.4 2.4 pad_maximum_fusion.refs_3_.refs_4_.refs_11_.refs_5_
  85.5 3.2 collective-permute-done.12.refs_8_.refs_7_
  90.7 10.0 %shard_map.491 = (f32[336,1152]{1,0:T(8,128)}, bf16[336,1152]{1,0:T(8,128)(2,1)}, f32[11,1152]{1,0:T(8,128)S(1)}) custom-call(s32[3]{0:T(128)S(1)} %pad_add_fusion.refs_0_, bf16[336,1152]{1,0:T(8,128)(2,1)} %bitcast.71, bf16[336,1152]{1,0:T(8,128)(2,1)} %bitcast.73, bf16[4,288,384]{2,1,0:T(8,128)(2,1)} %copy-done.26, ...), custom_call_target="tpu_custom_call" | custom-call | flops 1783627776 | bytes 5945425 | tf_op jit(solution)/shard_map/pallas_call | solution.py:473
  100.7 13.6 %collective-permute-done.21.refs_5_.refs_6_.refs_13_.refs_7_ = bf16[4,144,1152]{2,1,0:T(8,128)(2,1)} collective-permute-done((bf16[4,144,1152]{2,1,0:T(8,128)(2,1)}, bf16[4,144,1152]{2,1,0:T(8,128)(2,1)}, u32[]{:S(2)}, u32[]{:S(2)}) %collective-permute-start.21) | collective-permute-done | bytes 1327136 | tf_op jit(solution)/shard_map/ppermute | solution.py:48
  123.1 6.6 %shard_map.492 = (f32[336,1152]{1,0:T(8,128)}, f32[336,1152]{1,0:T(8,128)}, f32[336,1152]{1,0:T(8,128)}) custom-call(bf16[1152,1152]{1,0:T(8,128)(2,1)} %all-gather.3.cloned.1.call-done.refs_0_.refs_4_, bf16[336,1152]{1,0:T(8,128)(2,1)S(1)} %bitcast.79, bf16[336,1152]{1,0:T(8,128)(2,1)S(1)} %copy-done.15, bf16[336,1152]{1,0:T(8,128)(2,1)} %copy-done.69), custom_call_target="tpu_custom_call" | custom-call | flops 2675441664 | bytes 8918138 | tf_op jit(solution)/shard_map/pallas_call | solution.py:473
  129.8 2.7 collective-permute-done.22.refs_6_.refs_7_.refs_14_.refs_8_
  132.5 2.8 collective-permute-done.23.refs_7_.refs_8_.refs_15_.refs_9_
  140.5 15.4 %shard_map.493 = (bf16[4,336,864]{2,1,0:T(8,128)(2,1)}, bf16[336,1152]{1,0:T(8,128)(2,1)}, f32[336,16]{1,0:T(8,128)S(1)}) custom-call(s32[3]{0:T(128)S(1)} %pad_add_fusion.refs_0_, s32[1]{0:T(128)S(6)} %copy.81.refs_1_, bf16[336,1152]{1,0:T(8,128)(2,1)} %get-tuple-element.115.refs_2_.refs_1_, ...), custom_call_target="tpu_custom_call" | custom-call | flops 5350883328 | bytes 17836276 | tf_op jit(solution)/shard_map/pallas_call | solution.py:473
  155.9 9.6 %shard_map.494 = (f32[336,1152]{1,0:T(8,128)}, bf16[336,1152]{1,0:T(8,128)(2,1)}) custom-call(s32[3]{0:T(128)S(1)} %pad_add_fusion.refs_0_, bf16[336,1152]{1,0:T(8,128)(2,1)} %get-tuple-element.127.refs_1_.refs_2_, f32[336,1152]{1,0:T(8,128)} %get-tuple-element.118.refs_2_, f32[11,1152]{1,0:T(8,128)S(1)} %copy-done.7, ...), custom_call_target="tpu_custom_call" | custom-call | flops 891813888 | bytes 2972712 | tf_op jit(solution)/shard_map/pallas_call | solution.py:473
  167.9 7.4 %shard_map.495 = (bf16[336,1152]{1,0:T(8,128)(2,1)S(1)}, bf16[336,1152]{1,0:T(8,128)(2,1)S(1)}, bf16[336,1152]{1,0:T(8,128)(2,1)}, f32[1,1152]{1,0:T(1,128)S(1)}) custom-call(bf16[336,1152]{1,0:T(8,128)(2,1)} %get-tuple-element.132.refs_0_, f32[336,1152]{1,0:T(8,128)} %get-tuple-element.121.refs_1_, ...), custom_call_target="tpu_custom_call" | custom-call | flops 2675441664 | bytes 8918138 | tf_op jit(solution)/shard_map/pallas_call | solution.py:473
  176.1 8.5 %collective-permute-done.31.refs_0_.refs_1_ = bf16[336,1152]{1,0:T(8,128)(2,1)} collective-permute-done((bf16[336,1152]{1,0:T(8,128)(2,1)}, bf16[336,1152]{1,0:T(8,128)(2,1)}, u32[]{:S(2)}, u32[]{:S(2)}) %collective-permute-start.31) | collective-permute-done | bytes 774176 | tf_op jit(solution)/shard_map/ppermute | solution.py:48
  185.7 7.5 %shard_map.496 = (bf16[336,1152]{1,0:T(8,128)(2,1)S(1)}, bf16[336,1152]{1,0:T(8,128)(2,1)S(1)}, bf16[336,1152]{1,0:T(8,128)(2,1)}, f32[1,1152]{1,0:T(1,128)S(1)}) custom-call(bf16[336,1152]{1,0:T(8,128)(2,1)} %collective-permute-done.31.refs_0_.refs_1_, f32[336,1152]{1,0:T(8,128)} %get-tuple-element.122.refs_1_, ...), custom_call_target="tpu_custom_call" | custom-call | flops 2675441664 | bytes 8918138 | tf_op jit(solution)/shard_map/pallas_call | solution.py:473
  196.3 4.7 shard_map.498.refs_2_
  202.1 7.9 %shard_map.497 = (bf16[336,1152]{1,0:T(8,128)(2,1)S(1)}, bf16[336,1152]{1,0:T(8,128)(2,1)S(1)}, bf16[336,1152]{1,0:T(8,128)(2,1)}, f32[1,1152]{1,0:T(1,128)S(1)}) custom-call(bf16[336,1152]{1,0:T(8,128)(2,1)} %collective-permute-done.32.refs_0_.refs_2_, f32[336,1152]{1,0:T(8,128)} %get-tuple-element.123.refs_1_, ...), custom_call_target="tpu_custom_call" | custom-call | flops 2675441664 | bytes 8918138 | tf_op jit(solution)/shard_map/pallas_call | solution.py:473
  211.8 7.2 %shard_map.499 = (bf16[336,1152]{1,0:T(8,128)(2,1)S(1)}, bf16[336,1152]{1,0:T(8,128)(2,1)}, bf16[336,1152]{1,0:T(8,128)(2,1)}, f32[1,1152]{1,0:T(1,128)S(1)}) custom-call(bf16[160,1152]{1,0:T(8,128)(2,1)S(1)} %collective-permute-done.33.refs_0_.refs_3_, bf16[176,1152]{1,0:T(8,128)(2,1)S(1)} %collective-permute-done.34.refs_1_.refs_4_, ...), custom_call_target="tpu_custom_call" | custom-call | flops 2675441664 | bytes 8918138 | tf_op jit(solution)/shard_map/pallas_call | solution.py:473
  221.4 18.7 %shard_map.500.refs_5_ = bf16[8,288,1152]{2,1,0:T(8,128)(2,1)} custom-call(bf16[336,1152]{1,0:T(8,128)(2,1)} %get-tuple-element.132.refs_0_, bf16[336,1152]{1,0:T(8,128)(2,1)} %collective-permute-done.31.refs_0_.refs_1_, bf16[336,1152]{1,0:T(8,128)(2,1)} %collective-permute-done.32.refs_0_.refs_2_, ...), custom_call_target="tpu_custom_call" | custom-call | flops 7134511104 | bytes 23781704 | tf_op jit(solution)/shard_map/pallas_call | solution.py:473
  240.1 8.2 %shard_map.501 = (bf16[336,1152]{1,0:T(8,128)(2,1)S(1)}, bf16[336,1152]{1,0:T(8,128)(2,1)}, bf16[336,1152]{1,0:T(8,128)(2,1)}, bf16[336,1152]{1,0:T(8,128)(2,1)}) custom-call(bf16[336,1152]{1,0:T(8,128)(2,1)} %copy-done.19, bf16[336,1152]{1,0:T(8,128)(2,1)} %copy-done.20, bf16[336,1152]{1,0:T(8,128)(2,1)} %copy-done.21, bf16[336,1152]{1,0:T(8,128)(2,1)} %copy-done.22, ...), custom_call_target="tpu_custom_call" | custom-call | flops 3567255552 | bytes 11890851 | tf_op jit(solution)/shard_map/pallas_call | solution.py:473
  252.9 24.8 %shard_map.502 = (bf16[4,336,288]{2,1,0:T(8,128)(2,1)}, f32[336,1152]{1,0:T(8,128)}, bf16[4,336,864]{2,1,0:T(8,128)(2,1)}, f32[8,1152]{1,0:T(8,128)S(1)}) custom-call(s32[3]{0:T(128)S(1)} %pad_add_fusion.refs_0_, s32[1]{0:T(128)S(6)} %copy.81.refs_1_, bf16[336,1152]{1,0:T(8,128)(2,1)} %bitcast.76, f32[336,1152]{1,0:T(8,128)} %get-tuple-element.131.refs_3_, ...), custom_call_target="tpu_custom_call" | custom-call | flops 3567255552 | bytes 11890851 | tf_op jit(solution)/shard_map/pallas_call | solution.py:473
  277.7 5.8 %collective-permute-done.39.refs_6_ = bf16[336,1152]{1,0:T(8,128)(2,1)} collective-permute-done((bf16[336,1152]{1,0:T(8,128)(2,1)}, bf16[336,1152]{1,0:T(8,128)(2,1)}, u32[]{:S(2)}, u32[]{:S(2)}) %collective-permute-start.39) | collective-permute-done | bytes 774176 | tf_op jit(solution)/shard_map/ppermute | solution.py:48
  283.6 11.1 %shard_map.503 = (bf16[4,144,1152]{2,1,0:T(8,128)(2,1)}, bf16[4,144,1152]{2,1,0:T(8,128)(2,1)}, bf16[4,144,1152]{2,1,0:T(8,128)(2,1)}, bf16[4,144,1152]{2,1,0:T(...) custom-call(s32[3]{0:T(128)S(1)} %pad_add_fusion.refs_0_, ...), custom_call_target="tpu_custom_call" | custom-call | flops 3567255552 | bytes 11890851 | tf_op jit(solution)/shard_map/pallas_call | solution.py:473
  295.2 2.8 collective-permute-done.41
  302.4 12.3 %shard_map.504 = (bf16[4,336,288]{2,1,0:T(8,128)(2,1)}, f32[8,1152]{1,0:T(8,128)S(1)}) custom-call(s32[3]{0:T(128)S(1)} %pad_add_fusion.refs_0_, bf16[4,336,864]{2,1,0:T(8,128)(2,1)} %get-tuple-element.157.refs_3_.refs_1_, f32[336,1152]{1,0:T(8,128)} %get-tuple-element.118.refs_2_, f32[11,1152]{1,0:T(8,128)S(1)} %copy-done.8, ...), custom_call_target="tpu_custom_call" | custom-call | flops 2675441664 | bytes 8918138 | tf_op jit(solution)/shard_map/pallas_call | solution.py:473
  322.9 7.3 %shard_map.505 = (bf16[4,288,288]{2,1,0:T(8,128)(2,1)}, bf16[4,288,288]{2,1,0:T(8,128)(2,1)}, bf16[4,288,288]{2,1,0:T(8,128)(2,1)}, bf16[4,288,288]{2,1,0:T(8,12...) custom-call(s32[3]{0:T(128)S(1)} %pad_add_fusion.refs_0_, ...), custom_call_target="tpu_custom_call" | custom-call | flops 1783627776 | bytes 5945425 | tf_op jit(solution)/shard_map/pallas_call | solution.py:473
  334.4 2.9 collective-permute-done.54
  337.2 2.5 collective-permute-start.55
  341.6 7.8 %collective-permute-done.48 = bf16[4,144,1152]{2,1,0:T(8,128)(2,1)S(1)} collective-permute-done((bf16[4,144,1152]{2,1,0:T(8,128)(2,1)}, bf16[4,144,1152]{2,1,0:T(8,128)(2,1)S(1)}, u32[]{:S(2)}, u32[]{:S(2)}) %collective-permute-start.48) | collective-permute-done | bytes 1327136 | tf_op jit(solution)/shard_map/ppermute | solution.py:48
  349.4 2.5 collective-permute-done.49
  355.7 6.4 %collective-permute-done.50 = bf16[2,288,288]{2,1,0:T(8,128)(2,1)S(1)} collective-permute-done((bf16[2,288,288]{2,1,0:T(8,128)(2,1)S(1)}, bf16[2,288,288]{2,1,0:T(8,128)(2,1)S(1)}, u32[]{:S(2)}, u32[]{:S(2)}) %collective-permute-start.50) | collective-permute-done | bytes 331808 | tf_op jit(solution)/shard_map/ppermute | solution.py:48
  362.8 2.5 collective-permute-start.62
  368.9 3.3 add_bitcast_fusion
  372.2 14.6 %collective-permute-done.58 = bf16[4,288,288]{2,1,0:T(8,128)(2,1)S(1)} collective-permute-done((bf16[4,288,288]{2,1,0:T(8,128)(2,1)S(1)}, bf16[4,288,288]{2,1,0:T(8,128)(2,1)S(1)}, u32[]{:S(2)}, u32[]{:S(2)}) %collective-permute-start.58) | collective-permute-done | bytes 663584 | tf_op jit(solution)/shard_map/ppermute | solution.py:48
  390.6 9.4 %shard_map.506 = (f32[336,1152]{1,0:T(8,128)}, f32[336,1152]{1,0:T(8,128)}) custom-call(s32[3]{0:T(128)S(1)} %pad_add_fusion.refs_0_, bf16[4,336,288]{2,1,0:T(8,128)(2,1)} %get-tuple-element.162.refs_3_.refs_1_, bf16[4,288,384]{2,1,0:T(8,128)(2,1)} %copy-done.26, bf16[4,288,384]{2,1,0:T(8,128)(2,1)} %collective-permute-done.8.refs_4_.refs_3_, ...), custom_call_target="tpu_custom_call" | custom-call | flops 1783627776 | bytes 5945425 | tf_op jit(solution)/shard_map/pallas_call | solution.py:473
  407.3 13.6 %collective-permute-done.67 = bf16[2,288,288]{2,1,0:T(8,128)(2,1)S(1)} collective-permute-done((bf16[2,288,288]{2,1,0:T(8,128)(2,1)}, bf16[2,288,288]{2,1,0:T(8,128)(2,1)S(1)}, u32[]{:S(2)}, u32[]{:S(2)}) %collective-permute-start.67) | collective-permute-done | bytes 331808 | tf_op jit(solution)/shard_map/ppermute | solution.py:51
  432.6 2.4 collective-permute-done.65
  437.4 2.1 multiply_reduce_fusion
  447.7 3.2 collective-permute-start.70
  452.1 4.6 collective-permute-start.71
  457.6 2.5 collective-permute-start.72
  462.0 2.4 collective-permute-start.73
  467.0 3.3 multiply_add_fusion.6
  475.0 2.1 multiply_add_fusion.3
  (383 shorter events, 125.4 us)
Async XLA Ops:
  7.2 113.6 %all-gather.3.cloned.1.call-start = ((), (), s32[]{:S(2)}) async-start(), calls=%async_computation.1 | async-start | bytes 2985984 | tf_op jit(solution)/shard_map/all_gather | solution.py:550
  20.2 18.0 %collective-permute-start.1 = (bf16[288,384]{1,0:T(8,128)(2,1)S(1)}, bf16[288,384]{1,0:T(8,128)(2,1)S(1)}, u32[]{:S(2)}, u32[]{:S(2)}) collective-permute-start(bf16[288,384]{1,0:T(8,128)(2,1)S(1)} %fusion.7), channel_id=1, source_target_pairs={{0,16},{4,20},{8,24},{12,28},{16,0},{20,4},{24,8},{28,12},{1,17},{... | collective-permute-start | bytes 663560 | tf_op jit(solution)/shard_map/ppermute | solution.py:51
  21.0 17.1 %collective-permute-start = (bf16[288,384]{1,0:T(8,128)(2,1)S(1)}, bf16[288,384]{1,0:T(8,128)(2,1)S(1)}, u32[]{:S(2)}, u32[]{:S(2)}) collective-permute-start(bf16[288,384]{1,0:T(8,128)(2,1)S(1)} %fusion.7), channel_id=1, source_target_pairs={{0,8},{4,12},{8,0},{12,4},{16,24},{20,28},{24,16},{28,20},{1,9},{5... | collective-permute-start | bytes 663560 | tf_op jit(solution)/shard_map/ppermute | solution.py:51
  24.1 19.2 %collective-permute-start.3 = (bf16[336,1152]{1,0:T(8,128)(2,1)S(1)}, bf16[336,1152]{1,0:T(8,128)(2,1)S(1)}, u32[]{:S(2)}, u32[]{:S(2)}) collective-permute-start(bf16[336,1152]{1,0:T(8,128)(2,1)S(1)} %bitcast.77), channel_id=1, source_target_pairs={{0,1},{1,0},{2,3},{3,2},{4,5},{5,4},{6,7},{7,6},{8,9},{9,8},{10,11... | collective-permute-start | bytes 2322440 | tf_op jit(solution)/shard_map/ppermute | solution.py:48
  25.8 18.9 %collective-permute-start.4 = (bf16[336,1152]{1,0:T(8,128)(2,1)S(1)}, bf16[336,1152]{1,0:T(8,128)(2,1)S(1)}, u32[]{:S(2)}, u32[]{:S(2)}) collective-permute-start(bf16[336,1152]{1,0:T(8,128)(2,1)S(1)} %bitcast.78), channel_id=1, source_target_pairs={{0,2},{1,3},{2,0},{3,1},{4,6},{5,7},{6,4},{7,5},{8,10},{9,11},{10,... | collective-permute-start | bytes 2322440 | tf_op jit(solution)/shard_map/ppermute | solution.py:48
  44.7 20.5 %collective-permute-start.9 = (bf16[4,288,384]{2,1,0:T(8,128)(2,1)S(1)}, bf16[4,288,384]{2,1,0:T(8,128)(2,1)}, u32[]{:S(2)}, u32[]{:S(2)}) collective-permute-start(bf16[4,288,384]{2,1,0:T(8,128)(2,1)S(1)} %pad_maximum_fusion.3.refs_3_.refs_2_), channel_id=1, source_target_pairs={{0,2},{1,3},{2,0},{3,1},{4,6},{5,7},{6,4},{7,5},{8,10},{9,11},{10,... | collective-permute-start | bytes 2654216 | tf_op jit(solution)/shard_map/ppermute | solution.py:48
  45.1 21.9 %collective-permute-start.8 = (bf16[4,288,384]{2,1,0:T(8,128)(2,1)S(1)}, bf16[4,288,384]{2,1,0:T(8,128)(2,1)}, u32[]{:S(2)}, u32[]{:S(2)}) collective-permute-start(bf16[4,288,384]{2,1,0:T(8,128)(2,1)S(1)} %pad_maximum_fusion.3.refs_3_.refs_2_), channel_id=1, source_target_pairs={{0,1},{1,0},{2,3},{3,2},{4,5},{5,4},{6,7},{7,6},{8,9},{9,8},{10,11... | collective-permute-start | bytes 2654216 | tf_op jit(solution)/shard_map/ppermute | solution.py:48
  46.9 23.8 %collective-permute-start.19 = (bf16[144,1152]{1,0:T(8,128)(2,1)S(1)}, bf16[144,1152]{1,0:T(8,128)(2,1)S(1)}, u32[]{:S(2)}, u32[]{:S(2)}) collective-permute-start(bf16[144,1152]{1,0:T(8,128)(2,1)S(1)} %pad_maximum_fusion.6), channel_id=1, source_target_pairs={{0,24},{4,28},{8,16},{12,20},{16,8},{20,12},{24,0},{28,4},{1,25},{... | collective-permute-start | bytes 995336 | tf_op jit(solution)/shard_map/ppermute | solution.py:51
  50.6 26.8 %collective-permute-start.18 = (bf16[144,1152]{1,0:T(8,128)(2,1)S(1)}, bf16[144,1152]{1,0:T(8,128)(2,1)}, u32[]{:S(2)}, u32[]{:S(2)}) collective-permute-start(bf16[144,1152]{1,0:T(8,128)(2,1)S(1)} %pad_maximum_fusion.6), channel_id=1, source_target_pairs={{0,16},{4,20},{8,24},{12,28},{16,0},{20,4},{24,8},{28,12},{1,17},{... | collective-permute-start | bytes 995336 | tf_op jit(solution)/shard_map/ppermute | solution.py:51
  50.6 26.8 %collective-permute-start.17 = (bf16[144,1152]{1,0:T(8,128)(2,1)S(1)}, bf16[144,1152]{1,0:T(8,128)(2,1)}, u32[]{:S(2)}, u32[]{:S(2)}) collective-permute-start(bf16[144,1152]{1,0:T(8,128)(2,1)S(1)} %pad_maximum_fusion.6), channel_id=1, source_target_pairs={{0,8},{4,12},{8,0},{12,4},{16,24},{20,28},{24,16},{28,20},{1,9},{5... | collective-permute-start | bytes 995336 | tf_op jit(solution)/shard_map/ppermute | solution.py:51
  66.3 11.1 %collective-permute-start.10 = (bf16[2,288,384]{2,1,0:T(8,128)(2,1)S(1)}, bf16[2,288,384]{2,1,0:T(8,128)(2,1)S(1)}, u32[]{:S(2)}, u32[]{:S(2)}) collective-permute-start(bf16[2,288,384]{2,1,0:T(8,128)(2,1)S(1)} %slice.325), channel_id=1, source_target_pairs={{0,1},{1,0},{2,3},{3,2},{4,5},{5,4},{6,7},{7,6},{8,9},{9,8},{10,11... | collective-permute-start | bytes 1327112 | tf_op jit(solution)/shard_map/ppermute | solution.py:48
  78.2 89.6 %all-gather.5.cloned.1.call-start = ((), (), s32[]{:S(2)}) async-start(), calls=%async_computation.2 | async-start | bytes 2985984 | tf_op jit(solution)/shard_map/all_gather | solution.py:551
  79.3 343.5 %reduce-scatter.2.cloned.1.call-start = ((), (), s32[]{:S(2)}) async-start(), calls=%async_computation.3 | async-start | bytes 5971968 | tf_op jit(solution)/shard_map/reduce_scatter | solution.py:659
  82.8 31.4 %collective-permute-start.21 = (bf16[4,144,1152]{2,1,0:T(8,128)(2,1)}, bf16[4,144,1152]{2,1,0:T(8,128)(2,1)}, u32[]{:S(2)}, u32[]{:S(2)}) collective-permute-start(bf16[4,144,1152]{2,1,0:T(8,128)(2,1)} %pad_maximum_fusion.refs_3_.refs_4_.refs_11_.refs_5_), channel_id=1, source_target_pairs={{0,2},{1,3},{2,0},{3,1},{4,6},{5,7},{6,4},{7,5},{8,10},{9,11},{10,... | collective-permute-start | bytes 3981320 | tf_op jit(solution)/shard_map/ppermute | solution.py:48
  83.9 33.4 %collective-permute-start.20 = (bf16[4,144,1152]{2,1,0:T(8,128)(2,1)}, bf16[4,144,1152]{2,1,0:T(8,128)(2,1)}, u32[]{:S(2)}, u32[]{:S(2)}) collective-permute-start(bf16[4,144,1152]{2,1,0:T(8,128)(2,1)} %pad_maximum_fusion.refs_3_.refs_4_.refs_11_.refs_5_), channel_id=1, source_target_pairs={{0,1},{1,0},{2,3},{3,2},{4,5},{5,4},{6,7},{7,6},{8,9},{9,8},{10,11... | collective-permute-start | bytes 3981320 | tf_op jit(solution)/shard_map/ppermute | solution.py:48
  116.2 16.3 %collective-permute-start.22 = (bf16[2,144,1152]{2,1,0:T(8,128)(2,1)}, bf16[2,144,1152]{2,1,0:T(8,128)(2,1)S(1)}, u32[]{:S(2)}, u32[]{:S(2)}) collective-permute-start(bf16[2,144,1152]{2,1,0:T(8,128)(2,1)} %slice.327), channel_id=1, source_target_pairs={{0,1},{1,0},{2,3},{3,2},{4,5},{5,4},{6,7},{7,6},{8,9},{9,8},{10,11... | collective-permute-start | bytes 1990664 | tf_op jit(solution)/shard_map/ppermute | solution.py:48
  119.3 16.0 %collective-permute-start.23 = (bf16[2,144,1152]{2,1,0:T(8,128)(2,1)}, bf16[2,144,1152]{2,1,0:T(8,128)(2,1)S(1)}, u32[]{:S(2)}, u32[]{:S(2)}) collective-permute-start(bf16[2,144,1152]{2,1,0:T(8,128)(2,1)} %slice.332), channel_id=1, source_target_pairs={{0,2},{1,3},{2,0},{3,1},{4,6},{5,7},{6,4},{7,5},{8,10},{9,11},{10,... | collective-permute-start | bytes 1990664 | tf_op jit(solution)/shard_map/ppermute | solution.py:48
  120.3 20.2 %collective-permute-start.24 = (bf16[4,144,1152]{2,1,0:T(8,128)(2,1)}, bf16[4,144,1152]{2,1,0:T(8,128)(2,1)}, u32[]{:S(2)}, u32[]{:S(2)}) collective-permute-start(bf16[4,144,1152]{2,1,0:T(8,128)(2,1)} %pad_maximum_fusion.refs_3_.refs_4_.refs_11_.refs_5_), channel_id=1, source_target_pairs={{0,4},{4,0},{8,12},{12,8},{16,20},{20,16},{24,28},{28,24},{1,5},{5... | collective-permute-start | bytes 3981320 | tf_op jit(solution)/shard_map/ppermute | solution.py:54
  120.3 20.2 %collective-permute-start.25 = (bf16[4,144,1152]{2,1,0:T(8,128)(2,1)}, bf16[4,144,1152]{2,1,0:T(8,128)(2,1)}, u32[]{:S(2)}, u32[]{:S(2)}) collective-permute-start(bf16[4,144,1152]{2,1,0:T(8,128)(2,1)} %collective-permute-done.20.refs_4_.refs_5_.refs_12_.refs_6_), channel_id=1, source_target_pairs={{0,4},{4,0},{8,12},{12,8},{16,20},{20,16},{24,28},{28,24},{1,5},{5... | collective-permute-start | bytes 3981320 | tf_op jit(solution)/shard_map/ppermute | solution.py:54
  120.8 19.7 %collective-permute-start.26 = (bf16[4,144,1152]{2,1,0:T(8,128)(2,1)}, bf16[4,144,1152]{2,1,0:T(8,128)(2,1)}, u32[]{:S(2)}, u32[]{:S(2)}) collective-permute-start(bf16[4,144,1152]{2,1,0:T(8,128)(2,1)} %collective-permute-done.21.refs_5_.refs_6_.refs_13_.refs_7_), channel_id=1, source_target_pairs={{0,4},{4,0},{8,12},{12,8},{16,20},{20,16},{24,28},{28,24},{1,5},{5... | collective-permute-start | bytes 3981320 | tf_op jit(solution)/shard_map/ppermute | solution.py:54
  138.4 17.5 %collective-permute-start.29 = (bf16[160,1152]{1,0:T(8,128)(2,1)S(1)}, bf16[160,1152]{1,0:T(8,128)(2,1)S(1)}, u32[]{:S(2)}, u32[]{:S(2)}) collective-permute-start(bf16[160,1152]{1,0:T(8,128)(2,1)S(1)} %slice.333), channel_id=1, source_target_pairs={{0,1},{1,0},{2,3},{3,2},{4,5},{5,4},{6,7},{7,6},{8,9},{9,8},{10,11... | collective-permute-start | bytes 1105928 | tf_op jit(solution)/shard_map/ppermute | solution.py:48
  139.4 16.5 %collective-permute-start.30 = (bf16[176,1152]{1,0:T(8,128)(2,1)S(1)}, bf16[176,1152]{1,0:T(8,128)(2,1)S(1)}, u32[]{:S(2)}, u32[]{:S(2)}) collective-permute-start(bf16[176,1152]{1,0:T(8,128)(2,1)S(1)} %slice.334), channel_id=1, source_target_pairs={{0,2},{1,3},{2,0},{3,1},{4,6},{5,7},{6,4},{7,5},{8,10},{9,11},{10,... | collective-permute-start | bytes 1216520 | tf_op jit(solution)/shard_map/ppermute | solution.py:48
  165.6 19.1 %collective-permute-start.31 = (bf16[336,1152]{1,0:T(8,128)(2,1)}, bf16[336,1152]{1,0:T(8,128)(2,1)}, u32[]{:S(2)}, u32[]{:S(2)}) collective-permute-start(bf16[336,1152]{1,0:T(8,128)(2,1)} %get-tuple-element.132.refs_0_), channel_id=1, source_target_pairs={{0,1},{1,0},{2,3},{3,2},{4,5},{5,4},{6,7},{7,6},{8,9},{9,8},{10,11... | collective-permute-start | bytes 2322440 | tf_op jit(solution)/shard_map/ppermute | solution.py:48
  166.6 27.6 %collective-permute-start.32 = (bf16[336,1152]{1,0:T(8,128)(2,1)}, bf16[336,1152]{1,0:T(8,128)(2,1)}, u32[]{:S(2)}, u32[]{:S(2)}) collective-permute-start(bf16[336,1152]{1,0:T(8,128)(2,1)} %get-tuple-element.132.refs_0_), channel_id=1, source_target_pairs={{0,2},{1,3},{2,0},{3,1},{4,6},{5,7},{6,4},{7,5},{8,10},{9,11},{10,... | collective-permute-start | bytes 2322440 | tf_op jit(solution)/shard_map/ppermute | solution.py:48
  193.2 18.6 %collective-permute-start.34 = (bf16[176,1152]{1,0:T(8,128)(2,1)S(1)}, bf16[176,1152]{1,0:T(8,128)(2,1)S(1)}, u32[]{:S(2)}, u32[]{:S(2)}) collective-permute-start(bf16[176,1152]{1,0:T(8,128)(2,1)S(1)} %slice.339), channel_id=1, source_target_pairs={{0,2},{1,3},{2,0},{3,1},{4,6},{5,7},{6,4},{7,5},{8,10},{9,11},{10,... | collective-permute-start | bytes 1216520 | tf_op jit(solution)/shard_map/ppermute | solution.py:48
  195.3 16.5 %collective-permute-start.33 = (bf16[160,1152]{1,0:T(8,128)(2,1)S(1)}, bf16[160,1152]{1,0:T(8,128)(2,1)S(1)}, u32[]{:S(2)}, u32[]{:S(2)}) collective-permute-start(bf16[160,1152]{1,0:T(8,128)(2,1)S(1)} %slice.338), channel_id=1, source_target_pairs={{0,1},{1,0},{2,3},{3,2},{4,5},{5,4},{6,7},{7,6},{8,9},{9,8},{10,11... | collective-permute-start | bytes 1105928 | tf_op jit(solution)/shard_map/ppermute | solution.py:48
  201.0 48.2 %collective-permute-start.35 = (bf16[336,1152]{1,0:T(8,128)(2,1)}, bf16[336,1152]{1,0:T(8,128)(2,1)}, u32[]{:S(2)}, u32[]{:S(2)}) collective-permute-start(bf16[336,1152]{1,0:T(8,128)(2,1)} %get-tuple-element.146), channel_id=1, source_target_pairs={{0,1},{1,0},{2,3},{3,2},{4,5},{5,4},{6,7},{7,6},{8,9},{9,8},{10,11... | collective-permute-start | bytes 2322440 | tf_op jit(solution)/shard_map/ppermute | solution.py:48
  210.8 38.4 %collective-permute-start.36 = (bf16[336,1152]{1,0:T(8,128)(2,1)}, bf16[336,1152]{1,0:T(8,128)(2,1)}, u32[]{:S(2)}, u32[]{:S(2)}) collective-permute-start(bf16[336,1152]{1,0:T(8,128)(2,1)} %get-tuple-element.147), channel_id=1, source_target_pairs={{0,2},{1,3},{2,0},{3,1},{4,6},{5,7},{6,4},{7,5},{8,10},{9,11},{10,... | collective-permute-start | bytes 2322440 | tf_op jit(solution)/shard_map/ppermute | solution.py:48
  219.9 29.3 %collective-permute-start.37 = (bf16[336,1152]{1,0:T(8,128)(2,1)}, bf16[336,1152]{1,0:T(8,128)(2,1)}, u32[]{:S(2)}, u32[]{:S(2)}) collective-permute-start(bf16[336,1152]{1,0:T(8,128)(2,1)} %get-tuple-element.148), channel_id=1, source_target_pairs={{0,3},{1,2},{2,1},{3,0},{4,7},{5,6},{6,5},{7,4},{8,11},{9,10},{10,... | collective-permute-start | bytes 2322440 | tf_op jit(solution)/shard_map/ppermute | solution.py:48
  249.2 28.5 %collective-permute-start.40 = (bf16[336,1152]{1,0:T(8,128)(2,1)}, bf16[336,1152]{1,0:T(8,128)(2,1)}, u32[]{:S(2)}, u32[]{:S(2)}) collective-permute-start(bf16[336,1152]{1,0:T(8,128)(2,1)} %get-tuple-element.153), channel_id=1, source_target_pairs={{0,3},{1,2},{2,1},{3,0},{4,7},{5,6},{6,5},{7,4},{8,11},{9,10},{10,... | collective-permute-start | bytes 2322440 | tf_op jit(solution)/shard_map/ppermute | solution.py:48
  250.8 32.8 %collective-permute-start.39 = (bf16[336,1152]{1,0:T(8,128)(2,1)}, bf16[336,1152]{1,0:T(8,128)(2,1)}, u32[]{:S(2)}, u32[]{:S(2)}) collective-permute-start(bf16[336,1152]{1,0:T(8,128)(2,1)} %get-tuple-element.151), channel_id=1, source_target_pairs={{0,2},{1,3},{2,0},{3,1},{4,6},{5,7},{6,4},{7,5},{8,10},{9,11},{10,... | collective-permute-start | bytes 2322440 | tf_op jit(solution)/shard_map/ppermute | solution.py:48
  251.8 31.8 %collective-permute-start.38 = (bf16[336,1152]{1,0:T(8,128)(2,1)}, bf16[336,1152]{1,0:T(8,128)(2,1)}, u32[]{:S(2)}, u32[]{:S(2)}) collective-permute-start(bf16[336,1152]{1,0:T(8,128)(2,1)} %get-tuple-element.149), channel_id=1, source_target_pairs={{0,1},{1,0},{2,3},{3,2},{4,5},{5,4},{6,7},{7,6},{8,9},{9,8},{10,11... | collective-permute-start | bytes 2322440 | tf_op jit(solution)/shard_map/ppermute | solution.py:48
  294.8 22.8 %collective-permute-start.42 = (bf16[4,144,1152]{2,1,0:T(8,128)(2,1)}, bf16[4,144,1152]{2,1,0:T(8,128)(2,1)S(1)}, u32[]{:S(2)}, u32[]{:S(2)}) collective-permute-start(bf16[4,144,1152]{2,1,0:T(8,128)(2,1)} %get-tuple-element.164), channel_id=1, source_target_pairs={{0,4},{4,0},{8,12},{12,8},{16,20},{20,16},{24,28},{28,24},{1,5},{5... | collective-permute-start | bytes 3981320 | tf_op jit(solution)/shard_map/ppermute | solution.py:54
  299.8 17.0 %collective-permute-start.43 = (bf16[2,144,1152]{2,1,0:T(8,128)(2,1)S(1)}, bf16[2,144,1152]{2,1,0:T(8,128)(2,1)S(1)}, u32[]{:S(2)}, u32[]{:S(2)}) collective-permute-start(bf16[2,144,1152]{2,1,0:T(8,128)(2,1)S(1)} %get-tuple-element.240.refs_15_), channel_id=1, source_target_pairs={{0,1},{1,0},{2,3},{3,2},{4,5},{5,4},{6,7},{7,6},{8,9},{9,8},{10,11... | collective-permute-start | bytes 1990664 | tf_op jit(solution)/shard_map/ppermute | solution.py:48
  300.9 16.6 %collective-permute-start.44 = (bf16[2,144,1152]{2,1,0:T(8,128)(2,1)S(1)}, bf16[2,144,1152]{2,1,0:T(8,128)(2,1)S(1)}, u32[]{:S(2)}, u32[]{:S(2)}) collective-permute-start(bf16[2,144,1152]{2,1,0:T(8,128)(2,1)S(1)} %get-tuple-element.239.refs_16_), channel_id=1, source_target_pairs={{0,2},{1,3},{2,0},{3,1},{4,6},{5,7},{6,4},{7,5},{8,10},{9,11},{10,... | collective-permute-start | bytes 1990664 | tf_op jit(solution)/shard_map/ppermute | solution.py:48
  301.9 18.3 %collective-permute-start.45 = (bf16[4,144,1152]{2,1,0:T(8,128)(2,1)S(1)}, bf16[4,144,1152]{2,1,0:T(8,128)(2,1)S(1)}, u32[]{:S(2)}, u32[]{:S(2)}) collective-permute-start(bf16[4,144,1152]{2,1,0:T(8,128)(2,1)S(1)} %copy-done.74), channel_id=1, source_target_pairs={{0,4},{4,0},{8,12},{12,8},{16,20},{20,16},{24,28},{28,24},{1,5},{5... | collective-permute-start | bytes 3981320 | tf_op jit(solution)/shard_map/ppermute | solution.py:54
  301.9 51.0 %collective-permute-start.61 = (bf16[4,144,1152]{2,1,0:T(8,128)(2,1)}, bf16[4,144,1152]{2,1,0:T(8,128)(2,1)}, u32[]{:S(2)}, u32[]{:S(2)}) collective-permute-start(bf16[4,144,1152]{2,1,0:T(8,128)(2,1)} %get-tuple-element.191), channel_id=1, source_target_pairs={{0,4},{4,0},{8,12},{12,8},{16,20},{20,16},{24,28},{28,24},{1,5},{5... | collective-permute-start | bytes 3981320 | tf_op jit(solution)/shard_map/ppermute | solution.py:54
  319.2 30.2 %collective-permute-start.48 = (bf16[4,144,1152]{2,1,0:T(8,128)(2,1)}, bf16[4,144,1152]{2,1,0:T(8,128)(2,1)S(1)}, u32[]{:S(2)}, u32[]{:S(2)}) collective-permute-start(bf16[4,144,1152]{2,1,0:T(8,128)(2,1)} %pad_maximum_fusion.1.refs_4_), channel_id=1, source_target_pairs={{0,1},{1,0},{2,3},{3,2},{4,5},{5,4},{6,7},{7,6},{8,9},{9,8},{10,11... | collective-permute-start | bytes 3981320 | tf_op jit(solution)/shard_map/ppermute | solution.py:48
  321.8 30.1 %collective-permute-start.49 = (bf16[4,144,1152]{2,1,0:T(8,128)(2,1)}, bf16[4,144,1152]{2,1,0:T(8,128)(2,1)}, u32[]{:S(2)}, u32[]{:S(2)}) collective-permute-start(bf16[4,144,1152]{2,1,0:T(8,128)(2,1)} %pad_maximum_fusion.2.refs_5_), channel_id=1, source_target_pairs={{0,2},{1,3},{2,0},{3,1},{4,6},{5,7},{6,4},{7,5},{8,10},{9,11},{10,... | collective-permute-start | bytes 3981320 | tf_op jit(solution)/shard_map/ppermute | solution.py:48
  337.2 34.9 %collective-permute-start.55 = (f32[11,1152]{1,0:T(8,128)S(1)}, f32[11,1152]{1,0:T(8,128)S(1)}, u32[]{:S(2)}, u32[]{:S(2)}) collective-permute-start(f32[11,1152]{1,0:T(8,128)S(1)} %add.340), channel_id=1, source_target_pairs={{0,16},{4,20},{8,24},{12,28},{16,0},{20,4},{24,8},{28,12},{1,17},{... | collective-permute-start | bytes 152072 | tf_op jit(solution)/shard_map/ppermute | solution.py:51
  339.8 25.5 %collective-permute-start.52 = (bf16[4,288,288]{2,1,0:T(8,128)(2,1)}, bf16[4,288,288]{2,1,0:T(8,128)(2,1)S(1)}, u32[]{:S(2)}, u32[]{:S(2)}) collective-permute-start(bf16[4,288,288]{2,1,0:T(8,128)(2,1)} %get-tuple-element.177), channel_id=1, source_target_pairs={{0,4},{4,0},{8,12},{12,8},{16,20},{20,16},{24,28},{28,24},{1,5},{5... | collective-permute-start | bytes 1990664 | tf_op jit(solution)/shard_map/ppermute | solution.py:54
  349.4 17.4 %collective-permute-start.46 = (bf16[4,288,288]{2,1,0:T(8,128)(2,1)S(1)}, bf16[4,288,288]{2,1,0:T(8,128)(2,1)S(1)}, u32[]{:S(2)}, u32[]{:S(2)}) collective-permute-start(bf16[4,288,288]{2,1,0:T(8,128)(2,1)S(1)} %copy-done.76), channel_id=1, source_target_pairs={{0,4},{4,0},{8,12},{12,8},{16,20},{20,16},{24,28},{28,24},{1,5},{5... | collective-permute-start | bytes 1990664 | tf_op jit(solution)/shard_map/ppermute | solution.py:54
  362.8 38.9 %collective-permute-start.62 = (bf16[2,144,1152]{2,1,0:T(8,128)(2,1)S(1)}, bf16[2,144,1152]{2,1,0:T(8,128)(2,1)S(1)}, u32[]{:S(2)}, u32[]{:S(2)}) collective-permute-start(bf16[2,144,1152]{2,1,0:T(8,128)(2,1)S(1)} %add_convert_fusion.2), channel_id=1, source_target_pairs={{0,16},{4,20},{8,24},{12,28},{16,0},{20,4},{24,8},{28,12},{1,17},{... | collective-permute-start | bytes 1990664 | tf_op jit(solution)/shard_map/ppermute | solution.py:51
  365.7 21.1 %collective-permute-start.58 = (bf16[4,288,288]{2,1,0:T(8,128)(2,1)S(1)}, bf16[4,288,288]{2,1,0:T(8,128)(2,1)S(1)}, u32[]{:S(2)}, u32[]{:S(2)}) collective-permute-start(bf16[4,288,288]{2,1,0:T(8,128)(2,1)S(1)} %pad_maximum_fusion.5.refs_13_), channel_id=1, source_target_pairs={{0,2},{1,3},{2,0},{3,1},{4,6},{5,7},{6,4},{7,5},{8,10},{9,11},{10,... | collective-permute-start | bytes 1990664 | tf_op jit(solution)/shard_map/ppermute | solution.py:48
  367.4 21.1 %collective-permute-start.57 = (bf16[4,288,288]{2,1,0:T(8,128)(2,1)S(1)}, bf16[4,288,288]{2,1,0:T(8,128)(2,1)S(1)}, u32[]{:S(2)}, u32[]{:S(2)}) collective-permute-start(bf16[4,288,288]{2,1,0:T(8,128)(2,1)S(1)} %pad_maximum_fusion.4.refs_12_), channel_id=1, source_target_pairs={{0,1},{1,0},{2,3},{3,2},{4,5},{5,4},{6,7},{7,6},{8,9},{9,8},{10,11... | collective-permute-start | bytes 1990664 | tf_op jit(solution)/shard_map/ppermute | solution.py:48
  389.5 11.0 %collective-permute-start.59 = (f32[11,1152]{1,0:T(8,128)S(1)}, f32[11,1152]{1,0:T(8,128)S(1)}, u32[]{:S(2)}, u32[]{:S(2)}) collective-permute-start(f32[11,1152]{1,0:T(8,128)S(1)} %add.341), channel_id=1, source_target_pairs={{0,1},{1,0},{2,3},{3,2},{4,5},{5,4},{6,7},{7,6},{8,9},{9,8},{10,11... | collective-permute-start | bytes 152072 | tf_op jit(solution)/shard_map/ppermute | solution.py:48
  400.0 20.9 %collective-permute-start.67 = (bf16[2,288,288]{2,1,0:T(8,128)(2,1)}, bf16[2,288,288]{2,1,0:T(8,128)(2,1)S(1)}, u32[]{:S(2)}, u32[]{:S(2)}) collective-permute-start(bf16[2,288,288]{2,1,0:T(8,128)(2,1)} %add_convert_fusion.7), channel_id=1, source_target_pairs={{0,16},{4,20},{8,24},{12,28},{16,0},{20,4},{24,8},{28,12},{1,17},{... | collective-permute-start | bytes 995336 | tf_op jit(solution)/shard_map/ppermute | solution.py:51
  404.4 18.2 %collective-permute-start.63 = (bf16[1,144,1152]{2,1,0:T(8,128)(2,1)S(1)}, bf16[1,144,1152]{2,1,0:T(8,128)(2,1)S(1)}, u32[]{:S(2)}, u32[]{:S(2)}) collective-permute-start(bf16[1,144,1152]{2,1,0:T(8,128)(2,1)S(1)} %slice.445), channel_id=1, source_target_pairs={{0,8},{4,12},{8,0},{12,4},{16,24},{20,28},{24,16},{28,20},{1,9},{5... | collective-permute-start | bytes 995336 | tf_op jit(solution)/shard_map/ppermute | solution.py:51
  (106 other events, 751.2 us)
Sparse Core Ops, SparseCore 0:
  78.3 34.4 all-gather.2
  115.1 33.1 all-gather.4
  252.9 60.7 reduce-scatter.1

commit v3 on v2

--- a/solution.py
+++ b/solution.py
@@ -175,17 +175,25 @@
 NN, NT, TN = ((1,), (0,)), ((1,), (1,)), ((0,), (0,))
 
 
-def fetch(places, where_ref, pieces, into, sems):
-    copies = []
-    for piece, (core, k, start) in zip(pieces, places):
+def fetch(places, where_ref, pieces, into, sems, first=0):
+    groups, count = {}, 0
+    lanes = pl.ds(first, into.shape[3])
+    for piece, (core, k, start) in sorted(zip(pieces, places), key=lambda pair: pair[1][1]):
         for n in range(piece.shape[0]):
             row = (where_ref[0] ^ (start + n)) * 2 + (where_ref[1] ^ core)
             copy = pltpu.make_async_copy(
-                piece.at[n], into.at[where_ref[2] ^ k, row], sems.at[len(copies)]
+                piece.at[n, :, lanes], into.at[where_ref[2] ^ k, row], sems.at[count]
             )
             copy.start()
-            copies.append(copy)
-    return copies
+            groups.setdefault(k, []).append(copy)
+            count += 1
+    return groups
+
+
+def wait_all(groups):
+    for group in groups.values():
+        for copy in group:
+            copy.wait()
 
 
 def weight_rows(buffer, q):
@@ -213,8 +221,7 @@
 def merge_kernel(places, seq, part, cols, where_ref, tokens_ref, skipped_ref, *refs):
     pieces, rest = refs[: len(places)], refs[len(places) :]
     merged_ref, normed_ref, table_ref, weight, sems = rest
-    for copy in fetch(places, where_ref, pieces, weight, sems):
-        copy.wait()
+    wait_all(fetch(places, where_ref, pieces, weight, sems))
     chunks = -(-part[1] // (weight.shape[3] - cols))
     width = part[1] // chunks
     table = [
@@ -242,39 +249,36 @@
 
 
 def seen_keys(length, rows):
-    position = lax.broadcasted_iota(jnp.int32, (1, rows), 1)
+    position = lax.broadcasted_iota(jnp.int32, (rows, 1), 0)
     return (position < length) | ((position >= CAP) & (position < CAP + 1 + PATCHES))
 
 
 def attend_kernel(places, seq, where_ref, length_ref, normed_ref, *refs):
     pieces, rest = refs[: len(places)], refs[len(places) :]
     packed_ref, mixed_ref, logs_ref, weight, sems = rest
-    for copy in fetch(places, where_ref, pieces, weight, sems):
-        copy.wait()
+    wait_all(fetch(places, where_ref, pieces, weight, sems))
     split = packed_ref.shape[2]
     rows = normed_ref.shape[0]
     for q in range(seq):
         packed_ref[q] = dot(normed_ref[...], weight_rows(weight, q)[:, :split]).astype(jnp.bfloat16)
     seen = seen_keys(length_ref[0], rows)
-    outs, logs = [], []
+    outs = []
     for head in range(HEADS):
         query, key, value = (head_of(packed_ref, part, head) for part in range(3))
-        scores = jnp.where(seen, dot(query, key, NT) * HEAD_DIM ** (-0.5), MASKED)
-        peak = jnp.max(scores, axis=-1, keepdims=True)
+        scores = jnp.where(seen, dot(key, query, NT) * HEAD_DIM ** (-0.5), MASKED)
+        peak = jnp.max(scores, axis=0, keepdims=True)
         exponent = jnp.exp(scores - peak)
-        total = jnp.sum(exponent, axis=-1, keepdims=True)
-        outs.append(dot((exponent / total).astype(jnp.bfloat16), value))
-        logs.append(peak + jnp.log(total))
+        whole = jnp.sum(exponent, axis=0, keepdims=True)
+        outs.append(dot((exponent * (1.0 / whole)).astype(jnp.bfloat16), value, TN))
+        logs_ref[head : head + 1] = peak + jnp.log(whole)
     mixed_ref[...] = jnp.concatenate(outs, axis=1).astype(jnp.bfloat16)
-    logs_ref[...] = jnp.concatenate(logs, axis=1)
-
-
-def branch_kernel(places, seq, split, where_ref, mixed_ref, merged_ref, table_ref, *refs):
+
+
+def branch_kernel(places, seq, first, skip, where_ref, mixed_ref, merged_ref, table_ref, *refs):
     pieces, rest = refs[: len(places)], refs[len(places) :]
     residual_ref, normed_two_ref, weight, sems = rest
-    for copy in fetch(places, where_ref, pieces, weight, sems):
-        copy.wait()
-    blocks = [dot(mixed_ref[...], weight_rows(weight, q)[:, split:]) for q in range(seq)]
+    wait_all(fetch(places, where_ref, pieces, weight, sems, first))
+    blocks = [dot(mixed_ref[...], weight_rows(weight, q))[:, skip:] for q in range(seq)]
     residual = merged_ref[...] + jnp.concatenate(blocks, axis=1) + table_ref[3:4]
     residual_ref[...] = residual
     normed_two = norm_rows(residual)[0] * table_ref[4:5] + table_ref[5:6]
@@ -314,37 +318,38 @@
     back_ref[...] = dot(grad_preact, expand_ref[...], NT).astype(jnp.bfloat16)
 
 
-def forth_kernel(seq, *refs):
-    hiddens, shrink_ref, outs = refs[:seq], refs[seq], refs[seq + 1 :]
-    for k in range(seq):
-        outs[k][...] = dot(hiddens[k][...], shrink_ref[...]).astype(jnp.bfloat16)
-
-
 def feed_weights_kernel(seq, norm_parts, cot_parts, *refs):
     norms, refs = refs[: len(norm_parts)], refs[len(norm_parts) :]
     cots, refs = refs[: len(cot_parts)], refs[len(cot_parts) :]
-    grads, hiddens, outs = refs[:seq], refs[seq : 2 * seq], refs[2 * seq :]
-    expand = shrink = 0.0
-    for (k, start), norm in zip(norm_parts, norms):
-        expand = expand + dot(norm[...], grads[k][start : start + norm.shape[0]], TN)
-    expand = expand.astype(jnp.bfloat16)
-    for (k, start), cot in zip(cot_parts, cots):
-        shrink = shrink + dot(hiddens[k][start : start + cot.shape[0]], cot[...], TN)
-    shrink = shrink.astype(jnp.bfloat16)
-    if len(outs) == 2:
-        outs[0][...], outs[1][...] = expand, shrink
-        return
-    batch, rows = outs[0].shape[0], expand.shape[0] // outs[0].shape[0]
-    for b in range(batch):
-        outs[0][b, :rows] = expand[b * rows : (b + 1) * rows]
-        outs[0][b, rows:] = shrink[b * (outs[0].shape[1] - rows) : (b + 1) * (outs[0].shape[1] - rows)]
-
-
-def attend_back_kernel(places, seq, where_ref, length_ref, cot_ref, residual_ref, table_ref, packed_ref, logs_ref, *refs):
+    grads, hiddens, weight_ref, refs = refs[:seq], refs[seq : 2 * seq], refs[2 * seq], refs[2 * seq + 1 :]
+    forths, rest = refs[:seq], refs[seq:]
+    expand_ref, shrink_ref, staged_expand, staged_shrink, sems = rest if len(rest) == 5 else rest[:1] + rest
+    rows = staged_expand.shape[1]
+    norm = jnp.concatenate([norm[...] for norm in norms], axis=0)
+    grad = jnp.concatenate([grads[k][...] for k in range(seq)], axis=0)
+    staged_expand[...] = dot(norm, grad, TN).astype(jnp.bfloat16).reshape(staged_expand.shape)
+    if len(rest) == 5:
+        targets = expand_ref, shrink_ref
+    else:
+        targets = expand_ref.at[:, :rows], shrink_ref.at[:, rows:]
+    first = pltpu.make_async_copy(staged_expand, targets[0], sems.at[0])
+    first.start()
+    hidden = jnp.concatenate([hiddens[k][...] for k in range(seq)], axis=0)
+    cot = jnp.concatenate([cot[...] for cot in cots], axis=0)
+    staged_shrink[...] = dot(hidden, cot, TN).astype(jnp.bfloat16).reshape(staged_shrink.shape)
+    second = pltpu.make_async_copy(staged_shrink, targets[1], sems.at[1])
+    second.start()
+    for k in range(seq):
+        forths[k][...] = dot(hiddens[k][...], weight_ref[...]).astype(jnp.bfloat16)
+    first.wait()
+    second.wait()
+
+
+def attend_back_kernel(places, seq, first, skip, where_ref, length_ref, cot_ref, residual_ref, table_ref, packed_ref, logs_ref, *refs):
     backs, refs = refs[:seq], refs[seq:]
     pieces, rest = refs[: len(places)], refs[len(places) :]
     branch_ref, grad_residual_ref, grad_packed_ref, sums_ref, weight, sems = rest
-    copies = fetch(places, where_ref, pieces, weight, sems)
+    groups = fetch(places, where_ref, pieces, weight, sems, first)
     wide = lambda value: value.astype(jnp.float32)
     grads = sum(wide(back[...]) for back in backs)
     back, gain_sum, shift_sum = norm_pull(grads, table_ref[4:5], residual_ref[...])
@@ -359,12 +364,12 @@
     sums_ref[1:2] = shift_sum
     sums_ref[2:3] = jnp.sum(wide(branch), axis=0, keepdims=True)
     sums_ref[3:4] = jnp.sum(upstream, axis=0, keepdims=True)
-    for copy in copies:
-        copy.wait()
+    wait_all(groups)
     split = packed_ref.shape[2]
     rows = cot_ref.shape[0]
+    blank = jnp.zeros((rows, skip), jnp.bfloat16)
     grad_mixed = sum(
-        dot(branch_ref[q], weight_rows(weight, q)[:, split:], NT)
+        dot(jnp.concatenate([blank, branch_ref[q]], axis=1), weight_rows(weight, q), NT)
         for q in range(seq)
     ).astype(jnp.bfloat16)
     seen = seen_keys(length_ref[0], rows)
@@ -373,19 +378,18 @@
     for head in range(HEADS):
         query, key, value = (head_of(packed_ref, part, head) for part in range(3))
         upper = grad_mixed[:, head * HEAD_DIM : (head + 1) * HEAD_DIM]
-        scores = jnp.where(seen, dot(query, key, NT) * scaling, MASKED)
-        attention = jnp.exp(scores - logs_ref[:, head : head + 1])
-        grad_attention = dot(upper, value, NT)
-        inner = jnp.sum(attention * grad_attention, axis=-1, keepdims=True)
+        scores = jnp.where(seen, dot(key, query, NT) * scaling, MASKED)
+        attention = jnp.exp(scores - logs_ref[head : head + 1])
+        grad_attention = dot(value, upper, NT)
+        inner = jnp.sum(attention * grad_attention, axis=0, keepdims=True)
         grad_scores = (attention * (grad_attention - inner)).astype(jnp.bfloat16)
-        found[0].append(dot(grad_scores, key) * scaling)
-        found[1].append(dot(grad_scores, query, TN) * scaling)
-        found[2].append(dot(attention.astype(jnp.bfloat16), upper, TN))
+        found[0].append((dot(grad_scores, key, TN) * scaling).astype(jnp.bfloat16))
+        found[1].append((dot(grad_scores, query) * scaling).astype(jnp.bfloat16))
+        found[2].append(dot(attention.astype(jnp.bfloat16), upper).astype(jnp.bfloat16))
     slots = found[0] + found[1] + found[2]
     per_block = split // HEAD_DIM
     for q in range(seq):
-        block = jnp.concatenate(slots[q * per_block : (q + 1) * per_block], axis=1)
-        grad_packed_ref[q] = block.astype(jnp.bfloat16)
+        grad_packed_ref[q] = jnp.concatenate(slots[q * per_block : (q + 1) * per_block], axis=1)
 
 
 def send_out(depth, where_ref, staged, own_ref, other_ref, sems, base):
@@ -433,10 +437,14 @@
 def norm_back_kernel(places, seq, where_ref, grad_packed_ref, merged_ref, table_ref, grad_residual_ref, *refs):
     pieces, rest = refs[: len(places)], refs[len(places) :]
     grad_merged_ref, sums_ref, weight, sems = rest
-    for copy in fetch(places, where_ref, pieces, weight, sems):
-        copy.wait()
+    groups = fetch(places, where_ref, pieces, weight, sems)
     split = grad_packed_ref.shape[2]
-    grads = sum(dot(grad_packed_ref[q], weight_rows(weight, q)[:, :split], NT) for q in range(seq))
+    grads = 0.0
+    for k, group in groups.items():
+        for copy in group:
+            copy.wait()
+        q = where_ref[2] ^ k
+        grads = grads + dot(grad_packed_ref[q], weight_rows(weight, q)[:, :split], NT)
     back, gain_sum, shift_sum = norm_pull(grads, table_ref[1:2], merged_ref[...])
     grad_merged = (grad_residual_ref[...] + back).astype(jnp.bfloat16)
     wing = grad_merged_ref.shape[2]
@@ -450,8 +458,7 @@
 def joined_back_kernel(places, seq, where_ref, grad_ref, *refs):
     pieces, rest = refs[: len(places)], refs[len(places) :]
     tokens_ref, skipped_ref, weight, sems = rest
-    for copy in fetch(places, where_ref, pieces, weight, sems):
-        copy.wait()
+    wait_all(fetch(places, where_ref, pieces, weight, sems))
     half = tokens_ref.shape[1]
     cols = grad_ref.shape[2]
     blocks = [weight_rows(weight, q)[:, :cols] for q in range(seq)]
@@ -462,10 +469,25 @@
 VMEM = pl.BlockSpec(memory_space=pltpu.VMEM)
 SMEM = pl.BlockSpec(memory_space=pltpu.SMEM)
 ANY = pl.BlockSpec(memory_space=pl.ANY)
-
-
-def call(kernel, outs, specs, operands, out_specs=None, scratch=(), flops=0, behind=()):
+HBM = pl.BlockSpec(memory_space=pltpu.HBM)
+
+
+def padded_bytes(shape, kind):
+    size = jnp.dtype(kind).itemsize
+    rows, cols = ((1, 1) + tuple(shape))[-2:]
+    tiles = -(-rows * size // 32) * -(-cols // 128) * 32 * 128
+    for extent in shape[:-2]:
+        tiles *= extent
+    return tiles
+
+
+def call(kernel, outs, specs, operands, out_specs=None, scratch=(), flops=0, behind=(), spare=None):
     inputs = len(operands)
+
+    held = [(value.shape, value.dtype) for value, spec in zip(operands, specs) if spec is VMEM]
+    held += [shape for shape, spec in zip(outs, out_specs or [VMEM] * len(outs)) if spec is VMEM]
+    held += [(piece.shape, piece.dtype) for piece in scratch[:-1]]
+    need = sum(padded_bytes(*shape) for shape in held) + spare * 2**20 if spare else 52 * 2**20
 
     def body(*refs):
         kernel(*refs[:inputs], *refs[inputs + len(behind) :])
@@ -476,7 +498,7 @@
         in_specs=list(specs) + [ANY] * len(behind),
         out_specs=out_specs or [VMEM] * len(outs),
         scratch_shapes=list(scratch),
-        compiler_params=pltpu.CompilerParams(vmem_limit_bytes=52 * 1024 * 1024),
+        compiler_params=pltpu.CompilerParams(vmem_limit_bytes=need),
         cost_estimate=pl.CostEstimate(flops=flops, bytes_accessed=flops // 300, transcendentals=0),
     )(*operands, *behind)
 
@@ -557,10 +579,12 @@
         pltpu.VMEM((S, B, *merge_shard.shape), bf16),
         pltpu.SemaphoreType.DMA((2 * S * Z,)),
     ]
-    both_scratch = [
-        pltpu.VMEM((S, B, in_rows, both_cols), bf16),
-        pltpu.SemaphoreType.DMA((2 * S * Z,)),
-    ]
+    in_lanes = min(-(-in_cols // 128) * 128, both_cols)
+    out_first = in_cols // 128 * 128 if both_cols % 128 == 0 else 0
+    in_scratch, out_scratch = (
+        [pltpu.VMEM((S, B, in_rows, lanes), bf16), pltpu.SemaphoreType.DMA((2 * S * Z,))]
+        for lanes in (in_lanes, both_cols - out_first)
+    )
     many_merge = [ANY] * len(merge_pieces)
     layer_flops = 2 * row_count * model_width * model_width
 
@@ -583,7 +607,7 @@
     low_units = ((row_count, units), bf16)
     cot_plane = [(upstream, 0, 0)] + [(piece, k, 0) for k, piece in enumerate(cot_near, 1)]
 
-    def grad_hidden_of(chosen):
+    def grad_hidden_of(chosen, spare=None):
         cots = [piece for piece in cot_plane if piece[1] in chosen]
         parts = tuple((chosen.index(k), start) for _, k, start in cots)
         return call(
@@ -592,6 +616,7 @@
             [VMEM] * (len(cots) + 1),
             (shrink_part, *[piece[0] for piece in cots]),
             flops=len(chosen) * layer_flops,
+            spare=spare,
         )
 
     grad_hiddens = grad_hidden_of([0, 1, 2])
@@ -603,10 +628,10 @@
     many_both = [ANY] * len(both_pieces)
     packed, mixed, logs = call(
         partial(attend_kernel, both_places, S),
-        [((S, row_count, in_cols), bf16), low_rows, ((row_count, HEADS), f32)],
+        [((S, row_count, in_cols), bf16), low_rows, ((HEADS, row_count), f32)],
         [SMEM, SMEM, VMEM] + many_both,
         (where, lengths, normed, *both_pieces),
-        scratch=both_scratch,
+        scratch=in_scratch,
         flops=6 * layer_flops,
     )
     if S == 4:
@@ -615,15 +640,15 @@
         cot_plane.append((grid.plane(after(cot_near[0][split_rows:], *late), 2), 3, split_rows))
 
     residual, normed_two = call(
-        partial(branch_kernel, both_places, S, in_cols),
+        partial(branch_kernel, both_places, S, out_first, in_cols - out_first),
         [wide_rows, low_rows],
         [SMEM, VMEM, VMEM, VMEM] + many_both,
         (where, mixed, merged, table, *both_pieces),
-        scratch=both_scratch,
+        scratch=out_scratch,
         flops=layer_flops,
         behind=[piece[0] for piece in cot_plane[3:]],
     )
-    grad_hiddens += grad_hidden_of(list(range(3, S)))
+    grad_hiddens += grad_hidden_of(list(range(3, S)), 6)
     hiddens, grad_preacts, backs, unit_sums = [], [], [], []
     norm_plane = [(normed_two, 0, 0)]
     for k in range(S):
@@ -640,7 +665,8 @@
             [VMEM] * (len(norms) + 3),
             (*norms, grad_hiddens[k], expand_part, expand_bias),
             flops=3 * layer_flops,
-            behind=backs[-1:] and (hiddens[-1],),
+            spare=10,
+            behind=(hiddens[-1], *grad_hiddens[3:]) if k else (),
         )
         hiddens.append(hidden)
         grad_preacts.append(grad_preact)
@@ -648,31 +674,31 @@
         unit_sums.append(unit_sum)
     joint = units == model_width
     fed_rows = model_width // B + unit
-    fed = call(
+    found = call(
         partial(feed_weights_kernel, S, *(tuple(piece[1:] for piece in plane) for plane in (norm_plane, cot_plane))),
-        [((B, fed_rows, units), bf16)] if joint else [((model_width, units), bf16), ((units, model_width), bf16)],
-        [VMEM] * (len(norm_plane) + len(cot_plane) + 2 * S),
-        (*[piece[0] for piece in norm_plane], *[piece[0] for piece in cot_plane], *grad_preacts, *hiddens),
+        [low_rows] * S
+        + ([((B, fed_rows, units), bf16)] if joint else [((B, model_width // B, units), bf16), ((B, unit, model_width), bf16)]),
+        [VMEM] * (len(norm_plane) + len(cot_plane) + 2 * S + 1),
+        (*[piece[0] for piece in norm_plane], *[piece[0] for piece in cot_plane], *grad_preacts, *hiddens, shrink_part),
+        out_specs=[VMEM] * S + [HBM] * (1 if joint else 2),
+        scratch=[
+            pltpu.VMEM((B, model_width // B, units), bf16),
+            pltpu.VMEM((B, unit, model_width), bf16),
+            pltpu.SemaphoreType.DMA((2,)),
+        ],
         flops=2 * S * layer_flops,
     )
+    forths, fed = found[:S], found[S:]
     if joint:
         own_fed = lax.psum_scatter(fed[0], "batch", scatter_dimension=0)
         own_expand, own_shrink = own_fed[:-unit], own_fed[-unit:]
     else:
-        own_expand = lax.psum_scatter(fed[0].reshape(B, -1, units), "batch", scatter_dimension=0)
-        own_shrink = lax.psum_scatter(fed[1].reshape(B, unit, -1), "batch", scatter_dimension=0)
-    forths = call(
-        partial(forth_kernel, S),
-        [low_rows] * S,
-        [VMEM] * (S + 1),
-        (*hiddens, shrink_part),
-        flops=S * layer_flops,
-        behind=fed[:1],
-    )
+        own_expand = lax.psum_scatter(fed[0], "batch", scatter_dimension=0)
+        own_shrink = lax.psum_scatter(fed[1], "batch", scatter_dimension=0)
     forths = [forths[0]] + [grid.plane(after(forths[k], *backs[1:]), k) for k in range(1, S)]
     result = residual + sum(wide(piece) for piece in forths) + shrink_bias
     branches, grad_residual, grad_packed, sums_two = call(
-        partial(attend_back_kernel, both_places, S),
+        partial(attend_back_kernel, both_places, S, out_first, in_cols - out_first),
         [
             ((S, row_count, merge_cols), bf16),
             wide_rows,
@@ -681,7 +707,7 @@
         ],
         [SMEM, SMEM] + [VMEM] * (5 + S) + many_both,
         (where, lengths, upstream, residual, table, packed, logs, *backs, *both_pieces),
-        scratch=both_scratch,
+        scratch=out_scratch,
         flops=4 * layer_flops,
         behind=forths[:1],
     )
@@ -691,7 +717,7 @@
         [((Z, in_rows, both_cols), bf16)] * (2 * S),
         [SMEM] + [VMEM] * 4,
         (where, normed, mixed, grad_packed, branches),
-        out_specs=[ANY] * (2 * S),
+        out_specs=[HBM] * (2 * S),
         scratch=[pltpu.VMEM((S, B, in_rows, both_cols), bf16), pltpu.SemaphoreType.DMA((S * B,))],
         flops=4 * layer_flops,
         behind=forths[1:],
@@ -705,7 +731,7 @@
         [((S, row_count, merge_cols), bf16), ((8, model_width), f32)],
         [SMEM] + [VMEM] * 4 + many_both,
         (where, grad_packed, merged, table, grad_residual, *both_pieces),
-        scratch=both_scratch,
+        scratch=in_scratch,
         flops=3 * layer_flops,
         behind=both_far,
     )
@@ -715,16 +741,13 @@
         [SMEM] + [VMEM] * 3,
         (where, flat_tokens, flat_skipped, grad_merged),
         behind=both_sent,
-        out_specs=[ANY] * (2 * S),
+        out_specs=[HBM] * (2 * S),
         scratch=[pltpu.VMEM((S, B, merge_rows, merge_cols), bf16), pltpu.SemaphoreType.DMA((S * B,))],
         flops=2 * layer_flops,
     )
     merge_own, merge_other = found[:S], [grid.core(piece) for piece in found[S:]]
-    merge_far = [after(piece, *both_came) for piece in scatter_far(grid, merge_own, merge_other)]
+    merge_far = [after(piece, *both_came, both_away) for piece in scatter_far(grid, merge_own, merge_other)]
     merge_sent = scatter_near(grid, merge_own, merge_other, merge_far)
-    merge_away, merge_kept, _ = scatter_plane(grid, merge_own, merge_other, merge_sent)
-    shard_both = scatter_line(grid, both_away, both_kept, merge_away)
-    shard_inflow, shard_outflow = shard_both[:, :in_cols], shard_both[:, in_cols:]
     tokens_grad, skipped_grad = call(
         partial(joined_back_kernel, merge_places, S),
         [wide_rows, wide_rows],
@@ -734,10 +757,7 @@
         flops=2 * layer_flops,
         behind=merge_sent,
     )
-    tokens_grad = tokens_grad.reshape(tokens.shape)
-    skipped_grad = skipped_grad.reshape(tokens.shape)
-
-    own_expand, own_shrink = after(own_expand, merge_away), after(own_shrink, merge_away)
+    own_expand, own_shrink = after(own_expand, *merge_far), after(own_shrink, *merge_far)
     back_expand = own_expand.reshape(own_expand.shape[0], S, -1).transpose(1, 0, 2)
     back_shrink = own_shrink.reshape(unit, S, -1).transpose(1, 0, 2)
     expand_came, shrink_came = swap_both(grid, back_expand, back_shrink)
@@ -745,7 +765,14 @@
     shard_expand = shard_expand.reshape(S, expand.shape[0], B // S, unit).transpose(1, 2, 0, 3)
     shard_expand = wide(shard_expand).reshape(expand.shape)
     shard_shrink = wide(jnp.stack(shrink_came, axis=0)).reshape(shrink.shape)
-    shard_merging = scatter_line(grid, merge_away, merge_kept, *expand_came, *shrink_came)
+    merge_away, merge_kept, _ = scatter_plane(grid, merge_own, merge_other, merge_sent)
+    merge_away = after(merge_away, tokens_grad, *expand_came, *shrink_came)
+    tokens_grad = tokens_grad.reshape(tokens.shape)
+    skipped_grad = skipped_grad.reshape(tokens.shape)
+
+    shard_both = scatter_line(grid, both_away, after(both_kept, merge_away), merge_away)
+    shard_inflow, shard_outflow = shard_both[:, :in_cols], shard_both[:, in_cols:]
+    shard_merging = scatter_line(grid, merge_away, merge_kept)
     expand_sums = sum(unit_sums).reshape(B, 1, unit)
     expand_sums = lax.dynamic_update_slice(jnp.zeros((B, S, unit), f32), expand_sums, (0, grid.j, 0))
     grad_table = jnp.concatenate(

time: 492 us -> 466 us (0.947)
  Pallas kernels: 168 us -> 142 us
  waiting for transfers between devices: 144 us -> 125 us
  other arithmetic: 40.5 us -> 52 us
  local copies, waits for them, and re-layouts: 29.7 us -> 40.7 us
    pallas_call x16 -> x15, Pallas kernels: 168 us -> 142 us  [call(): pl.pallas_call(body, out_shape=[jax.ShapeDtypeStruct(shape, kind) for sha...]
    ppermute x14, waiting for transfers between devices: 35.5 us -> 25.4 us  [line(): lax.ppermute(value, 'batch', [(b, b ^ 2 * k) for b in range(self.batch)])]
    ppermute x40, waiting for transfers between devices: 98.6 us -> 89.3 us  [plane(): return lax.ppermute(value, 'seq', [(j, j ^ k) for j in range(self.seq)])]
    unnamed x155 -> x193, local copies, waits for them, and re-layouts: 9.04 us -> 14.3 us
  transfers between devices with their start and end apart: 77 -> 77, of which waited for: 35 -> 37; matrix products, arithmetic and copies ran while one was open for 9% -> 13% of each run, Pallas kernels for 35% -> 31%
where the time goes in v3:
time: 466 us; the launch traced here: 460 us
  Pallas kernels  142 us (30%)
  waiting for transfers between devices  125 us (27%)
  starting transfers between devices  76.2 us (16%)
  other arithmetic  52 us (11%)
  local copies, waits for them, and re-layouts  40.7 us (9%)
  between operations  24.7 us (5%)
    pallas_call x15, Pallas kernels, call(): pl.pallas_call(body, out_shape=[jax.ShapeDtypeStruct(shape, kind) for sha...  142 us
    ppermute x40, waiting for transfers between devices, plane(): return lax.ppermute(value, 'seq', [(j, j ^ k) for j in range(self.seq)])  89.3 us
    ppermute x40, starting transfers between devices, plane(): return lax.ppermute(value, 'seq', [(j, j ^ k) for j in range(self.seq)])  47.6 us
    ppermute x14, waiting for transfers between devices, line(): lax.ppermute(value, 'batch', [(b, b ^ 2 * k) for b in range(self.batch)])  25.4 us
    ppermute x14, starting transfers between devices, line(): lax.ppermute(value, 'batch', [(b, b ^ 2 * k) for b in range(self.batch)])  22.7 us
    unnamed x193, local copies, waits for them, and re-layouts  14.3 us
    add x6, other arithmetic, adamw(): smoothed = SHADOW * shadow + (1.0 - SHADOW) * trained  11.5 us
    ppermute x20, waiting for transfers between devices, core(): return lax.ppermute(value, 'batch', [(b, b ^ 1) for b in range(self.batch)])  10.1 us
  transfers between devices with their start and end apart: 77, of which 37 were waited for; matrix products, arithmetic and copies ran while one was open for 13% of the time, Pallas kernels for 31%

profile of v3, /device:TPU:0, one launch (start us, length us, event | category | flops | bytes accessed | tf_op | source)
XLA Modules:
  0.0 460.2 jit_solution(12015999021677277059)
XLA Ops:
  11.5 3.9 collective-permute-start.5
  16.8 4.1 collective-permute-start.2
  27.8 11.4 %collective-permute-done.1 = bf16[288,384]{1,0:T(8,128)(2,1)} collective-permute-done((bf16[288,384]{1,0:T(8,128)(2,1)}, bf16[288,384]{1,0:T(8,128)(2,1)}, u32[]{:S(2)}, u32[]{:S(2)}) %collective-permute-start.1) | collective-permute-done | bytes 221216 | tf_op jit(solution)/shard_map/ppermute | solution.py:51
  39.2 2.1 pad_maximum_fusion.3.refs_3_.refs_2_
  41.3 2.2 collective-permute-done.3.refs_2_.refs_6_
  47.1 3.7 collective-permute-start.19
  51.6 14.1 %collective-permute-done.9.refs_5_.refs_4_ = bf16[4,288,384]{2,1,0:T(8,128)(2,1)} collective-permute-done((bf16[4,288,384]{2,1,0:T(8,128)(2,1)}, bf16[4,288,384]{2,1,0:T(8,128)(2,1)}, u32[]{:S(2)}, u32[]{:S(2)}) %collective-permute-start.9) | collective-permute-done | bytes 884768 | tf_op jit(solution)/shard_map/ppermute | solution.py:48
  74.3 3.2 collective-permute-done.18
  77.9 2.5 collective-permute-done.11.refs_7_.refs_6_
  83.6 2.5 pad_maximum_fusion.refs_3_.refs_4_.refs_11_.refs_5_
  88.8 2.6 collective-permute-done.12.refs_8_.refs_7_
  94.0 9.9 %shard_map.491 = (f32[336,1152]{1,0:T(8,128)}, bf16[336,1152]{1,0:T(8,128)(2,1)}, f32[11,1152]{1,0:T(8,128)S(1)}) custom-call(s32[3]{0:T(128)S(1)} %pad_add_fusion.refs_0_, bf16[336,1152]{1,0:T(8,128)(2,1)} %bitcast.71, bf16[336,1152]{1,0:T(8,128)(2,1)} %bitcast.73, bf16[4,288,384]{2,1,0:T(8,128)(2,1)} %pad_maximum_fusion.3.refs_3_.refs_2_, ...), custom_call_target="tpu_custom_call" | custom-call | flops 1783627776 | bytes 5945425 | tf_op jit(solution)/shard_map/pallas_call | solution.py:495
  103.9 13.7 %collective-permute-done.21.refs_5_.refs_6_.refs_13_.refs_7_ = bf16[4,144,1152]{2,1,0:T(8,128)(2,1)} collective-permute-done((bf16[4,144,1152]{2,1,0:T(8,128)(2,1)}, bf16[4,144,1152]{2,1,0:T(8,128)(2,1)}, u32[]{:S(2)}, u32[]{:S(2)}) %collective-permute-start.21) | collective-permute-done | bytes 1327136 | tf_op jit(solution)/shard_map/ppermute | solution.py:48
  124.1 6.7 %shard_map.492 = (f32[336,1152]{1,0:T(8,128)}, f32[336,1152]{1,0:T(8,128)}, f32[336,1152]{1,0:T(8,128)}) custom-call(bf16[1152,1152]{1,0:T(8,128)(2,1)} %all-gather.3.cloned.1.call-done.refs_0_.refs_18_, bf16[336,1152]{1,0:T(8,128)(2,1)S(1)} %bitcast.79, bf16[336,1152]{1,0:T(8,128)(2,1)S(1)} %collective-permute-done.3.refs_2_.refs_6_, ...), custom_call_target="tpu_custom_call" | custom-call | flops 2675441664 | bytes 8918138 | tf_op jit(solution)/shard_map/pallas_call | solution.py:495
  130.8 5.0 %collective-permute-done.22.refs_6_.refs_7_.refs_14_.refs_8_ = bf16[2,144,1152]{2,1,0:T(8,128)(2,1)S(1)} collective-permute-done((bf16[2,144,1152]{2,1,0:T(8,128)(2,1)}, bf16[2,144,1152]{2,1,0:T(8,128)(2,1)S(1)}, u32[]{:S(2)}, u32[]{:S(2)}) %collective-permute-start.22) | collective-permute-done | bytes 663584 | tf_op jit(solution)/shard_map/ppermute | solution.py:48
  135.8 2.8 collective-permute-done.23.refs_7_.refs_8_.refs_15_.refs_9_
  143.8 14.1 %shard_map.493 = (bf16[4,336,864]{2,1,0:T(8,128)(2,1)}, bf16[336,1152]{1,0:T(8,128)(2,1)}, f32[16,336]{1,0:T(8,128)S(1)}) custom-call(s32[3]{0:T(128)S(1)} %pad_add_fusion.refs_0_, s32[1]{0:T(128)S(6)} %copy.81.refs_1_, bf16[336,1152]{1,0:T(8,128)(2,1)} %get-tuple-element.117.refs_2_.refs_1_, ...), custom_call_target="tpu_custom_call" | custom-call | flops 5350883328 | bytes 17836276 | tf_op jit(solution)/shard_map/pallas_call | solution.py:495
  158.0 7.6 %shard_map.494 = (f32[336,1152]{1,0:T(8,128)}, bf16[336,1152]{1,0:T(8,128)(2,1)}) custom-call(s32[3]{0:T(128)S(1)} %pad_add_fusion.refs_0_, bf16[336,1152]{1,0:T(8,128)(2,1)} %get-tuple-element.129.refs_1_.refs_2_, f32[336,1152]{1,0:T(8,128)} %get-tuple-element.120.refs_2_, f32[11,1152]{1,0:T(8,128)S(1)} %get-tuple-element.130.refs_3_.refs_4_, ...), custom_call_target="tpu_custom_call" | custom-call | flops 891813888 | bytes 2972712 | tf_op jit(solution)/shard_map/pallas_call | solution.py:495
  177.3 4.1 shard_map.495
  185.9 5.4 %shard_map.497 = (bf16[336,1152]{1,0:T(8,128)(2,1)S(1)}, bf16[336,1152]{1,0:T(8,128)(2,1)S(1)}, bf16[336,1152]{1,0:T(8,128)(2,1)S(1)}, f32[1,1152]{1,0:T(1,128)S(1)}) custom-call(bf16[336,1152]{1,0:T(8,128)(2,1)} %collective-permute-done.31.refs_0_.refs_1_, f32[336,1152]{1,0:T(8,128)S(1)} %copy-done.31, bf16[1152,1152]{1,0:T(8,128)(2,1)S(1)} %copy-done.27, ...), custom_call_target="tpu_custom_call" | custom-call | flops 2675441664 | bytes 8918138 | tf_op jit(solution)/shard_map/pallas_call | solution.py:495
  195.4 5.8 %shard_map.498 = (bf16[336,1152]{1,0:T(8,128)(2,1)S(1)}, bf16[336,1152]{1,0:T(8,128)(2,1)S(1)}, bf16[336,1152]{1,0:T(8,128)(2,1)S(1)}, f32[1,1152]{1,0:T(1,128)S(1)}) custom-call(bf16[336,1152]{1,0:T(8,128)(2,1)} %collective-permute-done.32.refs_0_.refs_2_, f32[336,1152]{1,0:T(8,128)S(1)} %copy-done.30, bf16[1152,1152]{1,0:T(8,128)(2,1)S(1)} %copy-done.27, ...), custom_call_target="tpu_custom_call" | custom-call | flops 2675441664 | bytes 8918138 | tf_op jit(solution)/shard_map/pallas_call | solution.py:495
  202.4 2.5 collective-permute-done.33.refs_0_.refs_3_
  204.9 5.0 %shard_map.499 = (bf16[336,1152]{1,0:T(8,128)(2,1)S(1)}, bf16[336,1152]{1,0:T(8,128)(2,1)S(1)}, bf16[336,1152]{1,0:T(8,128)(2,1)}, f32[1,1152]{1,0:T(1,128)S(1)}) custom-call(bf16[160,1152]{1,0:T(8,128)(2,1)S(1)} %collective-permute-done.33.refs_0_.refs_3_, bf16[176,1152]{1,0:T(8,128)(2,1)S(1)} %collective-permute-done.34.refs_1_.refs_4_, ...), custom_call_target="tpu_custom_call" | custom-call | flops 2675441664 | bytes 8918138 | tf_op jit(solution)/shard_map/pallas_call | solution.py:495
  213.2 20.5 %shard_map.500 = (bf16[336,1152]{1,0:T(8,128)(2,1)}, bf16[336,1152]{1,0:T(8,128)(2,1)}, bf16[336,1152]{1,0:T(8,128)(2,1)}, bf16[336,1152]{1,0:T(8,128)(2,1)}, bf16[8,288,1152]{2,1,0:T(8,128)(2,1)}) custom-call(bf16[336,1152]{1,0:T(8,128)(2,1)} %get-tuple-element.134.refs_0_, bf16[336,1152]{1,0:T(8,128)(2,1)} %collective-permute-done.31.refs_0_.refs_1_, ...), custom_call_target="tpu_custom_call" | custom-call | flops 7134511104 | bytes 23781704 | tf_op jit(solution)/shard_map/pallas_call | solution.py:495
  233.8 2.3 collective-permute-done.37.refs_10_
  239.6 21.5 %shard_map.501 = (bf16[4,336,288]{2,1,0:T(8,128)(2,1)}, f32[336,1152]{1,0:T(8,128)}, bf16[4,336,864]{2,1,0:T(8,128)(2,1)}, f32[8,1152]{1,0:T(8,128)S(1)}) custom-call(s32[3]{0:T(128)S(1)} %pad_add_fusion.refs_0_, s32[1]{0:T(128)S(6)} %copy.81.refs_1_, bf16[336,1152]{1,0:T(8,128)(2,1)} %bitcast.76, f32[336,1152]{1,0:T(8,128)} %get-tuple-element.133.refs_3_, ...), custom_call_target="tpu_custom_call" | custom-call | flops 3567255552 | bytes 11890851 | tf_op jit(solution)/shard_map/pallas_call | solution.py:495
  261.1 9.4 %collective-permute-done.39.refs_6_ = bf16[336,1152]{1,0:T(8,128)(2,1)S(1)} collective-permute-done((bf16[336,1152]{1,0:T(8,128)(2,1)}, bf16[336,1152]{1,0:T(8,128)(2,1)S(1)}, u32[]{:S(2)}, u32[]{:S(2)}) %collective-permute-start.39) | collective-permute-done | bytes 774176 | tf_op jit(solution)/shard_map/ppermute | solution.py:48
  271.7 10.9 %shard_map.502 = (bf16[4,144,1152]{2,1,0:T(8,128)(2,1)}, bf16[4,144,1152]{2,1,0:T(8,128)(2,1)}, bf16[4,144,1152]{2,1,0:T(8,128)(2,1)}, bf16[4,144,1152]{2,1,0:T(...) custom-call(s32[3]{0:T(128)S(1)} %pad_add_fusion.refs_0_, ...), custom_call_target="tpu_custom_call" | custom-call | flops 3567255552 | bytes 11890851 | tf_op jit(solution)/shard_map/pallas_call | solution.py:495
  283.2 2.8 collective-permute-done.41
  290.3 11.7 %shard_map.503 = (bf16[4,336,288]{2,1,0:T(8,128)(2,1)}, f32[8,1152]{1,0:T(8,128)S(1)}) custom-call(s32[3]{0:T(128)S(1)} %pad_add_fusion.refs_0_, bf16[4,336,864]{2,1,0:T(8,128)(2,1)} %get-tuple-element.159.refs_3_.refs_1_, f32[336,1152]{1,0:T(8,128)} %get-tuple-element.120.refs_2_, f32[11,1152]{1,0:T(8,128)S(1)} %get-tuple-element.130.refs_3_.refs_4_, ...), custom_call_target="tpu_custom_call" | custom-call | flops 2675441664 | bytes 8918138 | tf_op jit(solution)/shard_map/pallas_call | solution.py:495
  302.0 2.9 collective-permute-done.43
  310.3 7.3 %shard_map.504 = (bf16[4,288,288]{2,1,0:T(8,128)(2,1)}, bf16[4,288,288]{2,1,0:T(8,128)(2,1)}, bf16[4,288,288]{2,1,0:T(8,128)(2,1)}, bf16[4,288,288]{2,1,0:T(8,12...) custom-call(s32[3]{0:T(128)S(1)} %pad_add_fusion.refs_0_, ...), custom_call_target="tpu_custom_call" | custom-call | flops 1783627776 | bytes 5945425 | tf_op jit(solution)/shard_map/pallas_call | solution.py:495
  321.6 3.0 collective-permute-done.55
  324.6 2.5 collective-permute-start.56
  329.3 6.9 %collective-permute-done.48 = bf16[4,144,1152]{2,1,0:T(8,128)(2,1)} collective-permute-done((bf16[4,144,1152]{2,1,0:T(8,128)(2,1)S(1)}, bf16[4,144,1152]{2,1,0:T(8,128)(2,1)}, u32[]{:S(2)}, u32[]{:S(2)}) %collective-permute-start.48) | collective-permute-done | bytes 1327136 | tf_op jit(solution)/shard_map/ppermute | solution.py:48
  336.2 3.4 collective-permute-done.49
  339.7 3.7 convert_add_fusion.1
  347.6 6.0 %collective-permute-done.51 = bf16[2,288,288]{2,1,0:T(8,128)(2,1)S(1)} collective-permute-done((bf16[2,288,288]{2,1,0:T(8,128)(2,1)S(1)}, bf16[2,288,288]{2,1,0:T(8,128)(2,1)S(1)}, u32[]{:S(2)}, u32[]{:S(2)}) %collective-permute-start.51) | collective-permute-done | bytes 331808 | tf_op jit(solution)/shard_map/ppermute | solution.py:48
  353.6 2.2 collective-permute-start.65
  360.1 9.3 %shard_map.505 = (f32[336,1152]{1,0:T(8,128)}, f32[336,1152]{1,0:T(8,128)}) custom-call(s32[3]{0:T(128)S(1)} %pad_add_fusion.refs_0_, bf16[4,336,288]{2,1,0:T(8,128)(2,1)} %get-tuple-element.164.refs_3_.refs_1_, bf16[4,288,384]{2,1,0:T(8,128)(2,1)} %pad_maximum_fusion.3.refs_3_.refs_2_, bf16[4,288,384]{2,1,0:T(8,128)(2,1)} %collective-permute-done.8.refs_4_.refs_3_, ...), custom_call_target="tpu_custom_call" | custom-call | flops 1783627776 | bytes 5945425 | tf_op jit(solution)/shard_map/pallas_call | solution.py:495
  374.1 4.8 %collective-permute-done.59 = bf16[4,288,288]{2,1,0:T(8,128)(2,1)} collective-permute-done((bf16[4,288,288]{2,1,0:T(8,128)(2,1)S(1)}, bf16[4,288,288]{2,1,0:T(8,128)(2,1)}, u32[]{:S(2)}, u32[]{:S(2)}) %collective-permute-start.59) | collective-permute-done | bytes 663584 | tf_op jit(solution)/shard_map/ppermute | solution.py:48
  381.6 2.3 add_convert_fusion.7
  425.5 2.5 collective-permute-start.71
  430.6 2.1 collective-permute-start.72
  434.9 2.6 collective-permute-start.73
  439.9 3.1 multiply_add_fusion.6
  447.6 2.1 multiply_add_fusion.3
  449.8 2.5 multiply_add_fusion.7
  (420 shorter events, 152.2 us)
Async XLA Ops:
  7.2 116.9 %all-gather.3.cloned.1.call-start = ((), (), s32[]{:S(2)}) async-start(), calls=%async_computation.1 | async-start | bytes 2985984 | tf_op jit(solution)/shard_map/all_gather | solution.py:572
  20.9 18.3 %collective-permute-start.1 = (bf16[288,384]{1,0:T(8,128)(2,1)}, bf16[288,384]{1,0:T(8,128)(2,1)}, u32[]{:S(2)}, u32[]{:S(2)}) collective-permute-start(bf16[288,384]{1,0:T(8,128)(2,1)} %fusion.7), channel_id=1, source_target_pairs={{0,16},{4,20},{8,24},{12,28},{16,0},{20,4},{24,8},{28,12},{1,17},{... | collective-permute-start | bytes 663560 | tf_op jit(solution)/shard_map/ppermute | solution.py:51
  21.1 18.1 %collective-permute-start = (bf16[288,384]{1,0:T(8,128)(2,1)}, bf16[288,384]{1,0:T(8,128)(2,1)S(1)}, u32[]{:S(2)}, u32[]{:S(2)}) collective-permute-start(bf16[288,384]{1,0:T(8,128)(2,1)} %fusion.7), channel_id=1, source_target_pairs={{0,8},{4,12},{8,0},{12,4},{16,24},{20,28},{24,16},{28,20},{1,9},{5... | collective-permute-start | bytes 663560 | tf_op jit(solution)/shard_map/ppermute | solution.py:51
  24.2 19.3 %collective-permute-start.3 = (bf16[336,1152]{1,0:T(8,128)(2,1)S(1)}, bf16[336,1152]{1,0:T(8,128)(2,1)S(1)}, u32[]{:S(2)}, u32[]{:S(2)}) collective-permute-start(bf16[336,1152]{1,0:T(8,128)(2,1)S(1)} %bitcast.77), channel_id=1, source_target_pairs={{0,1},{1,0},{2,3},{3,2},{4,5},{5,4},{6,7},{7,6},{8,9},{9,8},{10,11... | collective-permute-start | bytes 2322440 | tf_op jit(solution)/shard_map/ppermute | solution.py:48
  25.9 19.0 %collective-permute-start.4 = (bf16[336,1152]{1,0:T(8,128)(2,1)S(1)}, bf16[336,1152]{1,0:T(8,128)(2,1)S(1)}, u32[]{:S(2)}, u32[]{:S(2)}) collective-permute-start(bf16[336,1152]{1,0:T(8,128)(2,1)S(1)} %bitcast.78), channel_id=1, source_target_pairs={{0,2},{1,3},{2,0},{3,1},{4,6},{5,7},{6,4},{7,5},{8,10},{9,11},{10,... | collective-permute-start | bytes 2322440 | tf_op jit(solution)/shard_map/ppermute | solution.py:48
  44.9 20.8 %collective-permute-start.9 = (bf16[4,288,384]{2,1,0:T(8,128)(2,1)}, bf16[4,288,384]{2,1,0:T(8,128)(2,1)}, u32[]{:S(2)}, u32[]{:S(2)}) collective-permute-start(bf16[4,288,384]{2,1,0:T(8,128)(2,1)} %pad_maximum_fusion.3.refs_3_.refs_2_), channel_id=1, source_target_pairs={{0,2},{1,3},{2,0},{3,1},{4,6},{5,7},{6,4},{7,5},{8,10},{9,11},{10,... | collective-permute-start | bytes 2654216 | tf_op jit(solution)/shard_map/ppermute | solution.py:48
  45.3 22.9 %collective-permute-start.8 = (bf16[4,288,384]{2,1,0:T(8,128)(2,1)}, bf16[4,288,384]{2,1,0:T(8,128)(2,1)}, u32[]{:S(2)}, u32[]{:S(2)}) collective-permute-start(bf16[4,288,384]{2,1,0:T(8,128)(2,1)} %pad_maximum_fusion.3.refs_3_.refs_2_), channel_id=1, source_target_pairs={{0,1},{1,0},{2,3},{3,2},{4,5},{5,4},{6,7},{7,6},{8,9},{9,8},{10,11... | collective-permute-start | bytes 2654216 | tf_op jit(solution)/shard_map/ppermute | solution.py:48
  47.1 27.1 %collective-permute-start.19 = (bf16[144,1152]{1,0:T(8,128)(2,1)S(1)}, bf16[144,1152]{1,0:T(8,128)(2,1)}, u32[]{:S(2)}, u32[]{:S(2)}) collective-permute-start(bf16[144,1152]{1,0:T(8,128)(2,1)S(1)} %pad_maximum_fusion.6), channel_id=1, source_target_pairs={{0,24},{4,28},{8,16},{12,20},{16,8},{20,12},{24,0},{28,4},{1,25},{... | collective-permute-start | bytes 995336 | tf_op jit(solution)/shard_map/ppermute | solution.py:51
  50.8 26.7 %collective-permute-start.18 = (bf16[144,1152]{1,0:T(8,128)(2,1)S(1)}, bf16[144,1152]{1,0:T(8,128)(2,1)}, u32[]{:S(2)}, u32[]{:S(2)}) collective-permute-start(bf16[144,1152]{1,0:T(8,128)(2,1)S(1)} %pad_maximum_fusion.6), channel_id=1, source_target_pairs={{0,16},{4,20},{8,24},{12,28},{16,0},{20,4},{24,8},{28,12},{1,17},{... | collective-permute-start | bytes 995336 | tf_op jit(solution)/shard_map/ppermute | solution.py:51
  50.8 26.7 %collective-permute-start.17 = (bf16[144,1152]{1,0:T(8,128)(2,1)S(1)}, bf16[144,1152]{1,0:T(8,128)(2,1)}, u32[]{:S(2)}, u32[]{:S(2)}) collective-permute-start(bf16[144,1152]{1,0:T(8,128)(2,1)S(1)} %pad_maximum_fusion.6), channel_id=1, source_target_pairs={{0,8},{4,12},{8,0},{12,4},{16,24},{20,28},{24,16},{28,20},{1,9},{5... | collective-permute-start | bytes 995336 | tf_op jit(solution)/shard_map/ppermute | solution.py:51
  80.4 92.6 %all-gather.5.cloned.1.call-start = ((), (), s32[]{:S(2)}) async-start(), calls=%async_computation.2 | async-start | bytes 2985984 | tf_op jit(solution)/shard_map/all_gather | solution.py:573
  82.4 286.9 %reduce-scatter.2.cloned.1.call-start = ((), (), s32[]{:S(2)}) async-start(), calls=%async_computation.3 | async-start | bytes 5971968 | tf_op jit(solution)/shard_map/reduce_scatter | solution.py:693
  86.1 31.5 %collective-permute-start.21 = (bf16[4,144,1152]{2,1,0:T(8,128)(2,1)}, bf16[4,144,1152]{2,1,0:T(8,128)(2,1)}, u32[]{:S(2)}, u32[]{:S(2)}) collective-permute-start(bf16[4,144,1152]{2,1,0:T(8,128)(2,1)} %pad_maximum_fusion.refs_3_.refs_4_.refs_11_.refs_5_), channel_id=1, source_target_pairs={{0,2},{1,3},{2,0},{3,1},{4,6},{5,7},{6,4},{7,5},{8,10},{9,11},{10,... | collective-permute-start | bytes 3981320 | tf_op jit(solution)/shard_map/ppermute | solution.py:48
  87.3 33.4 %collective-permute-start.20 = (bf16[4,144,1152]{2,1,0:T(8,128)(2,1)}, bf16[4,144,1152]{2,1,0:T(8,128)(2,1)}, u32[]{:S(2)}, u32[]{:S(2)}) collective-permute-start(bf16[4,144,1152]{2,1,0:T(8,128)(2,1)} %pad_maximum_fusion.refs_3_.refs_4_.refs_11_.refs_5_), channel_id=1, source_target_pairs={{0,1},{1,0},{2,3},{3,2},{4,5},{5,4},{6,7},{7,6},{8,9},{9,8},{10,11... | collective-permute-start | bytes 3981320 | tf_op jit(solution)/shard_map/ppermute | solution.py:48
  119.6 16.3 %collective-permute-start.22 = (bf16[2,144,1152]{2,1,0:T(8,128)(2,1)}, bf16[2,144,1152]{2,1,0:T(8,128)(2,1)S(1)}, u32[]{:S(2)}, u32[]{:S(2)}) collective-permute-start(bf16[2,144,1152]{2,1,0:T(8,128)(2,1)} %slice.327), channel_id=1, source_target_pairs={{0,1},{1,0},{2,3},{3,2},{4,5},{5,4},{6,7},{7,6},{8,9},{9,8},{10,11... | collective-permute-start | bytes 1990664 | tf_op jit(solution)/shard_map/ppermute | solution.py:48
  122.6 16.0 %collective-permute-start.23 = (bf16[2,144,1152]{2,1,0:T(8,128)(2,1)}, bf16[2,144,1152]{2,1,0:T(8,128)(2,1)S(1)}, u32[]{:S(2)}, u32[]{:S(2)}) collective-permute-start(bf16[2,144,1152]{2,1,0:T(8,128)(2,1)} %slice.332), channel_id=1, source_target_pairs={{0,2},{1,3},{2,0},{3,1},{4,6},{5,7},{6,4},{7,5},{8,10},{9,11},{10,... | collective-permute-start | bytes 1990664 | tf_op jit(solution)/shard_map/ppermute | solution.py:48
  123.6 20.2 %collective-permute-start.24 = (bf16[4,144,1152]{2,1,0:T(8,128)(2,1)}, bf16[4,144,1152]{2,1,0:T(8,128)(2,1)}, u32[]{:S(2)}, u32[]{:S(2)}) collective-permute-start(bf16[4,144,1152]{2,1,0:T(8,128)(2,1)} %pad_maximum_fusion.refs_3_.refs_4_.refs_11_.refs_5_), channel_id=1, source_target_pairs={{0,4},{4,0},{8,12},{12,8},{16,20},{20,16},{24,28},{28,24},{1,5},{5... | collective-permute-start | bytes 3981320 | tf_op jit(solution)/shard_map/ppermute | solution.py:54
  123.6 20.2 %collective-permute-start.25 = (bf16[4,144,1152]{2,1,0:T(8,128)(2,1)}, bf16[4,144,1152]{2,1,0:T(8,128)(2,1)}, u32[]{:S(2)}, u32[]{:S(2)}) collective-permute-start(bf16[4,144,1152]{2,1,0:T(8,128)(2,1)} %collective-permute-done.20.refs_4_.refs_5_.refs_12_.refs_6_), channel_id=1, source_target_pairs={{0,4},{4,0},{8,12},{12,8},{16,20},{20,16},{24,28},{28,24},{1,5},{5... | collective-permute-start | bytes 3981320 | tf_op jit(solution)/shard_map/ppermute | solution.py:54
  124.1 19.7 %collective-permute-start.26 = (bf16[4,144,1152]{2,1,0:T(8,128)(2,1)}, bf16[4,144,1152]{2,1,0:T(8,128)(2,1)}, u32[]{:S(2)}, u32[]{:S(2)}) collective-permute-start(bf16[4,144,1152]{2,1,0:T(8,128)(2,1)} %collective-permute-done.21.refs_5_.refs_6_.refs_13_.refs_7_), channel_id=1, source_target_pairs={{0,4},{4,0},{8,12},{12,8},{16,20},{20,16},{24,28},{28,24},{1,5},{5... | collective-permute-start | bytes 3981320 | tf_op jit(solution)/shard_map/ppermute | solution.py:54
  141.8 16.1 %collective-permute-start.29 = (bf16[160,1152]{1,0:T(8,128)(2,1)S(1)}, bf16[160,1152]{1,0:T(8,128)(2,1)S(1)}, u32[]{:S(2)}, u32[]{:S(2)}) collective-permute-start(bf16[160,1152]{1,0:T(8,128)(2,1)S(1)} %slice.333), channel_id=1, source_target_pairs={{0,1},{1,0},{2,3},{3,2},{4,5},{5,4},{6,7},{7,6},{8,9},{9,8},{10,11... | collective-permute-start | bytes 1105928 | tf_op jit(solution)/shard_map/ppermute | solution.py:48
  142.7 15.2 %collective-permute-start.30 = (bf16[176,1152]{1,0:T(8,128)(2,1)S(1)}, bf16[176,1152]{1,0:T(8,128)(2,1)S(1)}, u32[]{:S(2)}, u32[]{:S(2)}) collective-permute-start(bf16[176,1152]{1,0:T(8,128)(2,1)S(1)} %slice.334), channel_id=1, source_target_pairs={{0,2},{1,3},{2,0},{3,1},{4,6},{5,7},{6,4},{7,5},{8,10},{9,11},{10,... | collective-permute-start | bytes 1216520 | tf_op jit(solution)/shard_map/ppermute | solution.py:48
  165.6 19.2 %collective-permute-start.31 = (bf16[336,1152]{1,0:T(8,128)(2,1)}, bf16[336,1152]{1,0:T(8,128)(2,1)}, u32[]{:S(2)}, u32[]{:S(2)}) collective-permute-start(bf16[336,1152]{1,0:T(8,128)(2,1)} %get-tuple-element.134.refs_0_), channel_id=1, source_target_pairs={{0,1},{1,0},{2,3},{3,2},{4,5},{5,4},{6,7},{7,6},{8,9},{9,8},{10,11... | collective-permute-start | bytes 2322440 | tf_op jit(solution)/shard_map/ppermute | solution.py:48
  166.6 25.6 %collective-permute-start.32 = (bf16[336,1152]{1,0:T(8,128)(2,1)}, bf16[336,1152]{1,0:T(8,128)(2,1)}, u32[]{:S(2)}, u32[]{:S(2)}) collective-permute-start(bf16[336,1152]{1,0:T(8,128)(2,1)} %get-tuple-element.134.refs_0_), channel_id=1, source_target_pairs={{0,2},{1,3},{2,0},{3,1},{4,6},{5,7},{6,4},{7,5},{8,10},{9,11},{10,... | collective-permute-start | bytes 2322440 | tf_op jit(solution)/shard_map/ppermute | solution.py:48
  191.3 13.6 %collective-permute-start.34 = (bf16[176,1152]{1,0:T(8,128)(2,1)S(1)}, bf16[176,1152]{1,0:T(8,128)(2,1)S(1)}, u32[]{:S(2)}, u32[]{:S(2)}) collective-permute-start(bf16[176,1152]{1,0:T(8,128)(2,1)S(1)} %slice.339), channel_id=1, source_target_pairs={{0,2},{1,3},{2,0},{3,1},{4,6},{5,7},{6,4},{7,5},{8,10},{9,11},{10,... | collective-permute-start | bytes 1216520 | tf_op jit(solution)/shard_map/ppermute | solution.py:48
  193.3 11.6 %collective-permute-start.33 = (bf16[160,1152]{1,0:T(8,128)(2,1)S(1)}, bf16[160,1152]{1,0:T(8,128)(2,1)S(1)}, u32[]{:S(2)}, u32[]{:S(2)}) collective-permute-start(bf16[160,1152]{1,0:T(8,128)(2,1)S(1)} %slice.335), channel_id=1, source_target_pairs={{0,1},{1,0},{2,3},{3,2},{4,5},{5,4},{6,7},{7,6},{8,9},{9,8},{10,11... | collective-permute-start | bytes 1105928 | tf_op jit(solution)/shard_map/ppermute | solution.py:48
  194.5 39.3 %collective-permute-start.35 = (bf16[336,1152]{1,0:T(8,128)(2,1)S(1)}, bf16[336,1152]{1,0:T(8,128)(2,1)}, u32[]{:S(2)}, u32[]{:S(2)}) collective-permute-start(bf16[336,1152]{1,0:T(8,128)(2,1)S(1)} %get-tuple-element.148), channel_id=1, source_target_pairs={{0,1},{1,0},{2,3},{3,2},{4,5},{5,4},{6,7},{7,6},{8,9},{9,8},{10,11... | collective-permute-start | bytes 2322440 | tf_op jit(solution)/shard_map/ppermute | solution.py:48
  201.2 32.6 %collective-permute-start.36 = (bf16[336,1152]{1,0:T(8,128)(2,1)S(1)}, bf16[336,1152]{1,0:T(8,128)(2,1)}, u32[]{:S(2)}, u32[]{:S(2)}) collective-permute-start(bf16[336,1152]{1,0:T(8,128)(2,1)S(1)} %get-tuple-element.149), channel_id=1, source_target_pairs={{0,2},{1,3},{2,0},{3,1},{4,6},{5,7},{6,4},{7,5},{8,10},{9,11},{10,... | collective-permute-start | bytes 2322440 | tf_op jit(solution)/shard_map/ppermute | solution.py:48
  211.7 24.4 %collective-permute-start.37 = (bf16[336,1152]{1,0:T(8,128)(2,1)}, bf16[336,1152]{1,0:T(8,128)(2,1)}, u32[]{:S(2)}, u32[]{:S(2)}) collective-permute-start(bf16[336,1152]{1,0:T(8,128)(2,1)} %get-tuple-element.150), channel_id=1, source_target_pairs={{0,3},{1,2},{2,1},{3,0},{4,7},{5,6},{6,5},{7,4},{8,11},{9,10},{10,... | collective-permute-start | bytes 2322440 | tf_op jit(solution)/shard_map/ppermute | solution.py:48
  236.1 25.0 %collective-permute-start.40 = (bf16[336,1152]{1,0:T(8,128)(2,1)}, bf16[336,1152]{1,0:T(8,128)(2,1)S(1)}, u32[]{:S(2)}, u32[]{:S(2)}) collective-permute-start(bf16[336,1152]{1,0:T(8,128)(2,1)} %get-tuple-element.155), channel_id=1, source_target_pairs={{0,3},{1,2},{2,1},{3,0},{4,7},{5,6},{6,5},{7,4},{8,11},{9,10},{10,... | collective-permute-start | bytes 2322440 | tf_op jit(solution)/shard_map/ppermute | solution.py:48
  237.5 33.0 %collective-permute-start.39 = (bf16[336,1152]{1,0:T(8,128)(2,1)}, bf16[336,1152]{1,0:T(8,128)(2,1)S(1)}, u32[]{:S(2)}, u32[]{:S(2)}) collective-permute-start(bf16[336,1152]{1,0:T(8,128)(2,1)} %get-tuple-element.153), channel_id=1, source_target_pairs={{0,2},{1,3},{2,0},{3,1},{4,6},{5,7},{6,4},{7,5},{8,10},{9,11},{10,... | collective-permute-start | bytes 2322440 | tf_op jit(solution)/shard_map/ppermute | solution.py:48
  238.5 32.0 %collective-permute-start.38 = (bf16[336,1152]{1,0:T(8,128)(2,1)}, bf16[336,1152]{1,0:T(8,128)(2,1)S(1)}, u32[]{:S(2)}, u32[]{:S(2)}) collective-permute-start(bf16[336,1152]{1,0:T(8,128)(2,1)} %get-tuple-element.151), channel_id=1, source_target_pairs={{0,1},{1,0},{2,3},{3,2},{4,5},{5,4},{6,7},{7,6},{8,9},{9,8},{10,11... | collective-permute-start | bytes 2322440 | tf_op jit(solution)/shard_map/ppermute | solution.py:48
  282.8 22.5 %collective-permute-start.42 = (bf16[4,144,1152]{2,1,0:T(8,128)(2,1)}, bf16[4,144,1152]{2,1,0:T(8,128)(2,1)S(1)}, u32[]{:S(2)}, u32[]{:S(2)}) collective-permute-start(bf16[4,144,1152]{2,1,0:T(8,128)(2,1)} %get-tuple-element.166), channel_id=1, source_target_pairs={{0,4},{4,0},{8,12},{12,8},{16,20},{20,16},{24,28},{28,24},{1,5},{5... | collective-permute-start | bytes 3981320 | tf_op jit(solution)/shard_map/ppermute | solution.py:54
  287.7 17.2 %collective-permute-start.43 = (bf16[2,144,1152]{2,1,0:T(8,128)(2,1)S(1)}, bf16[2,144,1152]{2,1,0:T(8,128)(2,1)S(1)}, u32[]{:S(2)}, u32[]{:S(2)}) collective-permute-start(bf16[2,144,1152]{2,1,0:T(8,128)(2,1)S(1)} %get-tuple-element.246.refs_15_), channel_id=1, source_target_pairs={{0,1},{1,0},{2,3},{3,2},{4,5},{5,4},{6,7},{7,6},{8,9},{9,8},{10,11... | collective-permute-start | bytes 1990664 | tf_op jit(solution)/shard_map/ppermute | solution.py:48
  288.7 16.6 %collective-permute-start.44 = (bf16[2,144,1152]{2,1,0:T(8,128)(2,1)S(1)}, bf16[2,144,1152]{2,1,0:T(8,128)(2,1)S(1)}, u32[]{:S(2)}, u32[]{:S(2)}) collective-permute-start(bf16[2,144,1152]{2,1,0:T(8,128)(2,1)S(1)} %get-tuple-element.245.refs_16_), channel_id=1, source_target_pairs={{0,2},{1,3},{2,0},{3,1},{4,6},{5,7},{6,4},{7,5},{8,10},{9,11},{10,... | collective-permute-start | bytes 1990664 | tf_op jit(solution)/shard_map/ppermute | solution.py:48
  289.8 17.5 %collective-permute-start.45 = (bf16[4,144,1152]{2,1,0:T(8,128)(2,1)S(1)}, bf16[4,144,1152]{2,1,0:T(8,128)(2,1)S(1)}, u32[]{:S(2)}, u32[]{:S(2)}) collective-permute-start(bf16[4,144,1152]{2,1,0:T(8,128)(2,1)S(1)} %copy-done.94), channel_id=1, source_target_pairs={{0,4},{4,0},{8,12},{12,8},{16,20},{20,16},{24,28},{28,24},{1,5},{5... | collective-permute-start | bytes 3981320 | tf_op jit(solution)/shard_map/ppermute | solution.py:54
  289.8 38.9 %collective-permute-start.50 = (bf16[4,144,1152]{2,1,0:T(8,128)(2,1)}, bf16[4,144,1152]{2,1,0:T(8,128)(2,1)}, u32[]{:S(2)}, u32[]{:S(2)}) collective-permute-start(bf16[4,144,1152]{2,1,0:T(8,128)(2,1)} %get-tuple-element.176), channel_id=1, source_target_pairs={{0,4},{4,0},{8,12},{12,8},{16,20},{20,16},{24,28},{28,24},{1,5},{5... | collective-permute-start | bytes 3981320 | tf_op jit(solution)/shard_map/ppermute | solution.py:54
  306.0 30.3 %collective-permute-start.48 = (bf16[4,144,1152]{2,1,0:T(8,128)(2,1)S(1)}, bf16[4,144,1152]{2,1,0:T(8,128)(2,1)}, u32[]{:S(2)}, u32[]{:S(2)}) collective-permute-start(bf16[4,144,1152]{2,1,0:T(8,128)(2,1)S(1)} %pad_maximum_fusion.1.refs_4_), channel_id=1, source_target_pairs={{0,1},{1,0},{2,3},{3,2},{4,5},{5,4},{6,7},{7,6},{8,9},{9,8},{10,11... | collective-permute-start | bytes 3981320 | tf_op jit(solution)/shard_map/ppermute | solution.py:48
  309.2 30.4 %collective-permute-start.49 = (bf16[4,144,1152]{2,1,0:T(8,128)(2,1)}, bf16[4,144,1152]{2,1,0:T(8,128)(2,1)}, u32[]{:S(2)}, u32[]{:S(2)}) collective-permute-start(bf16[4,144,1152]{2,1,0:T(8,128)(2,1)} %pad_maximum_fusion.2.refs_5_), channel_id=1, source_target_pairs={{0,2},{1,3},{2,0},{3,1},{4,6},{5,7},{6,4},{7,5},{8,10},{9,11},{10,... | collective-permute-start | bytes 3981320 | tf_op jit(solution)/shard_map/ppermute | solution.py:48
  324.6 22.3 %collective-permute-start.56 = (f32[11,1152]{1,0:T(8,128)S(1)}, f32[11,1152]{1,0:T(8,128)S(1)}, u32[]{:S(2)}, u32[]{:S(2)}) collective-permute-start(f32[11,1152]{1,0:T(8,128)S(1)} %add.343), channel_id=1, source_target_pairs={{0,16},{4,20},{8,24},{12,28},{16,0},{20,4},{24,8},{28,12},{1,17},{... | collective-permute-start | bytes 152072 | tf_op jit(solution)/shard_map/ppermute | solution.py:51
  327.1 30.2 %collective-permute-start.46 = (bf16[4,288,288]{2,1,0:T(8,128)(2,1)}, bf16[4,288,288]{2,1,0:T(8,128)(2,1)S(1)}, u32[]{:S(2)}, u32[]{:S(2)}) collective-permute-start(bf16[4,288,288]{2,1,0:T(8,128)(2,1)} %get-tuple-element.172), channel_id=1, source_target_pairs={{0,4},{4,0},{8,12},{12,8},{16,20},{20,16},{24,28},{28,24},{1,5},{5... | collective-permute-start | bytes 1990664 | tf_op jit(solution)/shard_map/ppermute | solution.py:54
  328.7 27.1 %collective-permute-start.53 = (bf16[4,288,288]{2,1,0:T(8,128)(2,1)S(1)}, bf16[4,288,288]{2,1,0:T(8,128)(2,1)S(1)}, u32[]{:S(2)}, u32[]{:S(2)}) collective-permute-start(bf16[4,288,288]{2,1,0:T(8,128)(2,1)S(1)} %copy-done.95), channel_id=1, source_target_pairs={{0,4},{4,0},{8,12},{12,8},{16,20},{20,16},{24,28},{28,24},{1,5},{5... | collective-permute-start | bytes 1990664 | tf_op jit(solution)/shard_map/ppermute | solution.py:54
  347.6 25.4 %collective-permute-start.57 = (bf16[4,288,288]{2,1,0:T(8,128)(2,1)}, bf16[4,288,288]{2,1,0:T(8,128)(2,1)}, u32[]{:S(2)}, u32[]{:S(2)}) collective-permute-start(bf16[4,288,288]{2,1,0:T(8,128)(2,1)} %get-tuple-element.192), channel_id=1, source_target_pairs={{0,4},{4,0},{8,12},{12,8},{16,20},{20,16},{24,28},{28,24},{1,5},{5... | collective-permute-start | bytes 1990664 | tf_op jit(solution)/shard_map/ppermute | solution.py:54
  353.6 36.1 %collective-permute-start.65 = (bf16[2,144,1152]{2,1,0:T(8,128)(2,1)}, bf16[2,144,1152]{2,1,0:T(8,128)(2,1)}, u32[]{:S(2)}, u32[]{:S(2)}) collective-permute-start(bf16[2,144,1152]{2,1,0:T(8,128)(2,1)} %get-tuple-element.236), channel_id=1, source_target_pairs={{0,16},{4,20},{8,24},{12,28},{16,0},{20,4},{24,8},{28,12},{1,17},{... | collective-permute-start | bytes 1990664 | tf_op jit(solution)/shard_map/ppermute | solution.py:51
  356.3 22.6 %collective-permute-start.59 = (bf16[4,288,288]{2,1,0:T(8,128)(2,1)S(1)}, bf16[4,288,288]{2,1,0:T(8,128)(2,1)}, u32[]{:S(2)}, u32[]{:S(2)}) collective-permute-start(bf16[4,288,288]{2,1,0:T(8,128)(2,1)S(1)} %pad_maximum_fusion.5.refs_13_), channel_id=1, source_target_pairs={{0,2},{1,3},{2,0},{3,1},{4,6},{5,7},{6,4},{7,5},{8,10},{9,11},{10,... | collective-permute-start | bytes 1990664 | tf_op jit(solution)/shard_map/ppermute | solution.py:48
  358.9 22.7 %collective-permute-start.58 = (bf16[4,288,288]{2,1,0:T(8,128)(2,1)}, bf16[4,288,288]{2,1,0:T(8,128)(2,1)}, u32[]{:S(2)}, u32[]{:S(2)}) collective-permute-start(bf16[4,288,288]{2,1,0:T(8,128)(2,1)} %pad_maximum_fusion.4.refs_12_), channel_id=1, source_target_pairs={{0,1},{1,0},{2,3},{3,2},{4,5},{5,4},{6,7},{7,6},{8,9},{9,8},{10,11... | collective-permute-start | bytes 1990664 | tf_op jit(solution)/shard_map/ppermute | solution.py:48
  371.7 12.2 %collective-permute-start.60 = (bf16[144,576]{1,0:T(8,128)(2,1)S(1)}, bf16[144,576]{1,0:T(8,128)(2,1)S(1)}, u32[]{:S(2)}, u32[]{:S(2)}) collective-permute-start(bf16[144,576]{1,0:T(8,128)(2,1)S(1)} %get-tuple-element.248), channel_id=1, source_target_pairs={{0,3},{1,2},{2,1},{3,0},{4,7},{5,6},{6,5},{7,4},{8,11},{9,10},{10,... | collective-permute-start | bytes 497672 | tf_op jit(solution)/shard_map/ppermute | solution.py:48
  387.3 18.8 %collective-permute-start.67 = (bf16[2,288,288]{2,1,0:T(8,128)(2,1)}, bf16[2,288,288]{2,1,0:T(8,128)(2,1)}, u32[]{:S(2)}, u32[]{:S(2)}) collective-permute-start(bf16[2,288,288]{2,1,0:T(8,128)(2,1)} %add_convert_fusion.7), channel_id=1, source_target_pairs={{0,16},{4,20},{8,24},{12,28},{16,0},{20,4},{24,8},{28,12},{1,17},{... | collective-permute-start | bytes 995336 | tf_op jit(solution)/shard_map/ppermute | solution.py:51
  391.7 17.0 %collective-permute-start.66 = (bf16[1,144,1152]{2,1,0:T(8,128)(2,1)}, bf16[1,144,1152]{2,1,0:T(8,128)(2,1)}, u32[]{:S(2)}, u32[]{:S(2)}) collective-permute-start(bf16[1,144,1152]{2,1,0:T(8,128)(2,1)} %slice.445), channel_id=1, source_target_pairs={{0,8},{4,12},{8,0},{12,4},{16,24},{20,28},{24,16},{28,20},{1,9},{5... | collective-permute-start | bytes 995336 | tf_op jit(solution)/shard_map/ppermute | solution.py:51
  (125 other events, 940.5 us)
Sparse Core Ops, SparseCore 0:
  80.5 34.4 all-gather.2
  117.2 33.1 all-gather.4
  233.9 60.5 reduce-scatter.1
